TPU v7x, 32 devices: a whole 2x2x4 slice. The times are simulated.
32 devices in a mesh: ctx: 4 (over y, x), fsdp: 8 (over z, core).
Axes of the slice: x: 2, y: 2, z: 4, core: 2. Of those that a mesh axis runs over, the one named last changes fastest.
Arguments:
- hidden_in: bfloat16 [8, 1024, 1536], P('fsdp', 'ctx'), may hold values from -6 to 6
- cotangent: bfloat16 [8, 1024, 1536], P('fsdp', 'ctx'), may hold values from -6 to 6
- norm_mix: bfloat16 [1536], P('fsdp'), may hold values from 0.25 to 1.75
- in_proj: bfloat16 [4608, 1536], P('fsdp'), may hold values from -0.15625 to 0.15625
- conv_kernel: bfloat16 [1536, 3], P('fsdp'), may hold values from -3.5 to 3.5
- out_proj: bfloat16 [1536, 1536], P('fsdp'), may hold values from -0.15625 to 0.15625
- norm_ff1: bfloat16 [1536], P('fsdp'), may hold values from 0.25 to 1.75
- gate1: bfloat16 [6912, 1536], P('fsdp'), may hold values from -0.15625 to 0.15625
- up1: bfloat16 [6912, 1536], P('fsdp'), may hold values from -0.15625 to 0.15625
- down1: bfloat16 [6912, 1536], P('fsdp'), may hold values from -0.078125 to 0.078125
- norm_attn: bfloat16 [1536], P('fsdp'), may hold values from 0.25 to 1.75
- q_proj: bfloat16 [1536, 1536], P('fsdp'), may hold values from -0.15625 to 0.15625
- key_projection: bfloat16 [512, 1536], P('fsdp'), may hold values from -0.15625 to 0.15625
- value_projection: bfloat16 [512, 1536], P('fsdp'), may hold values from -0.15625 to 0.15625
- q_norm: bfloat16 [64], P('fsdp'), may hold values from 0.25 to 1.75
- k_norm: bfloat16 [64], P('fsdp'), may hold values from 0.25 to 1.75
- o_proj: bfloat16 [1536, 1536], P('fsdp'), may hold values from -0.4375 to 0.4375
- norm_ff2: bfloat16 [1536], P('fsdp'), may hold values from 0.25 to 1.75
- gate2: bfloat16 [6912, 1536], P('fsdp'), may hold values from -0.15625 to 0.15625
- up2: bfloat16 [6912, 1536], P('fsdp'), may hold values from -0.15625 to 0.15625
- down2: bfloat16 [6912, 1536], P('fsdp'), may hold values from -0.078125 to 0.078125
Outputs:
- hidden_out: bfloat16 [8, 1024, 1536], P('fsdp', 'ctx')
- grad_in: float32 [8, 1024, 1536], P('fsdp', 'ctx')
- grad_norm_mix: float32 [1536], P('fsdp')
- grad_in_proj: float32 [4608, 1536], P('fsdp')
- grad_conv_kernel: float32 [1536, 3], P('fsdp')
- grad_out_proj: float32 [1536, 1536], P('fsdp')
- grad_norm_ff1: float32 [1536], P('fsdp')
- grad_gate1: float32 [6912, 1536], P('fsdp')
- grad_up1: float32 [6912, 1536], P('fsdp')
- grad_down1: float32 [6912, 1536], P('fsdp')
- grad_norm_attn: float32 [1536], P('fsdp')
- grad_q_proj: float32 [1536, 1536], P('fsdp')
- grad_k_proj: float32 [512, 1536], P('fsdp')
- grad_v_proj: float32 [512, 1536], P('fsdp')
- grad_q_norm: float32 [64], P('fsdp')
- grad_k_norm: float32 [64], P('fsdp')
- grad_o_proj: float32 [1536, 1536], P('fsdp')
- grad_norm_ff2: float32 [1536], P('fsdp')
- grad_gate2: float32 [6912, 1536], P('fsdp')
- grad_up2: float32 [6912, 1536], P('fsdp')
- grad_down2: float32 [6912, 1536], P('fsdp')
All inputs are finite; a program needn't handle non-finite values.
Results may differ from a plain program's by a relative error of at most 0.028.
Values may be sent and summed in bfloat16 or wider, within the bound.
A program may use at most 640 MiB of HBM per device.

v0:
```python
from functools import partial

import jax
import jax.numpy as jnp
from jax import lax
from jax.sharding import PartitionSpec as P

MODEL_WIDTH = 1536
QUERY_HEADS = 24
KEY_VALUE_HEADS = 8
HEAD_SIZE = 64
KW = 3


EPS = 1e-05
THETA = 1000000.0
NEG = -1e30


def extended_2(array, sides, width):
    for axis, dim in sides:
        size, length = (lax.axis_size(axis), array.shape[dim])
        up = [(i, (i + 1) % size) for i in range(size - 1)]
        down = [(j, i) for i, j in up]
        last = lax.slice_in_dim(array, length - width, length, axis=dim)
        first = lax.slice_in_dim(array, 0, width, axis=dim)
        before = lax.ppermute(last, axis, up)
        after = lax.ppermute(first, axis, down)
        array = jnp.concatenate([before, array, after], axis=dim)
    return array


def rms_scale(value, gain):
    return value * lax.rsqrt(jnp.mean(value * value, axis=-1, keepdims=True) + EPS) * gain


def rotate(value, places):
    half_dim = value.shape[-1] // 2
    freqs = THETA ** (-jnp.arange(half_dim, dtype=jnp.float32) * 2.0 / value.shape[-1])
    angles = places[:, None] * freqs[None, :]
    cosine = jnp.cos(angles)[:, None, :]
    sine = jnp.sin(angles)[:, None, :]
    first = value[..., :half_dim]
    second = value[..., half_dim:]
    return jnp.concatenate(
        [first * cosine - second * sine, second * cosine + first * sine], axis=-1
    )


def head_prep(raw, gain, places):
    width = gain.shape[0]
    heads = raw.reshape(raw.shape[0], raw.shape[1] // width, width)
    return rotate(rms_scale(heads, gain), places)


def dot_rows(left, right):
    return lax.dot_general(
        left, right, (((1,), (1,)), ((), ())), preferred_element_type=jnp.float32
    )


def dot_cols(left, right):
    return lax.dot_general(
        left, right, (((0,), (0,)), ((), ())), preferred_element_type=jnp.float32
    )


def dot_plain(left, right):
    return jnp.dot(left, right, preferred_element_type=jnp.float32)


def swish_product(gate_val, up_val):
    return jax.nn.silu(gate_val) * up_val


def dealt_places(index, block, ctx_count):
    device = index // (2 * block)
    within = index % (2 * block)
    which = jnp.where(within < block, device, 2 * ctx_count - 1 - device)
    return which * block + within % block


def conv_apply(extended, kernel):
    sequence_length = extended.shape[0] - KW + 1
    total = extended[0:sequence_length] * kernel[:, 0]
    for place in range(1, KW):
        total = total + extended[place : place + sequence_length] * kernel[:, place]
    return total


def conv_input_grad(grad_conv, kernel):
    sequence_length = grad_conv.shape[0] + KW - 1
    padded = jnp.pad(grad_conv, ((KW - 1, KW - 1), (0, 0)))
    total = padded[KW - 1 : KW - 1 + sequence_length] * kernel[:, 0]
    for place in range(1, KW):
        total = total + padded[KW - 1 - place : KW - 1 - place + sequence_length] * kernel[:, place]
    return total


def kernel_grad(extended, grad_conv):
    sequence_length = grad_conv.shape[0]
    columns = [
        jnp.sum(grad_conv * extended[place : place + sequence_length], axis=0)
        for place in range(KW)
    ]
    return jnp.stack(columns, axis=1)


def masked_scores(query_narrow, grouped_key_rows, query_places, key_places):
    scores = jnp.einsum(
        "rhgd,lhd->hgrl", query_narrow, grouped_key_rows, preferred_element_type=jnp.float32
    )
    scores = scores * query_narrow.shape[-1] ** (-0.5)
    allowed = query_places[:, None] >= key_places[None, :]
    return jnp.where(allowed, scores, NEG)


def mix_weights(norm_mix, in_proj, conv_kernel, out_proj, norm_ff1):
    return (
        lax.all_gather(norm_mix, "fsdp", axis=0, tiled=True),
        lax.all_gather(in_proj, "fsdp", axis=0, tiled=True),
        lax.all_gather(conv_kernel, "fsdp", axis=0, tiled=True),
        lax.all_gather(out_proj, "fsdp", axis=0, tiled=True),
        lax.all_gather(norm_ff1, "fsdp", axis=0, tiled=True),
    )


def attn_weights(
    norm_attn, q_proj, key_projection, value_projection, q_norm, k_norm, o_proj, norm_ff2
):
    return (
        lax.all_gather(norm_attn, "fsdp", axis=0, tiled=True),
        lax.all_gather(q_proj, "fsdp", axis=0, tiled=True),
        lax.all_gather(key_projection, "fsdp", axis=0, tiled=True),
        lax.all_gather(value_projection, "fsdp", axis=0, tiled=True),
        lax.all_gather(q_norm, "fsdp", axis=0, tiled=True),
        lax.all_gather(k_norm, "fsdp", axis=0, tiled=True),
        lax.all_gather(o_proj, "fsdp", axis=0, tiled=True),
        lax.all_gather(norm_ff2, "fsdp", axis=0, tiled=True),
    )


def ff_weights(gate, up_w, down):
    return (
        lax.all_gather(gate, "fsdp", axis=0, tiled=True),
        lax.all_gather(up_w, "fsdp", axis=0, tiled=True),
        lax.all_gather(down, "fsdp", axis=0, tiled=True),
    )


def ff_grads(gate_grad, up_grad, down_grad):
    return (
        lax.psum_scatter(
            gate_grad.astype(jnp.bfloat16), "fsdp", scatter_dimension=0, tiled=True
        ).astype(jnp.float32),
        lax.psum_scatter(
            up_grad.astype(jnp.bfloat16), "fsdp", scatter_dimension=0, tiled=True
        ).astype(jnp.float32),
        lax.psum_scatter(
            down_grad.astype(jnp.bfloat16), "fsdp", scatter_dimension=0, tiled=True
        ).astype(jnp.float32),
    )


def ff_forward(normed, gate, up_w, down):
    full_gate, full_up, full_down = ff_weights(gate, up_w, down)
    gate_val = dot_rows(normed, full_gate)
    up_val = dot_rows(normed, full_up)
    hidden = swish_product(gate_val, up_val).astype(jnp.bfloat16)
    result = dot_plain(hidden, full_down)
    return (result, (normed, gate_val, up_val, hidden))


def ff_backward(grad_out, kept, gate, up_w, down):
    inputs, gate_val, up_val, hidden = kept
    full_gate, full_up, full_down = ff_weights(gate, up_w, down)
    grad_hidden = dot_rows(grad_out, full_down)
    grad_down = dot_cols(hidden, grad_out)
    _, swish_back = jax.vjp(swish_product, gate_val, up_val)
    grad_gate_val, grad_up_val = swish_back(grad_hidden)
    gate_low = grad_gate_val.astype(jnp.bfloat16)
    up_low = grad_up_val.astype(jnp.bfloat16)
    grad_gate = dot_cols(gate_low, inputs)
    grad_up = dot_cols(up_low, inputs)
    grad_inputs = dot_plain(gate_low, full_gate) + dot_plain(up_low, full_up)
    shares = ff_grads(grad_gate, grad_up, grad_down)
    return (grad_inputs, shares)


def local(
    hidden_in,
    cotangent,
    norm_mix,
    in_proj,
    conv_kernel,
    out_proj,
    norm_ff1,
    gate1,
    up1,
    down1,
    norm_attn,
    q_proj,
    key_projection,
    value_projection,
    q_norm,
    k_norm,
    o_proj,
    norm_ff2,
    gate2,
    up2,
    down2,
):
    narrow_dtype = jnp.bfloat16
    start = hidden_in[0].astype(jnp.float32)
    token_rows = start.shape[0]
    block = token_rows // 2
    margin = KW - 1
    ctx_count = lax.axis_size("ctx")
    ctx_place = lax.axis_index("ctx")
    is_last = ctx_place == ctx_count - 1
    query_places = dealt_places(
        ctx_place * token_rows + jnp.arange(token_rows, dtype=jnp.int32), block, ctx_count
    )
    key_places = dealt_places(jnp.arange(token_rows * ctx_count, dtype=jnp.int32), block, ctx_count)
    query_angles = query_places.astype(jnp.float32)
    mix_norm, mix_in, mix_kernel, mix_out, ff_norm_one = mix_weights(
        norm_mix, in_proj, conv_kernel, out_proj, norm_ff1
    )
    kernel = mix_kernel.astype(jnp.float32)
    normed_one, norm_back_one = jax.vjp(rms_scale, start, mix_norm.astype(jnp.float32))
    normed_one_low = normed_one.astype(narrow_dtype)
    projected = dot_rows(normed_one_low, mix_in)
    b_part = projected[:, :MODEL_WIDTH]
    c_part = projected[:, MODEL_WIDTH : 2 * MODEL_WIDTH]
    x_part = projected[:, 2 * MODEL_WIDTH :]
    mixed_low = (b_part * x_part).astype(narrow_dtype)
    front_tail = mixed_low[block - margin : block]
    back_tail = mixed_low[token_rows - margin :]
    edges = extended_2(jnp.concatenate([back_tail, front_tail], axis=0), (("ctx", 0),), margin)
    before_front = edges[:margin]
    before_back = jnp.where(is_last, front_tail, edges[edges.shape[0] - margin :])
    front_ext = jnp.concatenate([before_front, mixed_low[:block]], axis=0).astype(jnp.float32)
    back_ext = jnp.concatenate([before_back, mixed_low[block:]], axis=0).astype(jnp.float32)
    conv_out = jnp.concatenate(
        [conv_apply(front_ext, kernel), conv_apply(back_ext, kernel)], axis=0
    )
    gated_low = (c_part * conv_out).astype(narrow_dtype)
    first = start + dot_rows(gated_low, mix_out)
    normed_two, norm_back_two = jax.vjp(rms_scale, first, ff_norm_one.astype(jnp.float32))
    ff_out_one, kept_one = ff_forward(normed_two.astype(narrow_dtype), gate1, up1, down1)
    second = first + ff_out_one
    attn_norm, w_query, w_key, w_value, query_gain, key_gain, w_output, ff_norm_two = attn_weights(
        norm_attn, q_proj, key_projection, value_projection, q_norm, k_norm, o_proj, norm_ff2
    )
    normed_three, norm_back_three = jax.vjp(rms_scale, second, attn_norm.astype(jnp.float32))
    three_low = normed_three.astype(narrow_dtype)
    query_raw = dot_rows(three_low, w_query)
    key_raw = dot_rows(three_low, w_key)
    value_raw = dot_rows(three_low, w_value)
    query_head_split, query_back = jax.vjp(
        partial(head_prep, places=query_angles), query_raw, query_gain.astype(jnp.float32)
    )
    key_head_split, key_reverse_rotation = jax.vjp(
        partial(head_prep, places=query_angles), key_raw, key_gain.astype(jnp.float32)
    )
    query_narrow = query_head_split.astype(narrow_dtype).reshape(
        token_rows, KEY_VALUE_HEADS, QUERY_HEADS // KEY_VALUE_HEADS, HEAD_SIZE
    )
    key_narrow = key_head_split.astype(narrow_dtype).reshape(
        token_rows, KEY_VALUE_HEADS * HEAD_SIZE
    )
    value_low = value_raw.astype(narrow_dtype)
    gathered_keys, gathered_values = (
        lax.all_gather(key_narrow, "ctx", axis=0, tiled=True),
        lax.all_gather(value_low, "ctx", axis=0, tiled=True),
    )
    grouped_key_rows = gathered_keys.reshape(-1, KEY_VALUE_HEADS, HEAD_SIZE)
    grouped_value_rows = gathered_values.reshape(-1, KEY_VALUE_HEADS, HEAD_SIZE)
    scores = masked_scores(query_narrow, grouped_key_rows, query_places, key_places)
    peak = jnp.max(scores, axis=-1, keepdims=True)
    total = jnp.sum(jnp.exp(scores - peak), axis=-1, keepdims=True)
    probs_low = (jnp.exp(scores - peak) / total).astype(narrow_dtype)
    attended = jnp.einsum(
        "hgrl,lhd->rhgd", probs_low, grouped_value_rows, preferred_element_type=jnp.float32
    )
    attended_low = attended.reshape(token_rows, QUERY_HEADS * HEAD_SIZE).astype(narrow_dtype)
    third = second + dot_rows(attended_low, w_output)
    normed_four, norm_back_four = jax.vjp(rms_scale, third, ff_norm_two.astype(jnp.float32))
    ff_out_two, kept_two = ff_forward(normed_four.astype(narrow_dtype), gate2, up2, down2)
    final = third + ff_out_two
    grad_final = cotangent[0].astype(jnp.float32)
    grad_four, shares_two = ff_backward(
        grad_final.astype(narrow_dtype), kept_two, gate2, up2, down2
    )
    grad_third_part, grad_ff_norm_two = norm_back_four(grad_four)
    grad_third = grad_final + grad_third_part
    output_low = grad_third.astype(narrow_dtype)
    attended_gradient = dot_plain(output_low, w_output)
    grad_w_output = dot_cols(output_low, attended_low)
    attended_gradient_narrow = attended_gradient.astype(narrow_dtype).reshape(
        token_rows, KEY_VALUE_HEADS, QUERY_HEADS // KEY_VALUE_HEADS, HEAD_SIZE
    )
    scores = masked_scores(query_narrow, grouped_key_rows, query_places, key_places)
    probs = jnp.exp(scores - peak) / total
    probs_low = probs.astype(narrow_dtype)
    grad_probs = jnp.einsum(
        "rhgd,lhd->hgrl",
        attended_gradient_narrow,
        grouped_value_rows,
        preferred_element_type=jnp.float32,
    )
    weighted = jnp.sum(probs * grad_probs, axis=-1, keepdims=True)
    grad_scores = (probs * (grad_probs - weighted)).astype(narrow_dtype)
    scale = HEAD_SIZE ** (-0.5)
    grad_query = (
        jnp.einsum(
            "hgrl,lhd->rhgd", grad_scores, grouped_key_rows, preferred_element_type=jnp.float32
        )
        * scale
    )
    keys_gradient = (
        jnp.einsum("hgrl,rhgd->lhd", grad_scores, query_narrow, preferred_element_type=jnp.float32)
        * scale
    )
    values_gradient = jnp.einsum(
        "hgrl,rhgd->lhd", probs_low, attended_gradient_narrow, preferred_element_type=jnp.float32
    )
    local_keys, own_values = (
        lax.psum_scatter(
            keys_gradient.reshape(-1, KEY_VALUE_HEADS * HEAD_SIZE).astype(jnp.bfloat16),
            "ctx",
            scatter_dimension=0,
            tiled=True,
        ).astype(jnp.float32),
        lax.psum_scatter(
            values_gradient.reshape(-1, KEY_VALUE_HEADS * HEAD_SIZE).astype(jnp.bfloat16),
            "ctx",
            scatter_dimension=0,
            tiled=True,
        ).astype(jnp.float32),
    )
    grad_query_raw, grad_query_gain = query_back(
        grad_query.reshape(token_rows, QUERY_HEADS, HEAD_SIZE)
    )
    raw_key_gradient, key_gain_gradient = key_reverse_rotation(
        local_keys.reshape(token_rows, KEY_VALUE_HEADS, HEAD_SIZE)
    )
    query_grad_low = grad_query_raw.astype(narrow_dtype)
    key_grad_low = raw_key_gradient.astype(narrow_dtype)
    value_grad_low = own_values.astype(narrow_dtype)
    grad_three = (
        dot_plain(query_grad_low, w_query)
        + dot_plain(key_grad_low, w_key)
        + dot_plain(value_grad_low, w_value)
    )
    grad_w_query = dot_cols(query_grad_low, three_low)
    grad_w_key = dot_cols(key_grad_low, three_low)
    grad_w_value = dot_cols(value_grad_low, three_low)
    grad_second_part, grad_attn_norm = norm_back_three(grad_three)
    grad_second = grad_third + grad_second_part
    attn_shares = (
        lax.psum_scatter(
            grad_attn_norm.astype(jnp.bfloat16), "fsdp", scatter_dimension=0, tiled=True
        ).astype(jnp.float32),
        lax.psum_scatter(
            grad_w_query.astype(jnp.bfloat16), "fsdp", scatter_dimension=0, tiled=True
        ).astype(jnp.float32),
        lax.psum_scatter(
            grad_w_key.astype(jnp.bfloat16), "fsdp", scatter_dimension=0, tiled=True
        ).astype(jnp.float32),
        lax.psum_scatter(
            grad_w_value.astype(jnp.bfloat16), "fsdp", scatter_dimension=0, tiled=True
        ).astype(jnp.float32),
        lax.psum_scatter(
            grad_query_gain.astype(jnp.bfloat16), "fsdp", scatter_dimension=0, tiled=True
        ).astype(jnp.float32),
        lax.psum_scatter(
            key_gain_gradient.astype(jnp.bfloat16), "fsdp", scatter_dimension=0, tiled=True
        ).astype(jnp.float32),
        lax.psum_scatter(
            grad_w_output.astype(jnp.bfloat16), "fsdp", scatter_dimension=0, tiled=True
        ).astype(jnp.float32),
        lax.psum_scatter(
            grad_ff_norm_two.astype(jnp.bfloat16), "fsdp", scatter_dimension=0, tiled=True
        ).astype(jnp.float32),
    )
    grad_two, shares_one = ff_backward(
        grad_second.astype(narrow_dtype), kept_one, gate1, up1, down1
    )
    grad_first_part, grad_ff_norm_one = norm_back_two(grad_two)
    grad_first = grad_second + grad_first_part
    first_low = grad_first.astype(narrow_dtype)
    grad_gated = dot_plain(first_low, mix_out)
    grad_mix_out = dot_cols(first_low, gated_low)
    grad_c_part = grad_gated * conv_out
    grad_conv = grad_gated * c_part
    grad_front_ext = conv_input_grad(grad_conv[:block], kernel)
    grad_back_ext = conv_input_grad(grad_conv[block:], kernel)
    back_before = grad_back_ext[:margin]
    outgoing = jnp.concatenate(
        [grad_front_ext[:margin], jnp.where(is_last, 0.0, back_before)], axis=0
    )
    returned = extended_2(outgoing, (("ctx", 0),), margin)
    from_prev = returned[:margin]
    from_next = returned[returned.shape[0] - margin :]
    own_edge = jnp.where(is_last, back_before, 0.0)
    front_grad = grad_front_ext[margin:]
    back_grad = grad_back_ext[margin:]
    front_grad = jnp.concatenate(
        [front_grad[: block - margin], front_grad[block - margin :] + from_next + own_edge], axis=0
    )
    back_grad = jnp.concatenate(
        [back_grad[: block - margin], back_grad[block - margin :] + from_prev], axis=0
    )
    grad_mixed = jnp.concatenate([front_grad, back_grad], axis=0)
    grad_kernel = kernel_grad(front_ext, grad_conv[:block]) + kernel_grad(
        back_ext, grad_conv[block:]
    )
    grad_projected = jnp.concatenate(
        [grad_mixed * x_part, grad_c_part, grad_mixed * b_part], axis=-1
    ).astype(narrow_dtype)
    grad_mix_in = dot_cols(grad_projected, normed_one_low)
    grad_one = dot_plain(grad_projected, mix_in)
    grad_start_part, grad_mix_norm = norm_back_one(grad_one)
    grad_start = grad_first + grad_start_part
    mix_shares = (
        lax.psum_scatter(
            grad_mix_norm.astype(jnp.bfloat16), "fsdp", scatter_dimension=0, tiled=True
        ).astype(jnp.float32),
        lax.psum_scatter(
            grad_mix_in.astype(jnp.bfloat16), "fsdp", scatter_dimension=0, tiled=True
        ).astype(jnp.float32),
        lax.psum_scatter(
            grad_kernel.astype(jnp.bfloat16), "fsdp", scatter_dimension=0, tiled=True
        ).astype(jnp.float32),
        lax.psum_scatter(
            grad_mix_out.astype(jnp.bfloat16), "fsdp", scatter_dimension=0, tiled=True
        ).astype(jnp.float32),
        lax.psum_scatter(
            grad_ff_norm_one.astype(jnp.bfloat16), "fsdp", scatter_dimension=0, tiled=True
        ).astype(jnp.float32),
    )
    summed = (
        lax.psum(mix_shares[0].astype(jnp.bfloat16), "ctx").astype(jnp.float32),
        lax.psum(mix_shares[1].astype(jnp.bfloat16), "ctx").astype(jnp.float32),
        lax.psum(mix_shares[2].astype(jnp.bfloat16), "ctx").astype(jnp.float32),
        lax.psum(mix_shares[3].astype(jnp.bfloat16), "ctx").astype(jnp.float32),
        lax.psum(mix_shares[4].astype(jnp.bfloat16), "ctx").astype(jnp.float32),
        lax.psum(shares_one[0].astype(jnp.bfloat16), "ctx").astype(jnp.float32),
        lax.psum(shares_one[1].astype(jnp.bfloat16), "ctx").astype(jnp.float32),
        lax.psum(shares_one[2].astype(jnp.bfloat16), "ctx").astype(jnp.float32),
        lax.psum(attn_shares[0].astype(jnp.bfloat16), "ctx").astype(jnp.float32),
        lax.psum(attn_shares[1].astype(jnp.bfloat16), "ctx").astype(jnp.float32),
        lax.psum(attn_shares[2].astype(jnp.bfloat16), "ctx").astype(jnp.float32),
        lax.psum(attn_shares[3].astype(jnp.bfloat16), "ctx").astype(jnp.float32),
        lax.psum(attn_shares[4].astype(jnp.bfloat16), "ctx").astype(jnp.float32),
        lax.psum(attn_shares[5].astype(jnp.bfloat16), "ctx").astype(jnp.float32),
        lax.psum(attn_shares[6].astype(jnp.bfloat16), "ctx").astype(jnp.float32),
        lax.psum(attn_shares[7].astype(jnp.bfloat16), "ctx").astype(jnp.float32),
        lax.psum(shares_two[0].astype(jnp.bfloat16), "ctx").astype(jnp.float32),
        lax.psum(shares_two[1].astype(jnp.bfloat16), "ctx").astype(jnp.float32),
        lax.psum(shares_two[2].astype(jnp.bfloat16), "ctx").astype(jnp.float32),
    )
    return (
        final.astype(narrow_dtype)[None],
        grad_start[None],
        summed[0],
        summed[1],
        summed[2],
        summed[3],
        summed[4],
        summed[5],
        summed[6],
        summed[7],
        summed[8],
        summed[9],
        summed[10],
        summed[11],
        summed[12],
        summed[13],
        summed[14],
        summed[15],
        summed[16],
        summed[17],
        summed[18],
    )


def solution(mesh):
    in_specs = (
        P("fsdp", "ctx", None),
        P("fsdp", "ctx", None),
        P("fsdp"),
        P("fsdp", None),
        P("fsdp", None),
        P("fsdp", None),
        P("fsdp"),
        P("fsdp", None),
        P("fsdp", None),
        P("fsdp", None),
        P("fsdp"),
        P("fsdp", None),
        P("fsdp", None),
        P("fsdp", None),
        P("fsdp"),
        P("fsdp"),
        P("fsdp", None),
        P("fsdp"),
        P("fsdp", None),
        P("fsdp", None),
        P("fsdp", None),
    )
    out_specs = (
        P("fsdp", "ctx", None),
        P("fsdp", "ctx", None),
        P("fsdp"),
        P("fsdp", None),
        P("fsdp", None),
        P("fsdp", None),
        P("fsdp"),
        P("fsdp", None),
        P("fsdp", None),
        P("fsdp", None),
        P("fsdp"),
        P("fsdp", None),
        P("fsdp", None),
        P("fsdp", None),
        P("fsdp"),
        P("fsdp"),
        P("fsdp", None),
        P("fsdp"),
        P("fsdp", None),
        P("fsdp", None),
        P("fsdp", None),
    )
    return jax.shard_map(local, mesh=mesh, in_specs=in_specs, out_specs=out_specs, check_vma=False)
```

profile of v0, /device:TPU:16, one launch (start us, length us, event | category | flops | bytes accessed | tf_op | source)
XLA Modules:
  0.0 3757.8 jit_solution(2694870127750282488)
XLA Ops:
  16.2 29.6 all-reduce.19
  46.6 16.2 all-gather
  63.0 76.2 %all-gather.16.cloned.1.call-done = bf16[4608,1536]{1,0:T(8,128)(2,1)} async-done(((bf16[576,1536]{1,0:T(8,128)(2,1)}), bf16[4608,1536]{1,0:T(8,128)(2,1)}) %all-gather.16.cloned.1.call-update) | async-done | bytes 14155792 | tf_op jit(solution)/shard_map/all_gather | solution.py:121
  139.2 7.2 fusion.57
  148.0 4.2 collective-permute-done.1
  152.2 4.5 collective-permute-start
  160.3 31.1 all-gather.18.cloned.1.call-done
  196.0 182.9 %all-gather.20.cloned.1.call-done = bf16[6912,1536]{1,0:T(8,128)(2,1)} async-done(((bf16[864,1536]{1,0:T(8,128)(2,1)}), bf16[6912,1536]{1,0:T(8,128)(2,1)}) %all-gather.20.cloned.1.call-update) | async-done | bytes 21233680 | tf_op jit(solution)/shard_map/all_gather | solution.py:145
  379.0 13.7 fusion.95
  392.7 173.6 %all-gather.22.cloned.1.call-done = bf16[6912,1536]{1,0:T(8,128)(2,1)} async-done(((bf16[864,1536]{1,0:T(8,128)(2,1)}), bf16[6912,1536]{1,0:T(8,128)(2,1)}) %all-gather.22.cloned.1.call-update) | async-done | bytes 21233680 | tf_op jit(solution)/shard_map/all_gather | solution.py:146
  566.3 16.2 multiply_convert_fusion.3
  582.5 171.1 %all-gather.24.cloned.1.call-done = bf16[6912,1536]{1,0:T(8,128)(2,1)} async-done(((bf16[864,1536]{1,0:T(8,128)(2,1)}), bf16[6912,1536]{1,0:T(8,128)(2,1)}) %all-gather.24.cloned.1.call-update) | async-done | bytes 21233680 | tf_op jit(solution)/shard_map/all_gather | solution.py:147
  753.7 11.1 multiply_reduce_fusion.10
  765.1 14.4 all-gather.26.cloned.1.call-done
  782.5 23.2 all-gather.30.cloned.1.call-done
  813.6 44.6 %all-gather.34.cloned.1.call-done = bf16[1536,1536]{1,0:T(8,128)(2,1)} async-done(((bf16[192,1536]{1,0:T(8,128)(2,1)}), bf16[1536,1536]{1,0:T(8,128)(2,1)}) %all-gather.34.cloned.1.call-update) | async-done | bytes 4718608 | tf_op jit(solution)/shard_map/all_gather | solution.py:133
  864.4 22.9 all-gather.28.cloned.1.call-done
  888.8 27.3 all-gather.32.cloned.1.call-done
  916.0 13.9 fusion.94
  930.0 10.6 fusion.39
  940.6 27.7 all-gather.36.cloned.1.call-done
  968.3 4.1 multiply_reduce_fusion.8
  972.6 183.0 %all-gather.38.cloned.1.call-done = bf16[6912,1536]{1,0:T(8,128)(2,1)} async-done(((bf16[864,1536]{1,0:T(8,128)(2,1)}), bf16[6912,1536]{1,0:T(8,128)(2,1)}) %all-gather.38.cloned.1.call-update) | async-done | bytes 21233680 | tf_op jit(solution)/shard_map/all_gather | solution.py:145
  1155.7 13.7 fusion.97
  1169.3 173.8 %all-gather.40.cloned.1.call-done = bf16[6912,1536]{1,0:T(8,128)(2,1)} async-done(((bf16[864,1536]{1,0:T(8,128)(2,1)}), bf16[6912,1536]{1,0:T(8,128)(2,1)}) %all-gather.40.cloned.1.call-update) | async-done | bytes 21233680 | tf_op jit(solution)/shard_map/all_gather | solution.py:146
  1343.2 13.9 fusion.98
  1357.1 173.4 %all-gather.42.cloned.1.call-done = bf16[6912,1536]{1,0:T(8,128)(2,1)} async-done(((bf16[864,1536]{1,0:T(8,128)(2,1)}), bf16[6912,1536]{1,0:T(8,128)(2,1)}) %all-gather.42.cloned.1.call-update) | async-done | bytes 21233680 | tf_op jit(solution)/shard_map/all_gather | solution.py:147
  1530.5 23.3 multiply_convert_fusion.1
  1553.8 12.3 fusion.99
  1566.1 10.9 multiply_reduce_fusion
  1580.4 11.7 bitcast_convert_fusion
  1592.0 16.3 fusion.1
  1608.5 16.9 fusion.3
  1625.3 6.1 fusion.24
  1631.6 4.6 reduce-scatter.20.cloned.1.call-done
  1639.3 28.3 reduce-scatter.18.cloned.1.call-done
  1671.4 6.8 convolution_multiply_fusion
  1690.3 3.9 fusion.100
  1698.0 23.2 multiply_convert_fusion
  1721.2 12.5 fusion.101
  1733.7 10.3 multiply_reduce_fusion.3
  1749.1 5.8 multiply_convert_fusion.5
  1761.1 4.1 collective-permute-done.2
  1766.8 8.8 convolution_convert_fusion.6
  1776.8 12.4 convolution_convert_fusion.2
  1789.3 12.5 convolution_convert_fusion.1
  1803.0 12.4 convolution_convert_fusion
  1816.8 12.5 convolution_convert_fusion.3
  1830.4 12.4 convolution_convert_fusion.5
  1843.1 12.3 convolution_convert_fusion.4
  1856.8 47.2 %reduce-scatter.24.cloned.1.call-done = bf16[192,1536]{1,0:T(8,128)(2,1)} async-done(((bf16[1536,1536]{1,0:T(8,128)(2,1)}), bf16[192,1536]{1,0:T(8,128)(2,1)}) %reduce-scatter.24.cloned.1.call-update) | async-done | bytes 589840 | tf_op jit(solution)/shard_map/reduce_scatter | solution.py:436
  1904.0 144.7 %reduce-scatter.22.cloned.1.call-done = bf16[576,1536]{1,0:T(8,128)(2,1)} async-done(((bf16[4608,1536]{1,0:T(8,128)(2,1)}), bf16[576,1536]{1,0:T(8,128)(2,1)}) %reduce-scatter.22.cloned.1.call-update) | async-done | bytes 1769488 | tf_op jit(solution)/shard_map/reduce_scatter | solution.py:430
  2048.8 210.9 %reduce-scatter.40.cloned.1.call-done = bf16[864,1536]{1,0:T(8,128)(2,1)} async-done(((bf16[6912,1536]{1,0:T(8,128)(2,1)}), bf16[864,1536]{1,0:T(8,128)(2,1)}) %reduce-scatter.40.cloned.1.call-update) | async-done | bytes 2654224 | tf_op jit(solution)/shard_map/reduce_scatter | solution.py:153
  2259.7 210.9 %reduce-scatter.42.cloned.1.call-done = bf16[864,1536]{1,0:T(8,128)(2,1)} async-done(((bf16[6912,1536]{1,0:T(8,128)(2,1)}), bf16[864,1536]{1,0:T(8,128)(2,1)}) %reduce-scatter.42.cloned.1.call-update) | async-done | bytes 2654224 | tf_op jit(solution)/shard_map/reduce_scatter | solution.py:156
  2470.6 210.9 %reduce-scatter.44.cloned.1.call-done = bf16[864,1536]{1,0:T(8,128)(2,1)} async-done(((bf16[6912,1536]{1,0:T(8,128)(2,1)}), bf16[864,1536]{1,0:T(8,128)(2,1)}) %reduce-scatter.44.cloned.1.call-update) | async-done | bytes 2654224 | tf_op jit(solution)/shard_map/reduce_scatter | solution.py:159
  2681.5 210.9 %reduce-scatter.30.cloned.1.call-done = bf16[864,1536]{1,0:T(8,128)(2,1)} async-done(((bf16[6912,1536]{1,0:T(8,128)(2,1)}), bf16[864,1536]{1,0:T(8,128)(2,1)}) %reduce-scatter.30.cloned.1.call-update) | async-done | bytes 2654224 | tf_op jit(solution)/shard_map/reduce_scatter | solution.py:159
  2892.4 210.8 %reduce-scatter.26.cloned.1.call-done = bf16[864,1536]{1,0:T(8,128)(2,1)} async-done(((bf16[6912,1536]{1,0:T(8,128)(2,1)}), bf16[864,1536]{1,0:T(8,128)(2,1)}) %reduce-scatter.26.cloned.1.call-update) | async-done | bytes 2654224 | tf_op jit(solution)/shard_map/reduce_scatter | solution.py:153
  3103.2 211.0 %reduce-scatter.28.cloned.1.call-done = bf16[864,1536]{1,0:T(8,128)(2,1)} async-done(((bf16[6912,1536]{1,0:T(8,128)(2,1)}), bf16[864,1536]{1,0:T(8,128)(2,1)}) %reduce-scatter.28.cloned.1.call-update) | async-done | bytes 2654224 | tf_op jit(solution)/shard_map/reduce_scatter | solution.py:156
  3315.7 11.9 fusion.23
  3327.7 10.2 fusion.30
  3337.9 21.5 all-reduce.18
  3364.0 10.9 all-reduce.20
  3378.7 343.9 %all-reduce.24.cloned.1.call-done = (bf16[576,1536]{1,0:T(8,128)(2,1)}, bf16[192,1536]{1,0:T(8,128)(2,1)}, bf16[864,1536]{1,0:T(8,128)(2,1)}, bf16[864,1536]{1,0...) async-done(((bf16[576,1536]{1,0:T(8,128)(2,1)}, ...) | async-done | bytes 19857424 | tf_op jit(solution)/shard_map/psum | solution.py:445
  3722.6 5.0 convert_element_type.368
  (436 shorter events, 113.3 us)
Async XLA Ops:
  7.2 132.0 %all-gather.16.cloned.1.call-start = ((), (), s32[]{:S(2)}) async-start(), calls=%async_computation.15 | async-start | bytes 15925248 | tf_op jit(solution)/shard_map/all_gather | solution.py:121
  7.9 183.5 %all-gather.18.cloned.1.call-start = ((), (), s32[]{:S(2)}) async-start(), calls=%async_computation.16 | async-start | bytes 5308416 | tf_op jit(solution)/shard_map/all_gather | solution.py:123
  8.7 370.3 %all-gather.20.cloned.1.call-start = ((), (), s32[]{:S(2)}) async-start(), calls=%async_computation.17 | async-start | bytes 23887872 | tf_op jit(solution)/shard_map/all_gather | solution.py:145
  9.5 36.3 copy-start.30
  9.5 556.8 %all-gather.22.cloned.1.call-start = ((), (), s32[]{:S(2)}) async-start(), calls=%async_computation.18 | async-start | bytes 23887872 | tf_op jit(solution)/shard_map/all_gather | solution.py:146
  10.1 36.5 copy-start.108
  10.1 743.6 %all-gather.24.cloned.1.call-start = ((), (), s32[]{:S(2)}) async-start(), calls=%async_computation.19 | async-start | bytes 23887872 | tf_op jit(solution)/shard_map/all_gather | solution.py:147
  10.7 768.8 %all-gather.26.cloned.1.call-start = ((), (), s32[]{:S(2)}) async-start(), calls=%async_computation.20 | async-start | bytes 1769472 | tf_op jit(solution)/shard_map/all_gather | solution.py:135
  11.2 794.5 %all-gather.30.cloned.1.call-start = ((), (), s32[]{:S(2)}) async-start(), calls=%async_computation.22 | async-start | bytes 1769472 | tf_op jit(solution)/shard_map/all_gather | solution.py:134
  12.0 846.2 %all-gather.34.cloned.1.call-start = ((), (), s32[]{:S(2)}) async-start(), calls=%async_computation.24 | async-start | bytes 5308416 | tf_op jit(solution)/shard_map/all_gather | solution.py:133
  12.7 874.5 %all-gather.28.cloned.1.call-start = ((), (), s32[]{:S(2)}) async-start(), calls=%async_computation.21 | async-start | bytes 1310720 | tf_op jit(solution)/shard_map/all_gather | solution.py:275
  45.8 100.7 %copy-start.84 = (f32[1536]{0:T(1024)}, f32[1536]{0:T(1024)S(1)}, u32[]{:S(2)}) copy-start(f32[1536]{0:T(1024)S(1)} %convert_element_type.312) | copy-start | bytes 18436
  46.0 100.4 %copy-start.99 = (f32[256]{0:T(256)}, f32[256]{0:T(256)S(1)}, u32[]{:S(2)}) copy-start(f32[256]{0:T(256)S(1)} %fusion.77) | copy-start | bytes 3076
  62.9 95.1 %copy-start.78 = (f32[1536]{0:T(1024)}, f32[1536]{0:T(1024)S(1)}, u32[]{:S(2)}) copy-start(f32[1536]{0:T(1024)S(1)} %get-tuple-element.42) | copy-start | bytes 18436
  62.9 95.1 %copy-start.80 = (f32[1536]{0:T(1024)}, f32[1536]{0:T(1024)S(1)}, u32[]{:S(2)}) copy-start(f32[1536]{0:T(1024)S(1)} %get-tuple-element.43) | copy-start | bytes 18436
  62.9 95.1 %copy-start.82 = (f32[1536]{0:T(1024)}, f32[1536]{0:T(1024)S(1)}, u32[]{:S(2)}) copy-start(f32[1536]{0:T(1024)S(1)} %get-tuple-element.44) | copy-start | bytes 18436
  62.9 132.9 %copy-start.76 = (f32[1536]{0:T(1024)}, f32[1536]{0:T(1024)S(1)}, u32[]{:S(2)}) copy-start(f32[1536]{0:T(1024)S(1)} %convert_element_type.319) | copy-start | bytes 18436
  63.0 701.9 %copy-start.72 = (f32[1536]{0:T(1024)}, f32[1536]{0:T(1024)S(1)}, u32[]{:S(2)}) copy-start(f32[1536]{0:T(1024)S(1)} %convert_element_type.322) | copy-start | bytes 18436
  63.0 744.8 %copy-start.95 = (f32[64]{0:T(128)}, f32[64]{0:T(128)S(1)}, u32[]{:S(2)}) copy-start(f32[64]{0:T(128)S(1)} %convert_element_type.325) | copy-start | bytes 772
  146.7 5.5 collective-permute-start.1
  152.2 5.6 collective-permute-start
  195.3 558.4 %copy-start.26 = (f32[256,1536]{1,0:T(8,128)}, f32[256,1536]{1,0:T(8,128)S(1)}, u32[]{:S(2)}) copy-start(f32[256,1536]{1,0:T(8,128)S(1)} %get-tuple-element.110) | copy-start | bytes 4718596
  195.8 196.8 %copy-start.91 = (f32[256]{0:T(256)}, f32[256]{0:T(256)S(1)}, u32[]{:S(2)}) copy-start(f32[256]{0:T(256)S(1)} %fusion.78) | copy-start | bytes 3076
  196.0 370.3 %copy-start.20 = (bf16[256,1536]{1,0:T(8,128)(2,1)}, bf16[256,1536]{1,0:T(8,128)(2,1)S(1)}, u32[]{:S(2)}) copy-start(bf16[256,1536]{1,0:T(8,128)(2,1)S(1)} %multiply_convert_fusion.9) | copy-start | bytes 2359300
  764.8 203.5 %copy-start.12 = (f32[256,1536]{1,0:T(8,128)}, f32[256,1536]{1,0:T(8,128)S(1)}, u32[]{:S(2)}) copy-start(f32[256,1536]{1,0:T(8,128)S(1)} %get-tuple-element.114) | copy-start | bytes 4718596
  765.0 93.2 %copy-start.14 = (bf16[256,1536]{1,0:T(8,128)(2,1)}, bf16[256,1536]{1,0:T(8,128)(2,1)S(1)}, u32[]{:S(2)}) copy-start(bf16[256,1536]{1,0:T(8,128)(2,1)S(1)} %multiply_convert_fusion.8) | copy-start | bytes 2359300
  782.2 133.8 %all-gather.32.cloned.1.call-start = ((), (), s32[]{:S(2)}) async-start(), calls=%async_computation.23 | async-start | bytes 1310720 | tf_op jit(solution)/shard_map/all_gather | solution.py:274
  782.5 81.6 %copy-start.53 = (f32[256,32]{0,1:T(8,128)}, f32[256,32]{0,1:T(8,128)S(1)}, u32[]{:S(2)}) copy-start(f32[256,32]{0,1:T(8,128)S(1)} %get-tuple-element.105) | copy-start | bytes 98308
  782.5 81.6 %copy-start.55 = (f32[256,32]{0,1:T(8,128)}, f32[256,32]{0,1:T(8,128)S(1)}, u32[]{:S(2)}) copy-start(f32[256,32]{0,1:T(8,128)S(1)} %get-tuple-element.106) | copy-start | bytes 98308
  809.6 158.7 %all-gather.36.cloned.1.call-start = ((), (), s32[]{:S(2)}) async-start(), calls=%async_computation.25 | async-start | bytes 5308416 | tf_op jit(solution)/shard_map/all_gather | solution.py:138
  810.3 345.4 %all-gather.38.cloned.1.call-start = ((), (), s32[]{:S(2)}) async-start(), calls=%async_computation.26 | async-start | bytes 23887872 | tf_op jit(solution)/shard_map/all_gather | solution.py:145
  810.9 532.3 %all-gather.40.cloned.1.call-start = ((), (), s32[]{:S(2)}) async-start(), calls=%async_computation.27 | async-start | bytes 23887872 | tf_op jit(solution)/shard_map/all_gather | solution.py:146
  811.6 718.9 %all-gather.42.cloned.1.call-start = ((), (), s32[]{:S(2)}) async-start(), calls=%async_computation.28 | async-start | bytes 23887872 | tf_op jit(solution)/shard_map/all_gather | solution.py:147
  812.2 824.1 %reduce-scatter.20.cloned.1.call-start = ((), (), s32[]{:S(2)}) async-start(), calls=%async_computation.30 | async-start | bytes 1310720 | tf_op jit(solution)/shard_map/reduce_scatter | solution.py:335
  812.7 49.6 %copy-start.97 = (f32[64]{0:T(128)}, f32[64]{0:T(128)S(1)}, u32[]{:S(2)}) copy-start(f32[64]{0:T(128)S(1)} %convert_element_type.328) | copy-start | bytes 772
  864.4 65.5 %copy-start.46 = (bf16[256,24,32]{0,2,1:T(8,128)(2,1)}, bf16[256,24,32]{0,2,1:T(8,128)(2,1)S(1)}, u32[]{:S(2)}) copy-start(bf16[256,24,32]{0,2,1:T(8,128)(2,1)S(1)} %get-tuple-element.85) | copy-start | bytes 1179652
  864.4 65.5 %copy-start.48 = (bf16[256,24,32]{0,2,1:T(8,128)(2,1)}, bf16[256,24,32]{0,2,1:T(8,128)(2,1)S(1)}, u32[]{:S(2)}) copy-start(bf16[256,24,32]{0,2,1:T(8,128)(2,1)S(1)} %get-tuple-element.86) | copy-start | bytes 1179652
  888.8 41.2 %copy-start.50 = (bf16[1024,512]{0,1:T(8,128)(2,1)}, bf16[1024,512]{0,1:T(8,128)(2,1)S(1)}, u32[]{:S(2)}) copy-start(bf16[1024,512]{0,1:T(8,128)(2,1)S(1)} %copy.75) | copy-start | bytes 3145732
  972.4 604.7 %copy-start.24 = (f32[256,1536]{1,0:T(8,128)}, f32[256,1536]{1,0:T(8,128)S(1)}, u32[]{:S(2)}) copy-start(f32[256,1536]{1,0:T(8,128)S(1)} %get-tuple-element.120) | copy-start | bytes 4718596
  972.6 370.6 %copy-start.22 = (bf16[256,1536]{1,0:T(8,128)(2,1)}, bf16[256,1536]{1,0:T(8,128)(2,1)S(1)}, u32[]{:S(2)}) copy-start(bf16[256,1536]{1,0:T(8,128)(2,1)S(1)} %multiply_convert_fusion.7) | copy-start | bytes 2359300
  1169.3 361.2 %copy-start.34 = (bf16[1,256,1536]{2,1,0:T(8,128)(2,1)S(1)}, bf16[1,256,1536]{2,1,0:T(8,128)(2,1)}, u32[]{:S(2)}) copy-start(bf16[1,256,1536]{2,1,0:T(8,128)(2,1)} %param.22) | copy-start | bytes 2359300
  1608.4 59.2 %reduce-scatter.18.cloned.1.call-start = ((), (), s32[]{:S(2)}) async-start(), calls=%async_computation.29 | async-start | bytes 1310720 | tf_op jit(solution)/shard_map/reduce_scatter | solution.py:329
  1631.5 37.0 copy-start.54
  1631.5 37.0 copy-start.56
  1631.5 37.1 copy-start.17
  1631.5 37.1 copy-start.75
  1631.5 37.1 copy-start.96
  1631.6 225.2 %reduce-scatter.36.cloned.1.call-start = ((), (), s32[]{:S(2)}) async-start(), calls=%async_computation.38 | async-start | bytes 1769472 | tf_op jit(solution)/shard_map/reduce_scatter | solution.py:371
  1639.3 217.5 %reduce-scatter.34.cloned.1.call-start = ((), (), s32[]{:S(2)}) async-start(), calls=%async_computation.37 | async-start | bytes 1769472 | tf_op jit(solution)/shard_map/reduce_scatter | solution.py:368
  1671.4 185.4 %reduce-scatter.32.cloned.1.call-start = ((), (), s32[]{:S(2)}) async-start(), calls=%async_computation.36 | async-start | bytes 5308416 | tf_op jit(solution)/shard_map/reduce_scatter | solution.py:365
  1684.9 171.9 %reduce-scatter.38.cloned.1.call-start = ((), (), s32[]{:S(2)}) async-start(), calls=%async_computation.39 | async-start | bytes 5308416 | tf_op jit(solution)/shard_map/reduce_scatter | solution.py:380
  1690.2 213.8 %reduce-scatter.24.cloned.1.call-start = ((), (), s32[]{:S(2)}) async-start(), calls=%async_computation.32 | async-start | bytes 5308416 | tf_op jit(solution)/shard_map/reduce_scatter | solution.py:436
  1697.9 46.1 %copy-start.10 = (f32[256,1536]{1,0:T(8,128)}, f32[256,1536]{1,0:T(8,128)S(1)}, u32[]{:S(2)}) copy-start(f32[256,1536]{1,0:T(8,128)S(1)} %fusion.33) | copy-start | bytes 4718596
  1748.8 300.0 %reduce-scatter.22.cloned.1.call-start = ((), (), s32[]{:S(2)}) async-start(), calls=%async_computation.31 | async-start | bytes 15925248 | tf_op jit(solution)/shard_map/reduce_scatter | solution.py:430
  1756.2 4.9 collective-permute-start.3
  1759.7 5.6 collective-permute-start.2
  1775.7 484.0 %reduce-scatter.40.cloned.1.call-start = ((), (), s32[]{:S(2)}) async-start(), calls=%async_computation.40 | async-start | bytes 23887872 | tf_op jit(solution)/shard_map/reduce_scatter | solution.py:153
  1789.3 681.3 %reduce-scatter.42.cloned.1.call-start = ((), (), s32[]{:S(2)}) async-start(), calls=%async_computation.41 | async-start | bytes 23887872 | tf_op jit(solution)/shard_map/reduce_scatter | solution.py:156
  1801.9 879.6 %reduce-scatter.44.cloned.1.call-start = ((), (), s32[]{:S(2)}) async-start(), calls=%async_computation.42 | async-start | bytes 23887872 | tf_op jit(solution)/shard_map/reduce_scatter | solution.py:159
  1815.4 1077.0 %reduce-scatter.30.cloned.1.call-start = ((), (), s32[]{:S(2)}) async-start(), calls=%async_computation.35 | async-start | bytes 23887872 | tf_op jit(solution)/shard_map/reduce_scatter | solution.py:159
  1829.3 1273.9 %reduce-scatter.26.cloned.1.call-start = ((), (), s32[]{:S(2)}) async-start(), calls=%async_computation.33 | async-start | bytes 23887872 | tf_op jit(solution)/shard_map/reduce_scatter | solution.py:153
  1842.8 1471.4 %reduce-scatter.28.cloned.1.call-start = ((), (), s32[]{:S(2)}) async-start(), calls=%async_computation.34 | async-start | bytes 23887872 | tf_op jit(solution)/shard_map/reduce_scatter | solution.py:156
  1855.5 1507.7 %reduce-scatter.46.cloned.1.call-start = ((), (), s32[]{:S(2)}) async-start(), calls=%async_computation.43 | async-start | bytes 442368
  1856.6 1865.9 %all-reduce.24.cloned.1.call-start = ((), (), s32[]{:S(2)}) async-start(), calls=%async_computation.44 | async-start | bytes 39714816 | tf_op jit(solution)/shard_map/psum | solution.py:445
  (90 other events, 612.7 us)
Sparse Core Ops, SparseCore 0:
  9.7 129.4 all-gather.15
  140.8 50.5 all-gather.17
  193.1 185.8 all-gather.19
  380.5 185.8 all-gather.21
  567.8 185.8 all-gather.23
  755.2 24.2 all-gather.25
  781.1 24.5 all-gather.29
  807.4 50.7 all-gather.33
  860.6 26.6 all-gather.27
  889.5 26.4 all-gather.31
  917.7 50.5 all-gather.35
  969.8 185.8 all-gather.37
  1157.3 185.8 all-gather.39
  1344.6 185.8 all-gather.41
  1608.5 27.6 reduce-scatter.19
  1639.8 27.6 reduce-scatter.17
  1669.7 27.5 reduce-scatter.35
  1699.5 32.4 reduce-scatter.33
  1734.8 56.8 reduce-scatter.31
  1794.4 53.3 reduce-scatter.37
  1850.7 53.3 reduce-scatter.23
  1906.3 142.4 reduce-scatter.21
  2051.2 208.5 reduce-scatter.39
  2262.1 208.5 reduce-scatter.41
  2473.0 208.5 reduce-scatter.43
  2683.9 208.5 reduce-scatter.29
  2894.6 208.5 reduce-scatter.25
  3105.7 208.5 reduce-scatter.27
  3317.1 25.4 reduce-scatter.45
  3349.3 373.2 all-reduce.23
where the time goes:
time: 3760 us
  waiting for transfers between devices  3180 us (85%)
  matrix products  384 us (10%)
  blocking collectives  78.1 us (2%)
  other arithmetic  64.3 us (2%)
    reduce_scatter x2, waiting for transfers between devices, ff_grads(): lax.psum_scatter(up_grad.astype(jnp.bfloat16), 'fsdp', scatter_dimension=...  422 us
    reduce_scatter x2, waiting for transfers between devices, ff_grads(): lax.psum_scatter(down_grad.astype(jnp.bfloat16), 'fsdp', scatter_dimensio...  422 us
    reduce_scatter x2, waiting for transfers between devices, ff_grads(): lax.psum_scatter(gate_grad.astype(jnp.bfloat16), 'fsdp', scatter_dimensio...  422 us
    all_gather x2, waiting for transfers between devices, ff_weights(): lax.all_gather(gate, 'fsdp', axis=0, tiled=True)  366 us
    all_gather x2, waiting for transfers between devices, ff_weights(): lax.all_gather(up_w, 'fsdp', axis=0, tiled=True)  347 us
    all_gather x2, waiting for transfers between devices, ff_weights(): lax.all_gather(down, 'fsdp', axis=0, tiled=True)  345 us
    psum x1, waiting for transfers between devices, local(): lax.psum(mix_shares[1].astype(jnp.bfloat16), 'ctx').astype(jnp.float32)  344 us
    reduce_scatter x1, waiting for transfers between devices, local(): lax.psum_scatter(grad_mix_in.astype(jnp.bfloat16), 'fsdp', scatter_dimens...  145 us
  transfers between devices with their start and end apart: 34, of which 28 were waited for; matrix products, arithmetic and copies ran while one was open for 9% of the time, Pallas kernels for 0%

commit v1 on v0

v1 whole, which is shorter than its diff:
```python
from functools import partial

import jax
import jax.numpy as jnp
from jax import lax
from jax.experimental import pallas as pl
from jax.experimental.pallas import tpu as pltpu
from jax.sharding import PartitionSpec as P

MODEL_WIDTH = 1536
QUERY_HEADS = 24
KEY_VALUE_HEADS = 8
HEAD_SIZE = 64
KW = 3


EPS = 1e-05
THETA = 1000000.0
NEG = -1e30


def extended_2(array, sides, width):
    for axis, dim in sides:
        size, length = (lax.axis_size(axis), array.shape[dim])
        up = [(i, (i + 1) % size) for i in range(size - 1)]
        down = [(j, i) for i, j in up]
        last = lax.slice_in_dim(array, length - width, length, axis=dim)
        first = lax.slice_in_dim(array, 0, width, axis=dim)
        before = lax.ppermute(last, axis, up)
        after = lax.ppermute(first, axis, down)
        array = jnp.concatenate([before, array, after], axis=dim)
    return array


def rms_scale(value, gain):
    return value * lax.rsqrt(jnp.mean(value * value, axis=-1, keepdims=True) + EPS) * gain


def rotate(value, places):
    half_dim = value.shape[-1] // 2
    freqs = THETA ** (-jnp.arange(half_dim, dtype=jnp.float32) * 2.0 / value.shape[-1])
    angles = places[:, None] * freqs[None, :]
    cosine = jnp.cos(angles)[:, None, :]
    sine = jnp.sin(angles)[:, None, :]
    first = value[..., :half_dim]
    second = value[..., half_dim:]
    return jnp.concatenate(
        [first * cosine - second * sine, second * cosine + first * sine], axis=-1
    )


def head_prep(raw, gain, places):
    width = gain.shape[0]
    heads = raw.reshape(raw.shape[0], raw.shape[1] // width, width)
    return rotate(rms_scale(heads, gain), places)


def dot_rows(left, right):
    return lax.dot_general(
        left, right, (((1,), (1,)), ((), ())), preferred_element_type=jnp.float32
    )


def dot_cols(left, right):
    return lax.dot_general(
        left, right, (((0,), (0,)), ((), ())), preferred_element_type=jnp.float32
    )


def dot_plain(left, right):
    return jnp.dot(left, right, preferred_element_type=jnp.float32)


def swish_product(gate_val, up_val):
    return jax.nn.silu(gate_val) * up_val


def dealt_places(index, block, ctx_count):
    device = index // (2 * block)
    within = index % (2 * block)
    which = jnp.where(within < block, device, 2 * ctx_count - 1 - device)
    return which * block + within % block


def conv_apply(extended, kernel):
    sequence_length = extended.shape[0] - KW + 1
    total = extended[0:sequence_length] * kernel[:, 0]
    for place in range(1, KW):
        total = total + extended[place : place + sequence_length] * kernel[:, place]
    return total


def conv_input_grad(grad_conv, kernel):
    sequence_length = grad_conv.shape[0] + KW - 1
    padded = jnp.pad(grad_conv, ((KW - 1, KW - 1), (0, 0)))
    total = padded[KW - 1 : KW - 1 + sequence_length] * kernel[:, 0]
    for place in range(1, KW):
        total = total + padded[KW - 1 - place : KW - 1 - place + sequence_length] * kernel[:, place]
    return total


def kernel_grad(extended, grad_conv):
    sequence_length = grad_conv.shape[0]
    columns = [
        jnp.sum(grad_conv * extended[place : place + sequence_length], axis=0)
        for place in range(KW)
    ]
    return jnp.stack(columns, axis=1)


def masked_scores(query_narrow, grouped_key_rows, query_places, key_places):
    scores = jnp.einsum(
        "rhgd,lhd->hgrl", query_narrow, grouped_key_rows, preferred_element_type=jnp.float32
    )
    scores = scores * query_narrow.shape[-1] ** (-0.5)
    allowed = query_places[:, None] >= key_places[None, :]
    return jnp.where(allowed, scores, NEG)


def ff_weight_grads(inputs, grad_out, hidden, gate_low, up_low):
    inputs, grad_out, hidden, gate_low, up_low = [
        one.reshape(-1, one.shape[-1]) for one in (inputs, grad_out, hidden, gate_low, up_low)
    ]
    return (
        dot_cols(gate_low, inputs).astype(jnp.bfloat16),
        dot_cols(up_low, inputs).astype(jnp.bfloat16),
        dot_cols(hidden, grad_out).astype(jnp.bfloat16),
    )


def pick(value, index, axis):
    return lax.dynamic_index_in_dim(value, index, axis, keepdims=False)


def ring_sources():
    size = lax.axis_size("fsdp")
    place = lax.axis_index("fsdp")
    shard = jnp.arange(size, dtype=jnp.int32)
    hops = (place // 2 - shard // 2) % (size // 2)
    return 2 * hops + (shard + place) % 2


MESH = pl.DeviceIdType.MESH


def dims_nt(left, right):
    return lax.dot_general(
        left, right, (((1,), (1,)), ((), ())), preferred_element_type=jnp.float32
    )


def ff_kernel(chips, mode, *refs):
    forward = mode == "forward"
    if forward:
        x_ref, gate, up_w, down, out, xall = refs[:6]
        rest = refs[6:]
    else:
        x_ref, y_hbm, gate, up_w, down, out, xall, hid, dgate, dup = refs[:10]
        rest = refs[10:]
    part, other_send, other_recv, sum_send, sum_recv = rest[:5]
    ag_send, ag_recv, core_send, core_recv, ps_send, ps_recv, rs_send, rs_recv = rest[5:13]
    if not forward:
        ybuf, ysem = rest[13:]
    place = lax.axis_index("fsdp")
    chip = place // 2
    core = place % 2
    after = lax.rem(chip + 1, chips) * 2 + core
    before = lax.rem(chip + chips - 1, chips) * 2 + core
    peer = chip * 2 + 1 - core
    barrier = pltpu.get_barrier_semaphore()
    for target in (before, peer):
        pl.semaphore_signal(barrier, inc=1, device_id={"fsdp": target}, device_id_type=MESH)
    pl.semaphore_wait(barrier, 2)

    def remote(src, dst, send, recv, target):
        return pltpu.make_async_remote_copy(
            src_ref=src, dst_ref=dst, send_sem=send, recv_sem=recv,
            device_id={"fsdp": target}, device_id_type=MESH,
        )

    def ring_copy(k):
        return remote(xall.at[k, 0], xall.at[k + 1, 0], ag_send.at[k], ag_recv.at[k + 1], after)

    def core_copy(k):
        return remote(xall.at[k, 0], xall.at[k, 1], core_send.at[k], core_recv.at[k], peer)

    def part_copy(k):
        return remote(other_send.at[k], other_recv.at[k], ps_send.at[k], ps_recv.at[k], peer)

    def sum_copy(k):
        return remote(sum_send.at[k], sum_recv.at[k], rs_send.at[k], rs_recv.at[k], after)

    def y_copy(k, o):
        return pltpu.make_async_copy(y_hbm.at[k, o], ybuf.at[o], ysem.at[o])

    def block(k, o):
        x = xall[k, o]
        if forward:
            gate_val = dims_nt(x, gate[...])
            up_val = dims_nt(x, up_w[...])
            hidden = (gate_val / (1.0 + jnp.exp(-gate_val)) * up_val).astype(jnp.bfloat16)
            return jnp.dot(hidden, down[...], preferred_element_type=jnp.float32)
        y_copy(k, o).wait()
        y = ybuf[o]
        a, g = (x, y) if mode == "both" else (y, x)
        gate_val = dims_nt(a, gate[...])
        up_val = dims_nt(a, up_w[...])
        grad_hidden = dims_nt(g, down[...])
        sig = 1.0 / (1.0 + jnp.exp(-gate_val))
        act = gate_val * sig
        hid[k, o] = (act * up_val).astype(jnp.bfloat16)
        dup[k, o] = (grad_hidden * act).astype(jnp.bfloat16)
        dgate[k, o] = (
            grad_hidden * up_val * (sig * (1.0 + gate_val * (1.0 - sig)))
        ).astype(jnp.bfloat16)
        return jnp.dot(dgate[k, o], gate[...], preferred_element_type=jnp.float32) + jnp.dot(
            dup[k, o], up_w[...], preferred_element_type=jnp.float32
        )

    xall[0, 0] = x_ref[...]

    @pl.loop(0, chips)
    def _(k):
        if not forward:
            y_copy(k, 0).start()
            y_copy(k, 1).start()

        @pl.when(k > 0)
        def _():
            ring_copy(k - 1).wait_recv()

        @pl.when(k < chips - 1)
        def _():
            ring_copy(k).start()

        core_copy(k).start()
        own = jnp.minimum(k, 1)

        @pl.loop(0, 2)
        def _(o):
            @pl.when(o == 1)
            def _():
                core_copy(k).wait_recv()

            value = block(k, o)

            @pl.when(o == 0)
            def _():
                part[own] = value

            @pl.when(o == 1)
            def _():
                other_send[k] = value.astype(jnp.bfloat16)
                part_copy(k).start()

        @pl.when(k > 0)
        def _():
            part_copy(k).wait_recv()

            @pl.when(k == 1)
            def _():
                sum_send[k] = (part[1] + other_recv[k].astype(jnp.float32)).astype(jnp.bfloat16)

            @pl.when(k > 1)
            def _():
                sum_copy(k - 1).wait_recv()
                sum_send[k] = (
                    part[1]
                    + other_recv[k].astype(jnp.float32)
                    + sum_recv[k - 1].astype(jnp.float32)
                ).astype(jnp.bfloat16)

            sum_copy(k).start()

    part_copy(0).wait_recv()
    sum_copy(chips - 1).wait_recv()
    out[...] = (
        part[0] + other_recv[0].astype(jnp.float32) + sum_recv[chips - 1].astype(jnp.float32)
    )

    @pl.loop(0, chips)
    def _(k):
        core_copy(k).wait_send()
        part_copy(k).wait_send()

        @pl.when(k < chips - 1)
        def _():
            ring_copy(k).wait_send()

        @pl.when(k > 0)
        def _():
            sum_copy(k).wait_send()


def ff_call(mode, ident, x, gate, up_w, down, given=None):
    chips = lax.axis_size("fsdp") // 2
    rows, width = x.shape
    units = gate.shape[0]
    forward = mode == "forward"
    blocks = jax.ShapeDtypeStruct((chips, 2, rows, width), jnp.bfloat16)
    inner = jax.ShapeDtypeStruct((chips, 2, rows, units), jnp.bfloat16)
    vmem = pl.BlockSpec(memory_space=pltpu.VMEM)
    outs = [jax.ShapeDtypeStruct((rows, width), jnp.float32), blocks]
    args = [x, gate, up_w, down]
    specs = [vmem] * 4
    dma = pltpu.SemaphoreType.DMA
    scratch = [pltpu.VMEM((2, rows, width), jnp.float32)]
    scratch += [pltpu.VMEM((chips, rows, width), jnp.bfloat16)] * 4
    scratch += [dma((chips,))] * 8
    if not forward:
        outs += [inner] * 3
        args.insert(1, given)
        specs.insert(1, pl.BlockSpec(memory_space=pl.ANY))
        scratch += [pltpu.VMEM((2, rows, width), jnp.bfloat16), dma((2,))]
    total = chips * 2 * rows
    products = 3 if forward else 5
    return pl.pallas_call(
        partial(ff_kernel, chips, mode),
        out_shape=outs,
        in_specs=specs,
        out_specs=[vmem] * len(outs),
        scratch_shapes=scratch,
        compiler_params=pltpu.CompilerParams(
            collective_id=ident, has_side_effects=True, vmem_limit_bytes=60 * 2**20
        ),
        cost_estimate=pl.CostEstimate(
            flops=2 * products * total * units * width,
            bytes_accessed=4 * total * width,
            transcendentals=total * units,
        ),
    )(*args)


def places():
    count = lax.axis_size("fsdp") // 2
    place = lax.axis_index("fsdp")
    chip = place // 2
    core = place % 2
    after = lax.rem(chip + 1, count) * 2 + core
    before = lax.rem(chip + count - 1, count) * 2 + core
    return place, chip, core, after, before, chip * 2 + 1 - core


def greet(targets):
    barrier = pltpu.get_barrier_semaphore()
    for target in targets:
        pl.semaphore_signal(barrier, inc=1, device_id=target, device_id_type=MESH)
    pl.semaphore_wait(barrier, len(targets))


def push(src, dst, send, recv, target):
    return pltpu.make_async_remote_copy(
        src_ref=src, dst_ref=dst, send_sem=send, recv_sem=recv,
        device_id=target, device_id_type=MESH,
    )


def head_kernel(chips, count, *refs):
    shards = refs[:2]
    block, vector = refs[2:4]
    wholes = refs[4:6]
    blocks, vectors = refs[6:8]
    local, near_s, near_r, hop_s, hop_r, side_s, side_r, pass_s, pass_r = refs[8:]
    place, chip, core, after, before, peer = places()
    here = lax.axis_index("ctx")
    others = [{"ctx": lax.rem(here + t, count)} for t in range(1, count)]
    greet([{"fsdp": before}, {"fsdp": peer}] + others)
    started = []

    def go(copy):
        copy.start()
        started.append(copy)

    def shard_of(k):
        return lax.rem(chip + chips - k, chips) * 2 + core

    def hop(k, n):
        owner = shard_of(k)
        if n < 2:
            src = shards[n].at[here] if k == 0 else wholes[n].at[owner, here]
            dst = wholes[n].at[owner, here]
        elif n == 2:
            src = block if k == 0 else blocks.at[k, 0]
            dst = blocks.at[k + 1, 0]
        else:
            src = vector if k == 0 else vectors.at[owner]
            dst = vectors.at[owner]
        return push(src, dst, hop_s.at[n, k], hop_r.at[n, k], {"fsdp": after})

    def side(k, t, n):
        piece = wholes[n].at[shard_of(k), here]
        return push(piece, piece, side_s.at[n, k, t], side_r.at[n, k, t], others[t - 1])

    def side_in(k, t, n):
        piece = wholes[n].at[shard_of(k), lax.rem(here + count - t, count)]
        return piece, push(piece, piece, side_s.at[n, k, t], side_r.at[n, k, t], others[t - 1])

    def across(k, t, n):
        if n == 2:
            src, dst = blocks.at[k, 0], blocks.at[k, 1]
        elif n == 3:
            src = dst = vectors.at[shard_of(k)]
        else:
            src = dst = wholes[n].at[shard_of(k), lax.rem(here + count - t, count)]
        return push(src, dst, pass_s.at[n, k, t], pass_r.at[n, k, t], {"fsdp": peer})

    def across_in(k, t, n):
        owner = lax.rem(chip + chips - k, chips) * 2 + 1 - core
        if n == 2:
            dst = blocks.at[k, 1]
        elif n == 3:
            dst = vectors.at[owner]
        else:
            dst = wholes[n].at[owner, lax.rem(here + count - t, count)]
        return push(dst, dst, pass_s.at[n, k, t], pass_r.at[n, k, t], {"fsdp": peer})

    homes = [wholes[0].at[place], wholes[1].at[place], blocks.at[0, 0], vectors.at[place]]
    far = [wholes[0].at[place], wholes[1].at[place], blocks.at[0, 1], vectors.at[place]]
    came = [wholes[0].at[peer], wholes[1].at[peer], blocks.at[0, 1], vectors.at[peer]]
    sources = [shards[0], shards[1], block, vector]
    order = (3, 0, 1, 2)
    for n in order:
        go(hop(0, n))
    keeps = [pltpu.make_async_copy(sources[n], homes[n], local.at[n]) for n in order]
    for one in keeps:
        one.start()
    for n in order:
        go(push(sources[n], far[n], near_s.at[n], near_r.at[n], {"fsdp": peer}))
    for k in range(1, chips):
        for n in order:
            hop(k - 1, n).wait_recv()
            if k < chips - 1:
                go(hop(k, n))
            if n < 2:
                for t in range(1, count):
                    go(side(k, t, n))
            go(across(k, 0, n))
        if k > 1:
            for n in range(2):
                for t in range(1, count):
                    side_in(k - 1, t, n)[1].wait_recv()
                    go(across(k - 1, t, n))
    for n in range(2):
        for t in range(1, count):
            side_in(chips - 1, t, n)[1].wait_recv()
            go(across(chips - 1, t, n))
    for n in order:
        push(came[n], came[n], near_s.at[n], near_r.at[n], {"fsdp": peer}).wait_recv()
        for k in range(1, chips):
            for t in range(count if n < 2 else 1):
                across_in(k, t, n).wait_recv()
    for one in keeps:
        one.wait()
    for one in started:
        one.wait_send()


def head_call(ident, shard_a, shard_b, block, vector):
    size = lax.axis_size("fsdp")
    count = lax.axis_size("ctx")
    chips = size // 2
    width = shard_a.shape[1]
    shards = [one.reshape(count, -1, width) for one in (shard_a, shard_b)]
    outs = [jax.ShapeDtypeStruct((size,) + one.shape, jnp.bfloat16) for one in shards]
    outs.append(jax.ShapeDtypeStruct((chips, 2) + block.shape, jnp.bfloat16))
    outs.append(jax.ShapeDtypeStruct((size,) + vector.shape, jnp.bfloat16))
    anywhere = pl.BlockSpec(memory_space=pl.ANY)
    dma = pltpu.SemaphoreType.DMA
    whole_a, whole_b, blocks, vectors = pl.pallas_call(
        partial(head_kernel, chips, count),
        out_shape=outs,
        in_specs=[anywhere] * 4,
        out_specs=[anywhere] * 4,
        scratch_shapes=[
            dma((4,)), dma((4,)), dma((4,)),
            dma((4, chips)), dma((4, chips)),
            dma((2, chips, count)), dma((2, chips, count)),
            dma((4, chips, count)), dma((4, chips, count)),
        ],
        compiler_params=pltpu.CompilerParams(collective_id=ident, has_side_effects=True),
        cost_estimate=pl.CostEstimate(
            flops=0, bytes_accessed=2 * size * (shard_a.size + shard_b.size) * 2, transcendentals=0
        ),
    )(*shards, block, vector)
    return whole_a.reshape(-1, width), whole_b.reshape(-1, width), blocks, vectors


def tail_kernel(chips, count, pieces, *refs):
    number = len(pieces)
    grads = refs[:number]
    factor, inputs = refs[number : number + 2]
    total, total_in = refs[number + 2 : number + 4]
    own, near, out_sum, in_sum, fin, rc, fs, held, fin_in, rc_in, fs_in = refs[number + 4 : number + 15]
    (own_m, near_s, near_r, ring_s, ring_r, sc_s, sc_r, ag_s, ag_r, fac_m, fac_s, fac_r,
     sci_s, sci_r, agi_s, agi_r) = refs[number + 15 :]
    place, chip, core, after, before, peer = places()
    here = lax.axis_index("ctx")
    size = 2 * chips
    chunks = sum(pieces)
    ctx_others = [{"ctx": lax.rem(here + t, count)} for t in range(1, count)]
    shard_others = [{"fsdp": lax.rem(place + t, size)} for t in range(1, size)]
    greet(ctx_others + shard_others)

    def factor_copy(t):
        there = lax.rem(place + t, size)
        return push(factor.at[there], held.at[place], fac_s.at[t], fac_r.at[t], {"fsdp": there})

    for t in range(1, size):
        factor_copy(t).start()
    keep = pltpu.make_async_copy(factor.at[place], held.at[place], fac_m)
    keep.start()

    bases = [sum(pieces[:n]) for n in range(number)]

    def near_copy(n, j):
        at = bases[n] + j
        return push(
            grads[n].at[:, 1 - core, j], near.at[at], near_s.at[at], near_r.at[at], {"fsdp": peer}
        )

    def own_copy(n, j):
        at = bases[n] + j
        return pltpu.make_async_copy(grads[n].at[:, core, j], own.at[at], own_m.at[at])

    for n in range(number):
        @pl.loop(0, pieces[n])
        def _(j):
            near_copy(n, j).start()
            own_copy(n, j).start()

    def ring_copy(k, j):
        return push(
            out_sum.at[k, j], in_sum.at[k, j], ring_s.at[k, j], ring_r.at[k, j], {"fsdp": after}
        )

    def near_in(j):
        return push(near.at[j], near.at[j], near_s.at[j], near_r.at[j], {"fsdp": peer})

    def own_in(j):
        return pltpu.make_async_copy(own.at[j], own.at[j], own_m.at[j])

    def term(j, owner):
        return own[j, owner].astype(jnp.float32) + near[j, owner].astype(jnp.float32)

    def scatter_copy(j, t):
        there = lax.rem(here + t, count)
        return push(fin.at[j, there], rc.at[j, t], sc_s.at[j, t], sc_r.at[j, t], {"ctx": there})

    def gather_copy(j, t):
        return push(
            fs.at[j], total.at[j, here], ag_s.at[j, t], ag_r.at[j, t], ctx_others[t - 1]
        )

    def gather_in(j, t):
        there = total.at[j, lax.rem(here + count - t, count)]
        return push(there, there, ag_s.at[j, t], ag_r.at[j, t], ctx_others[t - 1])

    def scatter_in_copy(t):
        there = lax.rem(here + t, count)
        return push(fin_in.at[there], rc_in.at[t], sci_s.at[t], sci_r.at[t], {"ctx": there})

    def gather_in_copy(t):
        return push(fs_in, total_in.at[here], agi_s.at[t], agi_r.at[t], ctx_others[t - 1])

    def gather_in_wait(t):
        there = total_in.at[lax.rem(here + count - t, count)]
        return push(there, there, agi_s.at[t], agi_r.at[t], ctx_others[t - 1])

    def products():
        for t in range(1, size):
            src = held.at[lax.rem(place + size - t, size)]
            push(src, src, fac_s.at[t], fac_r.at[t], {"fsdp": peer}).wait_recv()
        keep.wait()

        @pl.loop(0, count)
        def _(c):
            sums = jnp.dot(held[0, c], inputs[0], preferred_element_type=jnp.float32)
            for s in range(1, size):
                sums = sums + jnp.dot(held[s, c], inputs[s], preferred_element_type=jnp.float32)
            fin_in[c] = sums.astype(jnp.bfloat16)

        for t in range(1, count):
            scatter_in_copy(t).start()

    def products_sum():
        sums = fin_in[here].astype(jnp.float32)
        for t in range(1, count):
            scatter_in_copy(t).wait_recv()
            sums = sums + rc_in[t].astype(jnp.float32)
        fs_in[...] = sums.astype(jnp.bfloat16)
        for t in range(1, count):
            gather_in_copy(t).start()
        total_in[here] = fs_in[...]

    @pl.loop(1, chips)
    def _(k):
        owner = lax.rem(chip + chips - k, chips)

        @pl.loop(0, chunks)
        def _(j):
            @pl.when(k == 1)
            def _():
                own_in(j).wait()
                near_in(j).wait_recv()
                out_sum[0, j] = term(j, owner).astype(jnp.bfloat16)

            @pl.when(k > 1)
            def _():
                ring_copy(k - 2, j).wait_recv()
                out_sum[k - 1, j] = (
                    term(j, owner) + in_sum[k - 2, j].astype(jnp.float32)
                ).astype(jnp.bfloat16)

            ring_copy(k - 1, j).start()

        @pl.when(k == 1)
        def _():
            products()

        @pl.when(k == 2)
        def _():
            products_sum()

    @pl.loop(0, chunks)
    def _(j):
        ring_copy(chips - 2, j).wait_recv()
        fin[j] = (term(j, chip) + in_sum[chips - 2, j].astype(jnp.float32)).astype(jnp.bfloat16)
        for t in range(1, count):
            scatter_copy(j, t).start()

    @pl.loop(0, chunks)
    def _(j):
        sums = fin[j, here].astype(jnp.float32)
        for t in range(1, count):
            scatter_copy(j, t).wait_recv()
            sums = sums + rc[j, t].astype(jnp.float32)
        fs[j] = sums.astype(jnp.bfloat16)
        for t in range(1, count):
            gather_copy(j, t).start()
        total[j, here] = fs[j]

    @pl.loop(0, chunks)
    def _(j):
        for t in range(1, count):
            gather_in(j, t).wait_recv()
            gather_copy(j, t).wait_send()
            scatter_copy(j, t).wait_send()

        near_in(j).wait_send()

        @pl.loop(0, chips - 1)
        def _(k):
            ring_copy(k, j).wait_send()

    for t in range(1, count):
        gather_in_wait(t).wait_recv()
        gather_in_copy(t).wait_send()
        scatter_in_copy(t).wait_send()
    for t in range(1, size):
        factor_copy(t).wait_send()


def tail_call(ident, grads, factor, inputs):
    size = lax.axis_size("fsdp")
    count = lax.axis_size("ctx")
    chips = size // 2
    width = inputs.shape[2]
    rows = inputs.shape[1]
    unit = min(one.shape[1] for one in grads) // 3
    pieces = [one.shape[1] // unit for one in grads]
    chunks = sum(pieces)
    part = unit // count
    views = [
        one.reshape(chips, 2, n, count, part, width) for one, n in zip(grads, pieces)
    ]
    factor = factor.T.reshape(size, count, -1, rows)
    mine = factor.shape[2]
    bf16 = jnp.bfloat16
    anywhere = pl.BlockSpec(memory_space=pl.ANY)
    vmem = pl.BlockSpec(memory_space=pltpu.VMEM)
    dma = pltpu.SemaphoreType.DMA
    total, total_in = pl.pallas_call(
        partial(tail_kernel, chips, count, pieces),
        out_shape=[
            jax.ShapeDtypeStruct((chunks, count, part, width), bf16),
            jax.ShapeDtypeStruct((count, mine, width), bf16),
        ],
        in_specs=[anywhere] * (len(views) + 1) + [vmem],
        out_specs=[vmem] * 2,
        scratch_shapes=[
            pltpu.VMEM((chunks, chips, count, part, width), bf16),
            pltpu.VMEM((chunks, chips, count, part, width), bf16),
            pltpu.VMEM((chips - 1, chunks, count, part, width), bf16),
            pltpu.VMEM((chips - 1, chunks, count, part, width), bf16),
            pltpu.VMEM((chunks, count, part, width), bf16),
            pltpu.VMEM((chunks, count, part, width), bf16),
            pltpu.VMEM((chunks, part, width), bf16),
            pltpu.VMEM((size, count, mine, rows), bf16),
            pltpu.VMEM((count, mine, width), bf16),
            pltpu.VMEM((count, mine, width), bf16),
            pltpu.VMEM((mine, width), bf16),
            dma((chunks,)), dma((chunks,)), dma((chunks,)),
            dma((chips - 1, chunks)), dma((chips - 1, chunks)),
            dma((chunks, count)), dma((chunks, count)), dma((chunks, count)), dma((chunks, count)),
            dma, dma((size,)), dma((size,)),
            dma((count,)), dma((count,)), dma((count,)), dma((count,)),
        ],
        compiler_params=pltpu.CompilerParams(
            collective_id=ident, has_side_effects=True, vmem_limit_bytes=61 * 2**20
        ),
        cost_estimate=pl.CostEstimate(
            flops=2 * size * rows * width * count * mine,
            bytes_accessed=4 * size * chunks * unit * width,
            transcendentals=0,
        ),
    )(*views, factor, inputs)
    total = total.reshape(-1, width).astype(jnp.float32)
    outs = []
    at = 0
    for one in grads:
        outs.append(total[at : at + one.shape[1]])
        at += one.shape[1]
    return outs + [total_in.reshape(-1, width).astype(jnp.float32)]


def local(
    hidden_in,
    cotangent,
    norm_mix,
    in_proj,
    conv_kernel,
    out_proj,
    norm_ff1,
    gate1,
    up1,
    down1,
    norm_attn,
    q_proj,
    key_projection,
    value_projection,
    q_norm,
    k_norm,
    o_proj,
    norm_ff2,
    gate2,
    up2,
    down2,
):
    narrow_dtype = jnp.bfloat16
    start = hidden_in[0].astype(jnp.float32)
    token_rows = start.shape[0]
    block = token_rows // 2
    margin = KW - 1
    ctx_count = lax.axis_size("ctx")
    ctx_place = lax.axis_index("ctx")
    is_last = ctx_place == ctx_count - 1
    query_places = dealt_places(
        ctx_place * token_rows + jnp.arange(token_rows, dtype=jnp.int32), block, ctx_count
    )
    key_places = dealt_places(jnp.arange(token_rows * ctx_count, dtype=jnp.int32), block, ctx_count)
    query_angles = query_places.astype(jnp.float32)
    vectors = (
        norm_mix, norm_ff1, norm_attn, norm_ff2, q_norm, k_norm, conv_kernel.reshape(-1)
    )
    lengths = [one.shape[0] for one in vectors]
    vector = jnp.concatenate(vectors)
    vector = jnp.pad(vector, (0, 2048 - sum(lengths))).reshape(16, 128)
    attn_shard = jnp.concatenate([q_proj, key_projection, value_projection, o_proj], axis=0)
    attn_rows = attn_shard.shape[0]
    attn_slice = pick(attn_shard.reshape(ctx_count, -1, MODEL_WIDTH), ctx_place, 0)
    attn_slices = lax.all_gather(attn_slice, "fsdp", axis=0)
    mix_in, mix_out, given, gathered_vectors = head_call(
        4, in_proj, out_proj, cotangent[0], vector
    )
    attn_slices, mix_in = lax.optimization_barrier((attn_slices, mix_in))
    attn_wholes = lax.all_gather(attn_slices, "ctx", axis=1)
    attn_wholes = attn_wholes.reshape(-1, attn_rows, MODEL_WIDTH)
    gathered_vectors = gathered_vectors.reshape(-1, 2048)
    wholes = []
    at = 0
    for one in lengths:
        wholes.append(gathered_vectors[:, at : at + one].reshape(-1))
        at += one
    mix_norm, ff_norm_one, attn_norm, ff_norm_two, query_gain, key_gain, mix_kernel = wholes
    mix_kernel = mix_kernel.reshape(-1, KW)
    kernel = mix_kernel.astype(jnp.float32)
    normed_one, norm_back_one = jax.vjp(rms_scale, start, mix_norm.astype(jnp.float32))
    normed_one_low = normed_one.astype(narrow_dtype)
    projected = dot_rows(normed_one_low, mix_in)
    b_part = projected[:, :MODEL_WIDTH]
    c_part = projected[:, MODEL_WIDTH : 2 * MODEL_WIDTH]
    x_part = projected[:, 2 * MODEL_WIDTH :]
    mixed_low = (b_part * x_part).astype(narrow_dtype)
    front_tail = mixed_low[block - margin : block]
    back_tail = mixed_low[token_rows - margin :]
    edges = extended_2(jnp.concatenate([back_tail, front_tail], axis=0), (("ctx", 0),), margin)
    before_front = edges[:margin]
    before_back = jnp.where(is_last, front_tail, edges[edges.shape[0] - margin :])
    front_ext = jnp.concatenate([before_front, mixed_low[:block]], axis=0).astype(jnp.float32)
    back_ext = jnp.concatenate([before_back, mixed_low[block:]], axis=0).astype(jnp.float32)
    conv_out = jnp.concatenate(
        [conv_apply(front_ext, kernel), conv_apply(back_ext, kernel)], axis=0
    )
    gated_low = (c_part * conv_out).astype(narrow_dtype)
    first = start + dot_rows(gated_low, mix_out)
    normed_two, norm_back_two = jax.vjp(rms_scale, first, ff_norm_one.astype(jnp.float32))
    ff_out_one, inputs_one = ff_call(
        "forward", 1, normed_two.astype(narrow_dtype), gate1, up1, down1
    )
    second = first + ff_out_one
    attn_parts = []
    at = 0
    for one in (q_proj, key_projection, value_projection, o_proj):
        attn_parts.append(attn_wholes[:, at : at + one.shape[0]].reshape(-1, MODEL_WIDTH))
        at += one.shape[0]
    w_query, w_key, w_value, w_output = attn_parts
    normed_three, norm_back_three = jax.vjp(rms_scale, second, attn_norm.astype(jnp.float32))
    three_low = normed_three.astype(narrow_dtype)
    query_raw = dot_rows(three_low, w_query)
    key_raw = dot_rows(three_low, w_key)
    value_raw = dot_rows(three_low, w_value)
    query_head_split, query_back = jax.vjp(
        partial(head_prep, places=query_angles), query_raw, query_gain.astype(jnp.float32)
    )
    key_head_split, key_reverse_rotation = jax.vjp(
        partial(head_prep, places=query_angles), key_raw, key_gain.astype(jnp.float32)
    )
    query_narrow = query_head_split.astype(narrow_dtype).reshape(
        token_rows, KEY_VALUE_HEADS, QUERY_HEADS // KEY_VALUE_HEADS, HEAD_SIZE
    )
    key_narrow = key_head_split.astype(narrow_dtype).reshape(
        token_rows, KEY_VALUE_HEADS * HEAD_SIZE
    )
    value_low = value_raw.astype(narrow_dtype)
    gathered = lax.all_gather(
        jnp.concatenate([key_narrow, value_low], axis=1), "ctx", axis=0, tiled=True
    )
    gathered_keys = gathered[:, : key_narrow.shape[1]]
    gathered_values = gathered[:, key_narrow.shape[1] :]
    normed_one_low, gathered = lax.optimization_barrier((normed_one_low, gathered))
    one_blocks = lax.all_gather(normed_one_low, "fsdp", axis=0)
    grouped_key_rows = gathered_keys.reshape(-1, KEY_VALUE_HEADS, HEAD_SIZE)
    grouped_value_rows = gathered_values.reshape(-1, KEY_VALUE_HEADS, HEAD_SIZE)
    scores = masked_scores(query_narrow, grouped_key_rows, query_places, key_places)
    peak = jnp.max(scores, axis=-1, keepdims=True)
    total = jnp.sum(jnp.exp(scores - peak), axis=-1, keepdims=True)
    probs_low = (jnp.exp(scores - peak) / total).astype(narrow_dtype)
    attended = jnp.einsum(
        "hgrl,lhd->rhgd", probs_low, grouped_value_rows, preferred_element_type=jnp.float32
    )
    attended_low = attended.reshape(token_rows, QUERY_HEADS * HEAD_SIZE).astype(narrow_dtype)
    third = second + dot_rows(attended_low, w_output)
    normed_four, norm_back_four = jax.vjp(rms_scale, third, ff_norm_two.astype(jnp.float32))
    grad_four, inputs_two, hidden_two, gate_low_two, up_low_two = ff_call(
        "both", 2, normed_four.astype(narrow_dtype), gate2, up2, down2, given
    )
    shards = lax.axis_size("fsdp")
    sources = ring_sources()
    outs_two = dot_plain(hidden_two.reshape(shards * token_rows, -1), down2).astype(narrow_dtype)
    outs_two = jnp.take(outs_two.reshape(shards, -1), sources, axis=0).reshape(-1, MODEL_WIDTH)
    final = third + lax.psum_scatter(
        outs_two, "fsdp", scatter_dimension=0, tiled=True
    ).astype(jnp.float32)
    grad_final = cotangent[0].astype(jnp.float32)
    two_grads = ff_weight_grads(inputs_two, given, hidden_two, gate_low_two, up_low_two)
    ff_two = [lax.psum(jnp.concatenate(two_grads, axis=0), "ctx")]
    grad_third_part, grad_ff_norm_two = norm_back_four(grad_four)
    grad_third = grad_final + grad_third_part
    output_low = grad_third.astype(narrow_dtype)
    attended_gradient = dot_plain(output_low, w_output)
    grad_w_output = (
        dot_cols(output_low, attended_low)
        .astype(narrow_dtype)
        .reshape(lax.axis_size("fsdp"), -1, MODEL_WIDTH)
    )
    attended_gradient_narrow = attended_gradient.astype(narrow_dtype).reshape(
        token_rows, KEY_VALUE_HEADS, QUERY_HEADS // KEY_VALUE_HEADS, HEAD_SIZE
    )
    scores = masked_scores(query_narrow, grouped_key_rows, query_places, key_places)
    probs = jnp.exp(scores - peak) / total
    probs_low = probs.astype(narrow_dtype)
    grad_probs = jnp.einsum(
        "rhgd,lhd->hgrl",
        attended_gradient_narrow,
        grouped_value_rows,
        preferred_element_type=jnp.float32,
    )
    weighted = jnp.sum(probs * grad_probs, axis=-1, keepdims=True)
    grad_scores = (probs * (grad_probs - weighted)).astype(narrow_dtype)
    scale = HEAD_SIZE ** (-0.5)
    grad_query = (
        jnp.einsum(
            "hgrl,lhd->rhgd", grad_scores, grouped_key_rows, preferred_element_type=jnp.float32
        )
        * scale
    )
    keys_gradient = (
        jnp.einsum("hgrl,rhgd->lhd", grad_scores, query_narrow, preferred_element_type=jnp.float32)
        * scale
    )
    values_gradient = jnp.einsum(
        "hgrl,rhgd->lhd", probs_low, attended_gradient_narrow, preferred_element_type=jnp.float32
    )
    both_grads = jnp.concatenate(
        [
            keys_gradient.reshape(-1, KEY_VALUE_HEADS * HEAD_SIZE),
            values_gradient.reshape(-1, KEY_VALUE_HEADS * HEAD_SIZE),
        ],
        axis=1,
    ).astype(jnp.bfloat16)
    both_grads = both_grads.reshape(ctx_count, token_rows, -1)
    own_grads = pick(both_grads, ctx_place, 0).astype(jnp.float32)
    for step in range(1, ctx_count):
        arrived = lax.ppermute(
            pick(both_grads, (ctx_place + step) % ctx_count, 0),
            "ctx",
            [(i, (i + step) % ctx_count) for i in range(ctx_count)],
        )
        own_grads = own_grads + arrived.astype(jnp.float32)
    local_keys = own_grads[:, : KEY_VALUE_HEADS * HEAD_SIZE]
    own_values = own_grads[:, KEY_VALUE_HEADS * HEAD_SIZE :]
    grad_query_raw, grad_query_gain = query_back(
        grad_query.reshape(token_rows, QUERY_HEADS, HEAD_SIZE)
    )
    raw_key_gradient, key_gain_gradient = key_reverse_rotation(
        local_keys.reshape(token_rows, KEY_VALUE_HEADS, HEAD_SIZE)
    )
    query_grad_low = grad_query_raw.astype(narrow_dtype)
    key_grad_low = raw_key_gradient.astype(narrow_dtype)
    value_grad_low = own_values.astype(narrow_dtype)
    grad_three = (
        dot_plain(query_grad_low, w_query)
        + dot_plain(key_grad_low, w_key)
        + dot_plain(value_grad_low, w_value)
    )
    grad_rows = [
        one.reshape(token_rows, shards, -1) for one in (query_grad_low, key_grad_low, value_grad_low)
    ]
    widths = [one.shape[2] for one in grad_rows]
    grad_rows = jnp.concatenate(grad_rows, axis=2).reshape(token_rows, -1)
    grad_w_qkv = (
        dot_cols(grad_rows, three_low).astype(narrow_dtype).reshape(shards, sum(widths), -1)
    )
    grad_second_part, grad_attn_norm = norm_back_three(grad_three)
    grad_second = grad_third + grad_second_part
    grad_two, grads_one, hidden_one, gate_low_one, up_low_one = ff_call(
        "backward", 3, grad_second.astype(narrow_dtype), gate1, up1, down1, inputs_one
    )
    one_grads = ff_weight_grads(inputs_one, grads_one, hidden_one, gate_low_one, up_low_one)
    one_packed, ff_two[0] = lax.optimization_barrier(
        (jnp.concatenate(one_grads, axis=0), ff_two[0])
    )
    ff_one = [lax.psum(one_packed, "ctx")]
    ff_one, ff_two = [
        [one[0][at : at + gate1.shape[0]].astype(jnp.float32) for at in range(0, 3 * gate1.shape[0], gate1.shape[0])]
        for one in (ff_one, ff_two)
    ]
    grad_first_part, grad_ff_norm_one = norm_back_two(grad_two)
    grad_first = grad_second + grad_first_part
    first_low = grad_first.astype(narrow_dtype)
    grad_gated = dot_plain(first_low, mix_out)
    grad_mix_out = (
        dot_cols(first_low, gated_low).astype(narrow_dtype).reshape(shards, -1, MODEL_WIDTH)
    )
    grad_c_part = grad_gated * conv_out
    grad_conv = grad_gated * c_part
    grad_front_ext = conv_input_grad(grad_conv[:block], kernel)
    grad_back_ext = conv_input_grad(grad_conv[block:], kernel)
    back_before = grad_back_ext[:margin]
    outgoing = jnp.concatenate(
        [grad_front_ext[:margin], jnp.where(is_last, 0.0, back_before)], axis=0
    )
    returned = extended_2(outgoing, (("ctx", 0),), margin)
    from_prev = returned[:margin]
    from_next = returned[returned.shape[0] - margin :]
    own_edge = jnp.where(is_last, back_before, 0.0)
    front_grad = grad_front_ext[margin:]
    back_grad = grad_back_ext[margin:]
    front_grad = jnp.concatenate(
        [front_grad[: block - margin], front_grad[block - margin :] + from_next + own_edge], axis=0
    )
    back_grad = jnp.concatenate(
        [back_grad[: block - margin], back_grad[block - margin :] + from_prev], axis=0
    )
    grad_mixed = jnp.concatenate([front_grad, back_grad], axis=0)
    grad_kernel = kernel_grad(front_ext, grad_conv[:block]) + kernel_grad(
        back_ext, grad_conv[block:]
    )
    grad_projected = jnp.concatenate(
        [grad_mixed * x_part, grad_c_part, grad_mixed * b_part], axis=-1
    ).astype(narrow_dtype)
    grad_w_qkv, grad_w_output, grad_mix_out, grad_mix_in = tail_call(
        5, [grad_w_qkv, grad_w_output, grad_mix_out], grad_projected, one_blocks
    )
    grad_w_query = grad_w_qkv[: widths[0]]
    grad_w_key = grad_w_qkv[widths[0] : widths[0] + widths[1]]
    grad_w_value = grad_w_qkv[widths[0] + widths[1] :]
    grad_one = dot_plain(grad_projected, mix_in)
    grad_start_part, grad_mix_norm = norm_back_one(grad_one)
    grad_start = grad_first + grad_start_part
    smalls = (
        grad_mix_norm,
        grad_kernel.reshape(-1),
        grad_ff_norm_one,
        grad_attn_norm,
        grad_query_gain,
        key_gain_gradient,
        grad_ff_norm_two,
    )
    small_sum = lax.psum(jnp.concatenate(smalls), ("fsdp", "ctx"))
    small_out = []
    at = 0
    shard = lax.axis_index("fsdp")
    for one in smalls:
        part = one.shape[0] // lax.axis_size("fsdp")
        small_out.append(lax.dynamic_slice_in_dim(small_sum, at + shard * part, part))
        at += one.shape[0]
    return (
        final.astype(narrow_dtype)[None],
        grad_start[None],
        small_out[0],
        grad_mix_in,
        small_out[1].reshape(-1, KW),
        grad_mix_out,
        small_out[2],
        ff_one[0],
        ff_one[1],
        ff_one[2],
        small_out[3],
        grad_w_query,
        grad_w_key,
        grad_w_value,
        small_out[4],
        small_out[5],
        grad_w_output,
        small_out[6],
        ff_two[0],
        ff_two[1],
        ff_two[2],
    )


def solution(mesh):
    in_specs = (
        P("fsdp", "ctx", None),
        P("fsdp", "ctx", None),
        P("fsdp"),
        P("fsdp", None),
        P("fsdp", None),
        P("fsdp", None),
        P("fsdp"),
        P("fsdp", None),
        P("fsdp", None),
        P("fsdp", None),
        P("fsdp"),
        P("fsdp", None),
        P("fsdp", None),
        P("fsdp", None),
        P("fsdp"),
        P("fsdp"),
        P("fsdp", None),
        P("fsdp"),
        P("fsdp", None),
        P("fsdp", None),
        P("fsdp", None),
    )
    out_specs = (
        P("fsdp", "ctx", None),
        P("fsdp", "ctx", None),
        P("fsdp"),
        P("fsdp", None),
        P("fsdp", None),
        P("fsdp", None),
        P("fsdp"),
        P("fsdp", None),
        P("fsdp", None),
        P("fsdp", None),
        P("fsdp"),
        P("fsdp", None),
        P("fsdp", None),
        P("fsdp", None),
        P("fsdp"),
        P("fsdp"),
        P("fsdp", None),
        P("fsdp"),
        P("fsdp", None),
        P("fsdp", None),
        P("fsdp", None),
    )
    return jax.shard_map(local, mesh=mesh, in_specs=in_specs, out_specs=out_specs, check_vma=False)
```

time: 3760 us -> 1400 us (0.37)
  waiting for transfers between devices: 3180 us -> 92.1 us
  Pallas kernels: 0 us -> 845 us
  matrix products: 384 us -> 176 us
  local copies, waits for them, and re-layouts: 22 us -> 99.7 us
    reduce_scatter x14 -> x1, waiting for transfers between devices: 1490 us -> 36 us  [local(): lax.psum_scatter(outs_two, 'fsdp', scatter_dimension=0, tiled=True)]
    all_gather x14 -> x4, waiting for transfers between devices: 1330 us -> 26.5 us  [the longest x1 26.5 us: local(): lax.all_gather(jnp.concatenate([key_narrow, value_low], axis=1), 'ctx', a...]
    pallas_call x0 -> x5, Pallas kernels: none -> 845 us  [the longest x3 399 us: ff_call(): pl.pallas_call(partial(ff_kernel, chips, mode), out_shape=outs, in_specs=...]
    psum x1 -> x2, waiting for transfers between devices: 344 us -> 0.01 us  [the longest x1 0.01 us: local(): ff_two = [lax.psum(jnp.concatenate(two_grads, axis=0), 'ctx')]]
    dot_general x12 -> x6, matrix products: 128 us -> 16 us  [dot_rows(): lax.dot_general(left, right, (((1,), (1,)), ((), ())), preferred_element_...]
    dot_general x12 -> x7, matrix products: 92.3 us -> 35.6 us  [dot_plain(): return jnp.dot(left, right, preferred_element_type=jnp.float32)]
    unnamed x2 -> x0, blocking collectives: 51.1 us -> none
    dot_general x12 -> x9, matrix products: 98.9 us -> 60.7 us  [dot_cols(): lax.dot_general(left, right, (((0,), (0,)), ((), ())), preferred_element_...]
  transfers between devices with their start and end apart: 34 -> 14, of which waited for: 28 -> 6; matrix products, arithmetic and copies ran while one was open for 9% -> 17% of each run, Pallas kernels for 0% -> 52%
where the time goes in v1:
time: 1400 us; the launch traced here: 1390 us
  Pallas kernels  845 us (60%)
  matrix products  176 us (13%)
  other arithmetic  101 us (7%)
  local copies, waits for them, and re-layouts  99.7 us (7%)
  waiting for transfers between devices  92.1 us (7%)
  blocking collectives  42.9 us (3%)
  between operations  16.2 us (1%)
  starting transfers between devices  15.1 us (1%)
    pallas_call x3, Pallas kernels, ff_call(): pl.pallas_call(partial(ff_kernel, chips, mode), out_shape=outs, in_specs=...  399 us
    pallas_call x1, Pallas kernels, tail_call(): pl.pallas_call(partial(tail_kernel, chips, count, pieces), out_shape=[jax...  319 us
    pallas_call x1, Pallas kernels, head_call(): pl.pallas_call(partial(head_kernel, chips, count), out_shape=outs, in_spe...  127 us
    dot_general x9, matrix products, dot_cols(): lax.dot_general(left, right, (((0,), (0,)), ((), ())), preferred_element_...  60.7 us
    psum x1, blocking collectives, local(): small_sum = lax.psum(jnp.concatenate(smalls), ('fsdp', 'ctx'))  42.9 us
    reduce_scatter x1, waiting for transfers between devices, local(): lax.psum_scatter(outs_two, 'fsdp', scatter_dimension=0, tiled=True)  36 us
    dot_general x7, matrix products, dot_plain(): return jnp.dot(left, right, preferred_element_type=jnp.float32)  35.6 us
    gather x6, local copies, waits for them, and re-layouts, local(): jnp.take(outs_two.reshape(shards, -1), sources, axis=0)  29.9 us
  transfers between devices with their start and end apart: 14, of which 6 were waited for; matrix products, arithmetic and copies ran while one was open for 17% of the time, Pallas kernels for 52%

profile of v1, /device:TPU:16, one launch (start us, length us, event | category | flops | bytes accessed | tf_op | source)
XLA Modules:
  0.0 1388.5 jit_solution(6174373532129100246)
XLA Ops:
  10.8 127.4 %shard_map.364 = (bf16[8,4,144,1536]{3,2,1,0:T(8,128)(2,1)}, bf16[8,4,48,1536]{3,2,1,0:T(8,128)(2,1)}, bf16[4,2,256,1536]{3,2,1,0:T(8,128)(2,1)}, bf16[8,16,128]{2,1,0:T(8,128)(2,1)}) custom-call(bf16[4,144,1536]{2,1,0:T(8,128)(2,1)} %bitcast.227, bf16[4,48,1536]{2,1,0:T(8,128)(2,1)} %bitcast.243, bf16[256,1536]{1,0:T(8,128)(2,1)} %bitcast.222, ...), custom_call_target="tpu_custom_call" | custom-call | bytes 37748736 | tf_op jit(solution)/shard_map/pallas_call | solution.py:469
  142.9 8.3 fusion.108
  152.8 4.3 collective-permute-done.1
  157.1 4.1 collective-permute-start
  168.8 116.0 %shard_map.365 = (f32[256,1536]{1,0:T(8,128)}, bf16[4,2,256,1536]{3,2,1,0:T(8,128)(2,1)}) custom-call(bf16[256,1536]{1,0:T(8,128)(2,1)} %multiply_convert_fusion.5.refs_0_, bf16[864,1536]{1,0:T(8,128)(2,1)} %refs_2_.5, bf16[864,1536]{1,0:T(8,128)(2,1)} %refs_3_.5, bf16[864,1536]{1,0:T(8,128)(2,1)} %refs_4_.3), custom_call_target="tpu_custom_call" | custom-call | flops 16307453952 | bytes 12582912 | tf_op jit(solution)/shard_map/pallas_call | solution.py:317
  286.8 2.6 multiply_reduce_fusion.20
  295.4 6.6 fusion.97
  306.0 26.5 %all-gather.9.cloned.1.call-done = bf16[1024,1024]{1,0:T(8,128)(2,1)} async-done(((bf16[256,1024]{1,0:T(8,128)(2,1)}), bf16[1024,1024]{1,0:T(8,128)(2,1)}) %all-gather.9.cloned.1.call-update) | async-done | bytes 2097168 | tf_op jit(solution)/shard_map/all_gather | solution.py:835
  332.5 3.0 fusion.101
  335.5 2.5 copy.85
  337.9 2.3 copy.84
  340.2 13.7 fusion.106
  353.9 10.9 fusion.29
  368.7 118.0 %shard_map.366 = (f32[256,1536]{1,0:T(8,128)}, bf16[4,2,256,1536]{3,2,1,0:T(8,128)(2,1)}, bf16[4,2,256,864]{3,2,1,0:T(8,128)(2,1)}, bf16[4,2,256,864]{3,2,1,0:T(8,128)(2,1)}, bf16[4,2,256,864]{3,2,1,0:T(8,128)(2,1)}) custom-call(bf16[256,1536]{1,0:T(8,128)(2,1)} %multiply_convert_fusion.3.refs_0_, bf16[4,2,256,1536]{3,2,1,0:T(8,128)(2,1)} %get-tuple-element.50.refs_1_, ...), custom_call_target="tpu_custom_call" | custom-call | flops 27179089920 | bytes 12582912 | tf_op jit(solution)/shard_map/pallas_call | solution.py:317
  486.7 11.1 convolution_convert_fusion.1
  497.7 8.3 reshape.628
  506.0 4.9 fusion.98
  510.9 5.6 gather_fusion
  516.5 5.6 gather_fusion.1
  522.1 2.7 gather_fusion.2
  524.9 2.7 gather_fusion.3
  527.6 16.9 %pad_maximum_fusion.2 = bf16[8,393216]{1,0:T(8,128)(2,1)} fusion(bf16[8,98304]{1,0:T(8,128)(2,1)} %gather_fusion.3, bf16[8,98304]{1,0:T(8,128)(2,1)} %gather_fusion.2, bf16[8,98304]{1,0:T(8,128)(2,1)} %gather_fusion.1, bf16[8,98304]{1,0:T(8,128)(2,1)S(1)} %copy-done.26), kind=kLoop, calls=%fused_computation.23 | loop fusion | flops 25165824 | bytes 12582912
  544.6 8.3 gather.7
  552.9 6.1 broadcast_select_fusion
  559.1 9.3 bitcast_convert_fusion
  568.4 8.1 bitcast_convert_fusion.1
  576.5 6.0 bitcast_convert_fusion.2
  582.6 3.9 pad_maximum_fusion.1
  589.5 36.0 %reduce-scatter.2.cloned.1.call-done = bf16[256,1536]{1,0:T(8,128)(2,1)} async-done(((bf16[2048,1536]{1,0:T(8,128)(2,1)}), bf16[256,1536]{1,0:T(8,128)(2,1)}) %reduce-scatter.2.cloned.1.call-update) | async-done | bytes 786448 | tf_op jit(solution)/shard_map/reduce_scatter | solution.py:861
  625.5 2.7 fusion.21
  629.4 3.8 convolution_convert_fusion.4
  633.5 17.8 %fusion.1 = (f32[8,3,256]{2,1,0:T(4,128)S(1)}, f32[8,1024,256,3]{2,1,3,0:T(8,128)}) fusion(f32[8,3,256,1024]{2,3,1,0:T(8,128)} %get-tuple-element.206, f32[8,3,256]{2,1,0:T(4,128)S(1)} %get-tuple-element.205, bf16[1024,8,64,1]{0,2,3,1:T(8,128)(2,1)S(1)} %bitcast.237, bf16[256,8,3,64]{0,3,2,1:T(8,128)(2,1)S(1)} %bitcast.239), kind=kOutput, calls=%fused_computation.7 | convolution fusion | flops 824174592 | bytes 52215808 | tf_op jit(solution)/shard_map/rhgd,lhd->hgrl/dot_general | solution.py:882
  651.3 12.0 fusion.36
  663.4 17.3 %fusion.3 = bf16[8,3,256,1024]{2,3,1,0:T(8,128)(2,1)S(1)} fusion(f32[8,1024,256,3]{2,1,3,0:T(8,128)} %get-tuple-element.210, f32[8,3,256]{2,1,0:T(4,128)S(1)} %get-tuple-element.209, f32[8,3,256,1024]{2,3,1,0:T(8,128)} %get-tuple-element.206, f32[8,3,256]{2,1,0:T(4,128)S(1)} %get-tuple-element.205), kind=kLoop, calls=%fused_computation.9 | loop fusion | flops 25165824 | bytes 62963712 | tf_op jit(solution)/shard_map/convert_element_type | solution.py:889
  680.7 3.4 convolution_multiply_fusion
  684.0 5.9 fusion.35
  689.9 1.7 multiply_add_fusion.3
  692.4 2.7 concatenate.70
  695.1 2.7 concatenate.69
  704.9 3.6 convolution_convert_fusion.3
  708.6 13.8 collective-permute-done.2
  722.4 10.3 collective-permute-done.3
  733.9 2.1 convolution_bitcast_fusion
  739.2 1.8 fusion.95
  741.0 164.9 %shard_map.367 = (f32[256,1536]{1,0:T(8,128)}, bf16[4,2,256,1536]{3,2,1,0:T(8,128)(2,1)}, bf16[4,2,256,864]{3,2,1,0:T(8,128)(2,1)}, bf16[4,2,256,864]{3,2,1,0:T(8,128)(2,1)}, bf16[4,2,256,864]{3,2,1,0:T(8,128)(2,1)}) custom-call(bf16[256,1536]{1,0:T(8,128)(2,1)} %get-tuple-element.133.refs_0_, bf16[4,2,256,1536]{3,2,1,0:T(8,128)(2,1)} %get-tuple-element.53.refs_1_, ...), custom_call_target="tpu_custom_call" | custom-call | flops 27179089920 | bytes 12582912 | tf_op jit(solution)/shard_map/pallas_call | solution.py:317
  906.0 9.1 bitcast_convert_fusion.4
  915.1 8.0 bitcast_convert_fusion.5
  923.2 6.3 bitcast_convert_fusion.3
  929.5 3.9 pad_maximum_fusion
  934.9 2.4 fusion.24
  937.3 5.3 multiply_convert_fusion.1
  944.8 4.9 convolution_convert_fusion.2
  950.8 3.2 collective-permute-start.6
  955.9 5.3 convolution_convert_fusion
  961.2 10.1 slice_convert_fusion.3
  976.9 3.0 multiply_convert_fusion.2
  982.6 4.3 copy.94
  987.0 11.0 fusion.20
  998.0 42.9 %psum.21 = f32[10880]{0:T(1024)S(1)} all-reduce(f32[10880]{0:T(1024)S(1)} %concatenate.74), channel_id=1, replica_groups=mesh['ctx'=4,'fsdp'=8] {'fsdp','ctx'}, use_global_device_ids=true, to_apply=%region_28.29 | all-reduce | flops 10880 | bytes 87040 | tf_op jit(solution)/shard_map/psum | solution.py:1010
  1043.2 319.1 %shard_map.368 = (bf16[11,4,16,1536]{3,2,1,0:T(8,128)(2,1)}, bf16[4,144,1536]{2,1,0:T(8,128)(2,1)}) custom-call(bf16[4,2,5,4,16,1536]{5,4,3,2,1,0:T(8,128)(2,1)} %bitcast.199, bf16[4,2,3,4,16,1536]{5,4,3,2,1,0:T(8,128)(2,1)} %bitcast.200, bf16[4,2,3,4,16,1536]{5,4,3,2,1,0:T(8,128)(2,1)} %bitcast.201, bf16[8,4,144,256]{3,2,1,0:T(8,128)(2,1)} %bitcast.202, ...), custom_call_target="tpu_custom_call" | custom-call | flops 3623878656 | bytes 34603008 | tf_op jit(solution)/shard_map/pallas_call | solution.py:682
  1362.3 2.0 fusion.100
  1364.3 3.5 fusion.99
  1367.7 2.4 bitcast_convert_fusion.7
  1371.7 9.8 slice_convert_fusion
  (370 shorter events, 67.6 us)
Async XLA Ops:
  7.2 131.0 %all-gather.7.cloned.1.call-start = ((), (), s32[]{:S(2)}) async-start(), calls=%async_computation.1 | async-start | bytes 3538944 | tf_op jit(solution)/shard_map/all_gather | solution.py:771
  9.6 277.2 %all-gather.11.cloned.1.call-start = ((), (), s32[]{:S(2)}) async-start(), calls=%async_computation.6 | async-start | bytes 15728640 | tf_op jit(solution)/shard_map/all_gather | solution.py:776
  138.3 194.2 %all-gather.9.cloned.1.call-start = ((), (), s32[]{:S(2)}) async-start(), calls=%async_computation.2 | async-start | bytes 2621440 | tf_op jit(solution)/shard_map/all_gather | solution.py:835
  139.8 27.7 %copy-start.57 = (f32[1536]{0:T(1024)}, f32[1536]{0:T(1024)S(1)}, u32[]{:S(2)}) copy-start(f32[1536]{0:T(1024)S(1)} %reshape.640) | copy-start | bytes 18436
  139.9 146.7 %copy-start.59 = (f32[1536]{0:T(1024)}, f32[1536]{0:T(1024)S(1)}, u32[]{:S(2)}) copy-start(f32[1536]{0:T(1024)S(1)} %reshape.641) | copy-start | bytes 18436
  140.1 149.4 %copy-start.87 = (f32[64]{0:T(128)}, f32[64]{0:T(128)S(1)}, u32[]{:S(2)}) copy-start(f32[64]{0:T(128)S(1)} %reshape.642) | copy-start | bytes 772
  140.3 10.9 copy-start.81
  141.5 21.0 %copy-start.65 = (f32[1536]{0:T(1024)}, f32[1536]{0:T(1024)S(1)}, u32[]{:S(2)}) copy-start(f32[1536]{0:T(1024)S(1)} %get-tuple-element.130) | copy-start | bytes 18436
  141.5 21.0 %copy-start.67 = (f32[1536]{0:T(1024)}, f32[1536]{0:T(1024)S(1)}, u32[]{:S(2)}) copy-start(f32[1536]{0:T(1024)S(1)} %get-tuple-element.131) | copy-start | bytes 18436
  141.5 21.0 %copy-start.69 = (f32[1536]{0:T(1024)}, f32[1536]{0:T(1024)S(1)}, u32[]{:S(2)}) copy-start(f32[1536]{0:T(1024)S(1)} %get-tuple-element.132) | copy-start | bytes 18436
  141.5 9.7 copy-start.85
  141.7 164.0 %copy-start.49 = (f32[256,32]{0,1:T(8,128)}, f32[256,32]{0,1:T(8,128)S(1)}, u32[]{:S(2)}) copy-start(f32[256,32]{0,1:T(8,128)S(1)} %get-tuple-element.197) | copy-start | bytes 98308
  141.7 164.0 %copy-start.51 = (f32[256,32]{0,1:T(8,128)}, f32[256,32]{0,1:T(8,128)S(1)}, u32[]{:S(2)}) copy-start(f32[256,32]{0,1:T(8,128)S(1)} %get-tuple-element.198) | copy-start | bytes 98308
  151.2 12.1 copy-start.10
  151.5 5.6 collective-permute-start.1
  157.1 5.3 collective-permute-start
  167.4 117.4 %copy-start.91 = (f32[256]{0:T(256)}, f32[256]{0:T(256)S(1)}, u32[]{:S(2)}) copy-start(f32[256]{0:T(256)S(1)} %get-tuple-element.199) | copy-start | bytes 3076
  167.5 117.4 %copy-start.4 = (f32[256,1536]{1,0:T(8,128)}, f32[256,1536]{1,0:T(8,128)S(1)}, u32[]{:S(2)}) copy-start(f32[256,1536]{1,0:T(8,128)S(1)} %get-tuple-element.200) | copy-start | bytes 4718596
  167.5 117.4 %copy-start.77 = (f32[256]{0:T(256)}, f32[256]{0:T(256)S(1)}, u32[]{:S(2)}) copy-start(f32[256]{0:T(256)S(1)} %fusion.72) | copy-start | bytes 3076
  286.6 78.3 %copy-start.6 = (f32[256,1536]{1,0:T(8,128)}, f32[256,1536]{1,0:T(8,128)S(1)}, u32[]{:S(2)}) copy-start(f32[256,1536]{1,0:T(8,128)S(1)} %get-tuple-element.136) | copy-start | bytes 4718596
  286.8 15.1 %copy-start.40 = (bf16[256,1536]{1,0:T(8,128)(2,1)}, bf16[256,1536]{1,0:T(8,128)(2,1)S(1)}, u32[]{:S(2)}) copy-start(bf16[256,1536]{1,0:T(8,128)(2,1)S(1)} %multiply_convert_fusion.4) | copy-start | bytes 2359300
  294.8 330.7 %reduce-scatter.2.cloned.1.call-start = ((), (), s32[]{:S(2)}) async-start(), calls=%async_computation.3 | async-start | bytes 7077888 | tf_op jit(solution)/shard_map/reduce_scatter | solution.py:861
  294.9 9.3 copy-start.89
  306.0 34.2 %copy-start.45 = (bf16[256,24,32]{0,2,1:T(8,128)(2,1)}, bf16[256,24,32]{0,2,1:T(8,128)(2,1)S(1)}, u32[]{:S(2)}) copy-start(bf16[256,24,32]{0,2,1:T(8,128)(2,1)S(1)} %get-tuple-element.163) | copy-start | bytes 1179652
  306.0 34.2 %copy-start.47 = (bf16[256,24,32]{0,2,1:T(8,128)(2,1)}, bf16[256,24,32]{0,2,1:T(8,128)(2,1)S(1)}, u32[]{:S(2)}) copy-start(bf16[256,24,32]{0,2,1:T(8,128)(2,1)S(1)} %get-tuple-element.164) | copy-start | bytes 1179652
  340.2 24.7 %slice-start.4 = ((s8[4718592]{0:T(1024)(128)(4,1)}), s8[524288]{0:T(1024)(128)(4,1)S(1)}, s32[]{:S(2)}) async-start(s8[4718592]{0:T(1024)(128)(4,1)} %bitcast.219), calls=%async_computation.12 | async-start | bytes 1048576
  353.9 11.0 slice-start.5
  368.7 118.0 %copy-start.100 = (bf16[864,1536]{1,0:T(8,128)(2,1)S(1)}, bf16[864,1536]{1,0:T(8,128)(2,1)}, u32[]{:S(2)}) copy-start(bf16[864,1536]{1,0:T(8,128)(2,1)} %refs_4_.2) | copy-start | bytes 7962628
  559.0 374.4 %all-reduce.10.cloned.1.call-start = ((), (), s32[]{:S(2)}) async-start(), calls=%async_computation.4 | async-start | bytes 15925248 | tf_op jit(solution)/shard_map/psum | solution.py:866
  559.0 9.4 copy-start.102
  559.1 17.5 %slice-start.6 = ((s8[6291456]{0:T(1024)(128)(4,1)}), s8[4194304]{0:T(1024)(128)(4,1)S(1)}, s32[]{:S(2)}) async-start(s8[6291456]{0:T(1024)(128)(4,1)} %bitcast.253), calls=%async_computation.14 | async-start | bytes 8388608
  568.4 8.1 slice-start.7
  568.4 8.1 copy-start.101
  586.5 456.6 %all-gather.13.cloned.1.call-start = ((), (), s32[]{:S(2)}) async-start(), calls=%async_computation.7 | async-start | bytes 7077888 | tf_op jit(solution)/shard_map/all_gather | solution.py:841
  589.4 782.3 %all-reduce.12.cloned.1.call-start = ((), (), s32[]{:S(2)}) async-start(), calls=%async_computation.5 | async-start | bytes 15925248 | tf_op jit(solution)/shard_map/psum | solution.py:953
  663.4 17.3 %copy-start.28 = (bf16[1024,512]{0,1:T(8,128)(2,1)S(1)}, bf16[1024,512]{0,1:T(8,128)(2,1)}, u32[]{:S(2)}) copy-start(bf16[1024,512]{0,1:T(8,128)(2,1)} %copy.85) | copy-start | bytes 3145732
  684.0 5.9 copy-start.50
  684.0 5.9 copy-start.52
  699.8 5.0 copy-start.9
  699.8 5.0 copy-start.54
  699.9 22.5 %collective-permute-start.2 = (bf16[256,1024]{0,1:T(8,128)(2,1)S(1)}, bf16[256,1024]{0,1:T(8,128)(2,1)S(1)}, u32[]{:S(2)}, u32[]{:S(2)}) collective-permute-start(bf16[256,1024]{0,1:T(8,128)(2,1)S(1)} %get-tuple-element.156), channel_id=1, source_target_pairs={{0,8},{8,16},{16,24},{24,0},{1,9},{9,17},{17,25},{25,1},{2,10},{10... | collective-permute-start | bytes 1572872 | tf_op jit(solution)/shard_map/ppermute | solution.py:914
  701.3 31.4 %collective-permute-start.3 = (bf16[256,1024]{0,1:T(8,128)(2,1)S(1)}, bf16[256,1024]{0,1:T(8,128)(2,1)S(1)}, u32[]{:S(2)}, u32[]{:S(2)}) collective-permute-start(bf16[256,1024]{0,1:T(8,128)(2,1)S(1)} %get-tuple-element.158), channel_id=1, source_target_pairs={{0,16},{8,24},{16,0},{24,8},{1,17},{9,25},{17,1},{25,9},{2,18},{10... | collective-permute-start | bytes 1572872 | tf_op jit(solution)/shard_map/ppermute | solution.py:914
  703.0 29.7 %collective-permute-start.4 = (bf16[256,1024]{0,1:T(8,128)(2,1)S(1)}, bf16[256,1024]{0,1:T(8,128)(2,1)S(1)}, u32[]{:S(2)}, u32[]{:S(2)}) collective-permute-start(bf16[256,1024]{0,1:T(8,128)(2,1)S(1)} %get-tuple-element.157), channel_id=1, source_target_pairs={{0,24},{8,0},{16,8},{24,16},{1,25},{9,1},{17,9},{25,17},{2,26},{10... | collective-permute-start | bytes 1572872 | tf_op jit(solution)/shard_map/ppermute | solution.py:914
  704.9 31.1 %copy-start.38 = (bf16[256,24,64]{0,2,1:T(8,128)(2,1)}, bf16[256,24,64]{0,2,1:T(8,128)(2,1)S(1)}, u32[]{:S(2)}) copy-start(bf16[256,24,64]{0,2,1:T(8,128)(2,1)S(1)} %fusion.22) | copy-start | bytes 2359300
  704.9 31.1 %slice-start.2 = ((s8[4718592]{0:T(1024)(128)(4,1)}), s8[4194304]{0:T(1024)(128)(4,1)S(1)}, s32[]{:S(2)}) async-start(s8[4718592]{0:T(1024)(128)(4,1)} %bitcast.215), calls=%async_computation.10 | async-start | bytes 8388608
  708.5 24.6 %copy-start.30 = (f32[256,8,64]{0,2,1:T(8,128)S(1)}, f32[256,8,64]{0,2,1:T(8,128)}, u32[]{:S(2)}) copy-start(f32[256,8,64]{0,2,1:T(8,128)} %copy-done.29) | copy-start | bytes 1572868
  708.5 24.6 %copy-start.62 = (f32[256,8]{0,1:T(8,128)S(1)}, f32[256,8]{0,1:T(8,128)}, u32[]{:S(2)}) copy-start(f32[256,8]{0,1:T(8,128)} %copy-done.61) | copy-start | bytes 24580
  708.5 24.6 %copy-start.88 = (f32[64]{0:T(128)S(1)}, f32[64]{0:T(128)}, u32[]{:S(2)}) copy-start(f32[64]{0:T(128)} %copy-done.87) | copy-start | bytes 772
  708.5 27.4 %slice-start.3 = ((s8[4718592]{0:T(1024)(128)(4,1)}), s8[524288]{0:T(1024)(128)(4,1)S(1)}, s32[]{:S(2)}) async-start(s8[4718592]{0:T(1024)(128)(4,1)} %bitcast.215), calls=%async_computation.11 | async-start | bytes 1048576
  732.9 4.5 copy-start.27
  905.9 9.2 copy-start.104
  905.9 17.2 %slice-start.8 = ((s8[6291456]{0:T(1024)(128)(4,1)}), s8[4194304]{0:T(1024)(128)(4,1)S(1)}, s32[]{:S(2)}) async-start(s8[6291456]{0:T(1024)(128)(4,1)} %bitcast.255), calls=%async_computation.16 | async-start | bytes 8388608
  915.1 8.1 slice-start.9
  915.1 8.1 copy-start.103
  937.3 5.3 copy-start.1
  937.3 5.3 copy-start.3
  944.7 9.2 copy-start.33
  944.7 11.1 copy-start.39
  949.6 6.3 copy-start.41
  950.8 25.3 %collective-permute-start.6 = (f32[2,1536]{1,0:T(2,128)S(1)}, f32[2,1536]{1,0:T(2,128)S(1)}, u32[]{:S(2)}, u32[]{:S(2)}) collective-permute-start(f32[2,1536]{1,0:T(2,128)S(1)} %broadcast_select_fusion.1), channel_id=1, source_target_pairs={{0,8},{8,16},{16,24},{1,9},{9,17},{17,25},{2,10},{10,18},{18,26},{... | collective-permute-start | bytes 36872 | tf_op jit(solution)/shard_map/ppermute | solution.py:29
  954.0 22.1 %collective-permute-start.5 = (f32[2,1536]{1,0:T(2,128)S(1)}, f32[2,1536]{1,0:T(2,128)S(1)}, u32[]{:S(2)}, u32[]{:S(2)}) collective-permute-start(f32[2,1536]{1,0:T(2,128)S(1)} %slice.334), channel_id=1, source_target_pairs={{8,0},{16,8},{24,16},{9,1},{17,9},{25,17},{10,2},{18,10},{26,18},{... | collective-permute-start | bytes 36872 | tf_op jit(solution)/shard_map/ppermute | solution.py:30
  982.6 4.4 copy-start.86
  986.9 11.0 copy-start.73
  987.0 56.2 %copy-start.82 = (f32[256]{0:T(256)S(1)}, f32[256]{0:T(256)}, u32[]{:S(2)}) copy-start(f32[256]{0:T(256)} %copy-done.81) | copy-start | bytes 3076
  (65 other events, 137.3 us)
Sparse Core Ops, SparseCore 0:
  10.2 63.7 all-gather.6
  138.4 123.6 all-gather.10
  294.9 37.5 all-gather.8
  559.1 66.3 reduce-scatter.1
  628.9 182.5 all-reduce.9
  813.1 89.4 all-gather.12
  944.9 186.0 all-reduce.11

commit v2 on v1

v2 whole, which is shorter than its diff:
```python
from functools import partial

import jax
import jax.numpy as jnp
from jax import lax
from jax.experimental import pallas as pl
from jax.experimental.pallas import tpu as pltpu
from jax.sharding import PartitionSpec as P

MODEL_WIDTH = 1536
QUERY_HEADS = 24
KEY_VALUE_HEADS = 8
HEAD_SIZE = 64
KW = 3


EPS = 1e-05
THETA = 1000000.0
NEG = -1e30


def extended_2(array, sides, width):
    for axis, dim in sides:
        size, length = (lax.axis_size(axis), array.shape[dim])
        up = [(i, (i + 1) % size) for i in range(size - 1)]
        down = [(j, i) for i, j in up]
        last = lax.slice_in_dim(array, length - width, length, axis=dim)
        first = lax.slice_in_dim(array, 0, width, axis=dim)
        before = lax.ppermute(last, axis, up)
        after = lax.ppermute(first, axis, down)
        array = jnp.concatenate([before, array, after], axis=dim)
    return array


def rms_scale(value, gain):
    return value * lax.rsqrt(jnp.mean(value * value, axis=-1, keepdims=True) + EPS) * gain


def rotate(value, angles):
    half_dim = value.shape[1] // 2
    cosine = jnp.cos(angles)
    sine = jnp.sin(angles)
    first = value[:, :half_dim]
    second = value[:, half_dim:]
    return jnp.concatenate(
        [first * cosine - second * sine, second * cosine + first * sine], axis=1
    )


def head_prep(raw, gain, angles):
    heads = raw.reshape(-1, gain.shape[0], raw.shape[1])
    mean = jnp.mean(heads * heads, axis=1, keepdims=True)
    return rotate(heads * lax.rsqrt(mean + EPS) * gain[:, None], angles)


def dot_rows(left, right):
    return lax.dot_general(
        left, right, (((1,), (1,)), ((), ())), preferred_element_type=jnp.float32
    )


def dot_cols(left, right):
    return lax.dot_general(
        left, right, (((0,), (0,)), ((), ())), preferred_element_type=jnp.float32
    )


def dot_plain(left, right):
    return jnp.dot(left, right, preferred_element_type=jnp.float32)


def swish_product(gate_val, up_val):
    return jax.nn.silu(gate_val) * up_val


def dealt_places(index, block, ctx_count):
    device = index // (2 * block)
    within = index % (2 * block)
    which = jnp.where(within < block, device, 2 * ctx_count - 1 - device)
    return which * block + within % block


def conv_apply(extended, kernel):
    sequence_length = extended.shape[0] - KW + 1
    total = extended[0:sequence_length] * kernel[:, 0]
    for place in range(1, KW):
        total = total + extended[place : place + sequence_length] * kernel[:, place]
    return total


def conv_input_grad(grad_conv, kernel):
    sequence_length = grad_conv.shape[0] + KW - 1
    padded = jnp.pad(grad_conv, ((KW - 1, KW - 1), (0, 0)))
    total = padded[KW - 1 : KW - 1 + sequence_length] * kernel[:, 0]
    for place in range(1, KW):
        total = total + padded[KW - 1 - place : KW - 1 - place + sequence_length] * kernel[:, place]
    return total


def kernel_grad(extended, grad_conv):
    sequence_length = grad_conv.shape[0]
    columns = [
        jnp.sum(grad_conv * extended[place : place + sequence_length], axis=0)
        for place in range(KW)
    ]
    return jnp.stack(columns, axis=1)


def pick(value, index, axis):
    return lax.dynamic_index_in_dim(value, index, axis, keepdims=False)


MESH = pl.DeviceIdType.MESH


def dims_nt(left, right):
    return lax.dot_general(
        left, right, (((1,), (1,)), ((), ())), preferred_element_type=jnp.float32
    )


def dims_tn(left, right):
    return lax.dot_general(
        left, right, (((0,), (0,)), ((), ())), preferred_element_type=jnp.float32
    )


def ff_call(mode, ident, x, gate, up_w, down, given=None):
    size = lax.axis_size("fsdp")
    chips = size // 2
    rows, width = x.shape
    units = gate.shape[0]
    forward = mode == "forward"
    bf16 = jnp.bfloat16
    blocks = jax.ShapeDtypeStruct((size, rows, width), bf16)
    vmem = pl.BlockSpec(memory_space=pltpu.VMEM)
    anywhere = pl.BlockSpec(memory_space=pl.ANY)
    outs = [jax.ShapeDtypeStruct((rows, width), jnp.float32), blocks]
    out_specs = [vmem, vmem]
    args = [x, gate, up_w, down]
    specs = [vmem] * 4
    dma = pltpu.SemaphoreType.DMA
    scratch = [pltpu.VMEM((rows, width), jnp.float32)]
    scratch += [pltpu.VMEM((chips, rows, width), bf16)] * 3
    scratch += [pltpu.VMEM((chips + 1, rows, width), bf16)]
    scratch += [dma((chips,))] * 8 + [dma((chips, 4))] * 4
    if not forward:
        for share in (1, 2) if mode == "both" else (3,):
            outs.append(jax.ShapeDtypeStruct((share * units, width), bf16))
            out_specs.append(anywhere)
        if mode == "both":
            outs.append(blocks)
            out_specs.append(anywhere)
        args.insert(1, given)
        specs.insert(1, anywhere)
        scratch += [pltpu.VMEM(blocks.shape, bf16)]
        scratch += [pltpu.VMEM((units, size * rows), bf16)] * 3
        scratch += [pltpu.VMEM((2, units, 256), bf16), dma((size,)), dma((2,))]
        if mode == "both":
            scratch += [pltpu.VMEM((2, rows, width), bf16), dma((2,))]
    products = 3 if forward else 9
    return pl.pallas_call(
        partial(ff_kernel, chips, mode),
        out_shape=outs,
        in_specs=specs,
        out_specs=out_specs,
        scratch_shapes=scratch,
        compiler_params=pltpu.CompilerParams(
            collective_id=ident, has_side_effects=True, vmem_limit_bytes=61 * 2**20
        ),
        cost_estimate=pl.CostEstimate(
            flops=2 * products * size * rows * units * width,
            bytes_accessed=4 * size * rows * width,
            transcendentals=size * rows * units,
        ),
    )(*args)


def places():
    count = lax.axis_size("fsdp") // 2
    place = lax.axis_index("fsdp")
    chip = place // 2
    core = place % 2
    after = lax.rem(chip + 1, count) * 2 + core
    before = lax.rem(chip + count - 1, count) * 2 + core
    return place, chip, core, after, before, chip * 2 + 1 - core


def greet(targets):
    barrier = pltpu.get_barrier_semaphore()
    for target in targets:
        pl.semaphore_signal(barrier, inc=1, device_id=target, device_id_type=MESH)
    pl.semaphore_wait(barrier, len(targets))


def push(src, dst, send, recv, target):
    return pltpu.make_async_remote_copy(
        src_ref=src, dst_ref=dst, send_sem=send, recv_sem=recv,
        device_id=target, device_id_type=MESH,
    )


def ff_kernel(chips, mode, *refs):
    forward = mode == "forward"
    if forward:
        x_ref, gate, up_w, down, out, xall = refs[:6]
        rest = refs[6:]
    elif mode == "both":
        x_ref, y_hbm, gate, up_w, down, out, xall, gate_grads, weight_grads, result = refs[:10]
        rest = refs[10:]
    else:
        x_ref, y_hbm, gate, up_w, down, out, xall, weight_grads = refs[:8]
        rest = refs[8:]
    part, term, other_send, other_recv, in_sum = rest[:5]
    (up_s, up_r, down_s, down_r, core_s, core_r, ps_s, ps_r, ups_s, ups_r, downs_s, downs_r) = rest[5:17]
    if not forward:
        yall, hid, dgate, dup, stage, ysem, stage_sem = rest[17:24]
        if mode == "both":
            out_stage, out_sem = rest[24:]
    rows, width = x_ref.shape
    units = gate.shape[0]
    place, chip, core, _, _, peer = places()
    low_side = chip > 0
    high_side = chip < chips - 1
    below = {"fsdp": lax.rem(place + 2 * chips - 2, 2 * chips)}
    above = {"fsdp": lax.rem(place + 2, 2 * chips)}
    pieces = 4
    piece = rows // pieces
    greet([below, above, {"fsdp": peer}])

    def up_rows(d):
        block = xall.at[2 * d + core]
        return push(block, block, up_s.at[d], up_r.at[d], above)

    def down_rows(d):
        block = xall.at[2 * d + core]
        return push(block, block, down_s.at[d], down_r.at[d], below)

    def core_copy(d):
        block = xall.at[2 * d + core]
        return push(block, block, core_s.at[d], core_r.at[d], {"fsdp": peer})

    def core_in(d):
        block = xall.at[2 * d + 1 - core]
        return push(block, block, core_s.at[d], core_r.at[d], {"fsdp": peer})

    def part_copy(d):
        return push(other_send.at[d], other_recv.at[d], ps_s.at[d], ps_r.at[d], {"fsdp": peer})

    def span(b):
        return pl.ds(pl.multiple_of(b * piece, piece), piece)

    def up_sum(d, b):
        return push(
            term.at[d, span(b)], in_sum.at[d + 1, span(b)], ups_s.at[d, b], ups_r.at[d, b], above
        )

    def down_sum(d, b):
        return push(
            term.at[d, span(b)], in_sum.at[d, span(b)], downs_s.at[d, b], downs_r.at[d, b], below
        )

    def y_copy(s):
        return pltpu.make_async_copy(y_hbm.at[s], yall.at[s], ysem.at[s])

    def across(s):
        return pl.ds(pl.multiple_of(s * rows, rows), rows)

    def block(s):
        x = xall[s]
        if forward:
            gate_val = dims_nt(gate[...], x)
            up_val = dims_nt(up_w[...], x)
            hidden = (gate_val / (1.0 + jnp.exp(-gate_val)) * up_val).astype(jnp.bfloat16)
            return dims_tn(hidden, down[...])
        y_copy(s).wait()
        y = yall[s]
        a, g = (x, y) if mode == "both" else (y, x)
        gate_val = dims_nt(gate[...], a)
        up_val = dims_nt(up_w[...], a)
        grad_hidden = dims_nt(down[...], g)
        sig = 1.0 / (1.0 + jnp.exp(-gate_val))
        act = gate_val * sig
        grad_up = (grad_hidden * act).astype(jnp.bfloat16)
        grad_gate = (
            grad_hidden * up_val * (sig * (1.0 + gate_val * (1.0 - sig)))
        ).astype(jnp.bfloat16)
        hid[:, across(s)] = (act * up_val).astype(jnp.bfloat16)
        dup[:, across(s)] = grad_up
        dgate[:, across(s)] = grad_gate
        return dims_tn(grad_gate, gate[...]) + dims_tn(grad_up, up_w[...])

    xall[place] = x_ref[...]
    if not forward:
        @pl.loop(0, 2 * chips)
        def _(s):
            y_copy(s).start()

    @pl.when(high_side)
    def _():
        up_rows(chip).start()

    @pl.when(low_side)
    def _():
        down_rows(chip).start()

    inside = low_side & high_side
    reach = jnp.minimum(chip, chips - 1 - chip)

    def turn(r):
        far = jnp.where(r <= 2 * reach, (r + 1) // 2, r - reach)
        downward = jnp.where(r <= 2 * reach, r % 2 == 1, chip > chips - 1 - chip)
        return jnp.where(downward, chip - far, chip + far)

    def receive(r):
        d = turn(r)

        @pl.when(d < chip)
        def _():
            up_rows(d).wait_recv()

            @pl.when(high_side)
            def _():
                up_rows(d).start()

        @pl.when(d > chip)
        def _():
            down_rows(d).wait_recv()

            @pl.when(low_side)
            def _():
                down_rows(d).start()

        core_copy(d).start()

    core_copy(chip).start()

    @pl.loop(0, chips)
    def _(r):
        @pl.when((r == 1) | ((r > 1) & ~inside))
        def _():
            receive(r)

        @pl.when((r >= 1) & (r < chips - 1) & inside)
        def _():
            receive(r + 1)

        d = turn(r)

        @pl.loop(0, 2)
        def _(o):
            @pl.when(o == 1)
            def _():
                core_in(d).wait_recv()

            value = block(2 * d + (core + o) % 2)

            @pl.when(o == 0)
            def _():
                part[...] = value

            @pl.when(o == 1)
            def _():
                other_send[d] = value.astype(jnp.bfloat16)
                part_copy(d).start()

        part_copy(d).wait_recv()

        @pl.when(d == chip)
        def _():
            out[...] = part[...] + other_recv[d].astype(jnp.float32)

        @pl.when(d != chip)
        def _():
            term[d] = (part[...] + other_recv[d].astype(jnp.float32)).astype(jnp.bfloat16)

        @pl.when((d > chip) & (chip == 0))
        def _():
            for b in range(pieces):
                up_sum(d, b).start()

        @pl.when((d < chip) & (chip == chips - 1))
        def _():
            for b in range(pieces):
                down_sum(d, b).start()

    lag = 2
    items = (chips - 2) * pieces
    relays = items + lag * max(chips - 3, 0)

    def relay(n):
        rise = n - lag * (chip - 1)
        fall = n - lag * (chips - 2 - chip)
        high = jnp.maximum(rise, 0) // pieces + 2
        low = chips - 3 - jnp.maximum(fall, 0) // pieces

        @pl.when((rise >= 0) & (rise < items) & (high > chip) & low_side)
        def _():
            b = rise % pieces
            up_sum(high, b).wait_recv()
            term[high, span(b)] = (
                term[high, span(b)].astype(jnp.float32)
                + in_sum[high + 1, span(b)].astype(jnp.float32)
            ).astype(jnp.bfloat16)
            up_sum(high, b).start()

        @pl.when((fall >= 0) & (fall < items) & (low < chip) & high_side)
        def _():
            b = fall % pieces
            down_sum(low, b).wait_recv()
            term[low, span(b)] = (
                term[low, span(b)].astype(jnp.float32) + in_sum[low, span(b)].astype(jnp.float32)
            ).astype(jnp.bfloat16)
            down_sum(low, b).start()

    if forward:
        @pl.loop(0, relays)
        def _(n):
            relay(n)
    else:
        step = stage.shape[2]
        steps = width // step
        gate_right, hid_right = (xall, yall) if mode == "both" else (yall, xall)
        pairs = ((dgate, gate_right), (dup, gate_right), (hid, hid_right))

        def stage_copy(n, j):
            there, at = weight_grads, n
            if mode == "both":
                there, at = (gate_grads, 0) if n == 0 else (weight_grads, n - 1)
            there = there.at[
                pl.ds(at * units, units), pl.ds(pl.multiple_of(j * step, step), step)
            ]
            return pltpu.make_async_copy(stage.at[j % 2], there, stage_sem.at[j % 2])

        @pl.loop(0, max(2 * relays, 3 * steps))
        def _(m):
            @pl.when((m % 2 == 0) & (m < 2 * relays))
            def _():
                relay(m // 2)

            j = m % steps
            for n, (left, right) in enumerate(pairs):
                @pl.when(m // steps == n)
                def _():
                    @pl.when(m >= 2)
                    def _():
                        stage_copy(n, j).wait()

                    at = pl.ds(pl.multiple_of(j * step, step), step)
                    sums = jnp.dot(
                        left[...],
                        right[:, :, at].reshape(2 * chips * rows, step),
                        preferred_element_type=jnp.float32,
                    )
                    stage[j % 2] = sums.astype(jnp.bfloat16)
                    stage_copy(n, j).start()

        for j in range(2):
            stage_copy(2, j).wait()
        if mode == "both":
            def result_copy(s):
                return pltpu.make_async_copy(out_stage.at[s % 2], result.at[s], out_sem.at[s % 2])

            @pl.loop(0, 2 * chips)
            def _(s):
                @pl.when(s >= 2)
                def _():
                    result_copy(s).wait()

                out_stage[s % 2] = dims_tn(hid[:, across(s)], down[...]).astype(jnp.bfloat16)
                result_copy(s).start()

            for s in range(2):
                result_copy(s).wait()

    @pl.when(low_side)
    def _():
        for b in range(pieces):
            up_sum(chip, b).wait_recv()
        out[...] += in_sum[chip + 1].astype(jnp.float32)

    @pl.when(high_side)
    def _():
        for b in range(pieces):
            down_sum(chip, b).wait_recv()
        out[...] += in_sum[chip].astype(jnp.float32)

    @pl.loop(0, chips)
    def _(d):
        core_copy(d).wait_send()
        part_copy(d).wait_send()

        @pl.when((d <= chip) & high_side)
        def _():
            up_rows(d).wait_send()

        @pl.when((d >= chip) & low_side)
        def _():
            down_rows(d).wait_send()

        @pl.when(d > chip)
        def _():
            for b in range(pieces):
                up_sum(d, b).wait_send()

        @pl.when(d < chip)
        def _():
            for b in range(pieces):
                down_sum(d, b).wait_send()


def head_kernel(chips, count, *refs):
    shards = refs[:2]
    block, vector = refs[2:4]
    wholes = refs[4:6]
    blocks, vectors = refs[6:8]
    local, near_s, near_r, hop_s, hop_r, side_s, side_r, pass_s, pass_r = refs[8:]
    place, chip, core, after, before, peer = places()
    here = lax.axis_index("ctx")
    others = [{"ctx": lax.rem(here + t, count)} for t in range(1, count)]
    greet([{"fsdp": before}, {"fsdp": peer}] + others)
    started = []

    def go(copy):
        copy.start()
        started.append(copy)

    def shard_of(k):
        return lax.rem(chip + chips - k, chips) * 2 + core

    def hop(k, n):
        owner = shard_of(k)
        if n < 2:
            src = shards[n].at[here] if k == 0 else wholes[n].at[owner, here]
            dst = wholes[n].at[owner, here]
        elif n == 2:
            src = block if k == 0 else blocks.at[owner]
            dst = blocks.at[owner]
        else:
            src = vector if k == 0 else vectors.at[owner]
            dst = vectors.at[owner]
        return push(src, dst, hop_s.at[n, k], hop_r.at[n, k], {"fsdp": after})

    def side(k, t, n):
        piece = wholes[n].at[shard_of(k), here]
        return push(piece, piece, side_s.at[n, k, t], side_r.at[n, k, t], others[t - 1])

    def side_in(k, t, n):
        piece = wholes[n].at[shard_of(k), lax.rem(here + count - t, count)]
        return piece, push(piece, piece, side_s.at[n, k, t], side_r.at[n, k, t], others[t - 1])

    def across(k, t, n):
        if n == 2:
            src = dst = blocks.at[shard_of(k)]
        elif n == 3:
            src = dst = vectors.at[shard_of(k)]
        else:
            src = dst = wholes[n].at[shard_of(k), lax.rem(here + count - t, count)]
        return push(src, dst, pass_s.at[n, k, t], pass_r.at[n, k, t], {"fsdp": peer})

    def across_in(k, t, n):
        owner = lax.rem(chip + chips - k, chips) * 2 + 1 - core
        if n == 2:
            dst = blocks.at[owner]
        elif n == 3:
            dst = vectors.at[owner]
        else:
            dst = wholes[n].at[owner, lax.rem(here + count - t, count)]
        return push(dst, dst, pass_s.at[n, k, t], pass_r.at[n, k, t], {"fsdp": peer})

    homes = [one.at[place] for one in (*wholes, blocks, vectors)]
    came = [one.at[peer] for one in (*wholes, blocks, vectors)]
    sources = [shards[0], shards[1], block, vector]
    order = (3, 0, 1, 2)
    for n in order:
        go(hop(0, n))
    keeps = [pltpu.make_async_copy(sources[n], homes[n], local.at[n]) for n in order]
    for one in keeps:
        one.start()
    for n in order:
        go(push(sources[n], homes[n], near_s.at[n], near_r.at[n], {"fsdp": peer}))
    for k in range(1, chips):
        for n in order:
            hop(k - 1, n).wait_recv()
            if k < chips - 1:
                go(hop(k, n))
            if n < 2:
                for t in range(1, count):
                    go(side(k, t, n))
            go(across(k, 0, n))
        if k > 1:
            for n in range(2):
                for t in range(1, count):
                    side_in(k - 1, t, n)[1].wait_recv()
                    go(across(k - 1, t, n))
    for n in range(2):
        for t in range(1, count):
            side_in(chips - 1, t, n)[1].wait_recv()
            go(across(chips - 1, t, n))
    for n in order:
        push(came[n], came[n], near_s.at[n], near_r.at[n], {"fsdp": peer}).wait_recv()
        for k in range(1, chips):
            for t in range(count if n < 2 else 1):
                across_in(k, t, n).wait_recv()
    for one in keeps:
        one.wait()
    for one in started:
        one.wait_send()


def head_call(ident, shard_a, shard_b, block, vector):
    size = lax.axis_size("fsdp")
    count = lax.axis_size("ctx")
    chips = size // 2
    width = shard_a.shape[1]
    shards = [one.reshape(count, -1, width) for one in (shard_a, shard_b)]
    outs = [jax.ShapeDtypeStruct((size,) + one.shape, jnp.bfloat16) for one in shards]
    outs.append(jax.ShapeDtypeStruct((size,) + block.shape, jnp.bfloat16))
    outs.append(jax.ShapeDtypeStruct((size,) + vector.shape, jnp.bfloat16))
    anywhere = pl.BlockSpec(memory_space=pl.ANY)
    dma = pltpu.SemaphoreType.DMA
    whole_a, whole_b, blocks, vectors = pl.pallas_call(
        partial(head_kernel, chips, count),
        out_shape=outs,
        in_specs=[anywhere] * 4,
        out_specs=[anywhere] * 4,
        scratch_shapes=[
            dma((4,)), dma((4,)), dma((4,)),
            dma((4, chips)), dma((4, chips)),
            dma((2, chips, count)), dma((2, chips, count)),
            dma((4, chips, count)), dma((4, chips, count)),
        ],
        compiler_params=pltpu.CompilerParams(collective_id=ident, has_side_effects=True),
        cost_estimate=pl.CostEstimate(
            flops=0, bytes_accessed=2 * size * (shard_a.size + shard_b.size) * 2, transcendentals=0
        ),
    )(*shards, block, vector)
    return whole_a.reshape(-1, width), whole_b.reshape(-1, width), blocks, vectors


def tail_kernel(chips, count, pieces, *refs):
    number = len(pieces)
    grads = refs[:number]
    factor, inputs, small = refs[number : number + 3]
    total, total_in, small_total = refs[number + 3 : number + 6]
    rest = refs[number + 6 :]
    own, near, line, in_sum, fin, rc, fs, held, fin_in, rc_in, fs_in, small_in, small_sums = rest[:13]
    (own_m, near_s, near_r, up_s, up_r, down_s, down_r, sc_s, sc_r, ag_s, ag_r, fac_m, fac_s, fac_r,
     sci_s, sci_r, agi_s, agi_r, sm_s, sm_r, smc_s, smc_r) = rest[13:]
    place, chip, core, after, before, peer = places()
    here = lax.axis_index("ctx")
    size = 2 * chips
    chunks = sum(pieces)
    ctx_others = [{"ctx": lax.rem(here + t, count)} for t in range(1, count)]
    shard_others = [{"fsdp": lax.rem(place + t, size)} for t in range(1, size)]
    greet(ctx_others + shard_others)

    def factor_copy(t):
        there = lax.rem(place + t, size)
        return push(factor.at[there], held.at[place], fac_s.at[t], fac_r.at[t], {"fsdp": there})

    def small_copy(t):
        there = lax.rem(place + t, size)
        return push(small.at[there], small_in.at[t], sm_s.at[t], sm_r.at[t], {"fsdp": there})

    def small_share(t):
        return push(
            small_sums.at[0], small_sums.at[t], smc_s.at[t], smc_r.at[t], ctx_others[t - 1]
        )

    for t in range(1, size):
        small_copy(t).start()
        factor_copy(t).start()
    keep = pltpu.make_async_copy(factor.at[place], held.at[place], fac_m)
    keep.start()

    bases = [sum(pieces[:n]) for n in range(number)]

    def near_copy(n, j):
        at = bases[n] + j
        return push(
            grads[n].at[:, 1 - core, j], near.at[at], near_s.at[at], near_r.at[at], {"fsdp": peer}
        )

    def own_copy(n, j):
        at = bases[n] + j
        return pltpu.make_async_copy(grads[n].at[:, core, j], own.at[at], own_m.at[at])

    for n in range(number):
        @pl.loop(0, pieces[n])
        def _(j):
            near_copy(n, j).start()
            own_copy(n, j).start()

    def up_copy(d, j):
        there = {"fsdp": lax.rem(place + 2, size)}
        return push(own.at[j, d], in_sum.at[d + 1, j], up_s.at[d, j], up_r.at[d, j], there)

    def down_copy(d, j):
        there = {"fsdp": lax.rem(place + size - 2, size)}
        return push(own.at[j, d], in_sum.at[d, j], down_s.at[d, j], down_r.at[d, j], there)

    def near_in(j):
        return push(near.at[j], near.at[j], near_s.at[j], near_r.at[j], {"fsdp": peer})

    def own_in(j):
        return pltpu.make_async_copy(own.at[j], own.at[j], own_m.at[j])

    def term(j, owner):
        return own[j, owner].astype(jnp.float32) + near[j, owner].astype(jnp.float32)

    def scatter_copy(j, t):
        there = lax.rem(here + t, count)
        return push(fin.at[j, there], rc.at[j, t], sc_s.at[j, t], sc_r.at[j, t], {"ctx": there})

    def gather_copy(j, t):
        return push(
            fs.at[j], total.at[j, here], ag_s.at[j, t], ag_r.at[j, t], ctx_others[t - 1]
        )

    def gather_in(j, t):
        there = total.at[j, lax.rem(here + count - t, count)]
        return push(there, there, ag_s.at[j, t], ag_r.at[j, t], ctx_others[t - 1])

    def scatter_in_copy(t):
        there = lax.rem(here + t, count)
        return push(fin_in.at[there], rc_in.at[t], sci_s.at[t], sci_r.at[t], {"ctx": there})

    def gather_in_copy(t):
        return push(fs_in, total_in.at[here], agi_s.at[t], agi_r.at[t], ctx_others[t - 1])

    def gather_in_wait(t):
        there = total_in.at[lax.rem(here + count - t, count)]
        return push(there, there, agi_s.at[t], agi_r.at[t], ctx_others[t - 1])

    def products():
        for t in range(1, size):
            src = held.at[lax.rem(place + size - t, size)]
            push(src, src, fac_s.at[t], fac_r.at[t], {"fsdp": peer}).wait_recv()
        keep.wait()

        tall = held.shape[2]
        joined = 1 if tall % 16 else count
        step = 256

        @pl.loop(0, count // joined)
        def _(c):
            @pl.loop(0, inputs.shape[2] // step)
            def _(n):
                at = pl.ds(pl.multiple_of(n * step, step), step)
                sums = 0.0
                for s in range(size):
                    left = held[s].reshape(count * tall, -1) if joined > 1 else held[s, c]
                    sums = sums + jnp.dot(
                        left, inputs[s, :, at], preferred_element_type=jnp.float32
                    )
                sums = sums.astype(jnp.bfloat16)
                if joined > 1:
                    fin_in[:, :, at] = sums.reshape(count, tall, step)
                else:
                    fin_in[c, :, at] = sums

        for t in range(1, count):
            scatter_in_copy(t).start()
        sums = small[place]
        for t in range(1, size):
            small_copy(t).wait_recv()
            sums = sums + small_in[t]
        small_sums[0] = sums
        for t in range(1, count):
            small_share(t).start()

    def products_sum():
        sums = fin_in[here].astype(jnp.float32)
        for t in range(1, count):
            scatter_in_copy(t).wait_recv()
            sums = sums + rc_in[t].astype(jnp.float32)
        fs_in[...] = sums.astype(jnp.bfloat16)
        for t in range(1, count):
            gather_in_copy(t).start()
        total_in[here] = fs_in[...]
        sums = small_sums[0]
        for t in range(1, count):
            small_share(t).wait_recv()
            sums = sums + small_sums[t]
        small_total[...] = sums

    def relay(d, j, arrives, arrived, slot, leave):
        line[...] = term(j, d)

        @pl.when(arrives)
        def _():
            arrived(d, j).wait_recv()
            line[...] += in_sum[slot, j].astype(jnp.float32)

        own[j, d] = line[...].astype(jnp.bfloat16)
        leave(d, j).start()

    lag = 2
    items = (chips - 1) * chunks

    @pl.loop(0, items + lag * (chips - 1))
    def _(i):
        @pl.when(i < chunks)
        def _():
            own_in(i).wait()
            near_in(i).wait_recv()

        rise = i - lag * chip
        upward = chips - 1 - jnp.maximum(rise, 0) // chunks

        @pl.when((rise >= 0) & (rise < items) & (upward > chip))
        def _():
            relay(upward, rise % chunks, chip > 0, up_copy, upward + 1, up_copy)

        fall = i - lag * (chips - 1 - chip)
        downward = jnp.maximum(fall, 0) // chunks

        @pl.when((fall >= 0) & (fall < items) & (downward < chip))
        def _():
            relay(downward, fall % chunks, chip < chips - 1, down_copy, downward, down_copy)

        @pl.when(i == items // 2)
        def _():
            products()

    def reduce_chunk(j):
        sums = fin[j, here].astype(jnp.float32)
        for t in range(1, count):
            scatter_copy(j, t).wait_recv()
            sums = sums + rc[j, t].astype(jnp.float32)
        fs[j] = sums.astype(jnp.bfloat16)
        for t in range(1, count):
            gather_copy(j, t).start()
        total[j, here] = fs[j]

    @pl.loop(0, chunks)
    def _(j):
        line[...] = term(j, chip)

        @pl.when(chip > 0)
        def _():
            up_copy(chip, j).wait_recv()
            line[...] += in_sum[chip + 1, j].astype(jnp.float32)

        @pl.when(chip < chips - 1)
        def _():
            down_copy(chip, j).wait_recv()
            line[...] += in_sum[chip, j].astype(jnp.float32)

        fin[j] = line[...].astype(jnp.bfloat16)
        for t in range(1, count):
            scatter_copy(j, t).start()

        @pl.when(j >= 2)
        def _():
            reduce_chunk(j - 2)

        @pl.when(j == chunks // 2)
        def _():
            products_sum()

    @pl.loop(chunks - 2, chunks)
    def _(j):
        reduce_chunk(j)

    @pl.loop(0, chunks)
    def _(j):
        for t in range(1, count):
            gather_in(j, t).wait_recv()
            gather_copy(j, t).wait_send()
            scatter_copy(j, t).wait_send()

        near_in(j).wait_send()

        @pl.loop(0, chips)
        def _(d):
            @pl.when(d > chip)
            def _():
                up_copy(d, j).wait_send()

            @pl.when(d < chip)
            def _():
                down_copy(d, j).wait_send()

    for t in range(1, count):
        gather_in_wait(t).wait_recv()
        gather_in_copy(t).wait_send()
        scatter_in_copy(t).wait_send()
        small_share(t).wait_send()
    for t in range(1, size):
        small_copy(t).wait_send()
        factor_copy(t).wait_send()


def tail_call(ident, grads, factor, inputs, small):
    size = lax.axis_size("fsdp")
    count = lax.axis_size("ctx")
    chips = size // 2
    width = inputs.shape[2]
    rows = inputs.shape[1]
    unit = min(one.shape[1] for one in grads) // 3
    pieces = [one.shape[1] // unit for one in grads]
    chunks = sum(pieces)
    part = unit // count
    views = [
        one.reshape(chips, 2, n, count, part, width) for one, n in zip(grads, pieces)
    ]
    factor = factor.T.reshape(size, count, -1, rows)
    mine = factor.shape[2]
    bf16 = jnp.bfloat16
    anywhere = pl.BlockSpec(memory_space=pl.ANY)
    vmem = pl.BlockSpec(memory_space=pltpu.VMEM)
    dma = pltpu.SemaphoreType.DMA
    total, total_in, small_total = pl.pallas_call(
        partial(tail_kernel, chips, count, pieces),
        out_shape=[
            jax.ShapeDtypeStruct((chunks, count, part, width), bf16),
            jax.ShapeDtypeStruct((count, mine, width), bf16),
            jax.ShapeDtypeStruct(small.shape[1:], jnp.float32),
        ],
        in_specs=[anywhere] * (len(views) + 1) + [vmem] * 2,
        out_specs=[vmem] * 3,
        scratch_shapes=[
            pltpu.VMEM((chunks, chips, count, part, width), bf16),
            pltpu.VMEM((chunks, chips, count, part, width), bf16),
            pltpu.VMEM((count, part, width), jnp.float32),
            pltpu.VMEM((chips + 1, chunks, count, part, width), bf16),
            pltpu.VMEM((chunks, count, part, width), bf16),
            pltpu.VMEM((chunks, count, part, width), bf16),
            pltpu.VMEM((chunks, part, width), bf16),
            pltpu.VMEM((size, count, mine, rows), bf16),
            pltpu.VMEM((count, mine, width), bf16),
            pltpu.VMEM((count, mine, width), bf16),
            pltpu.VMEM((mine, width), bf16),
            pltpu.VMEM(small.shape, jnp.float32),
            pltpu.VMEM((count,) + small.shape[1:], jnp.float32),
            dma((chunks,)), dma((chunks,)), dma((chunks,)),
            dma((chips, chunks)), dma((chips, chunks)), dma((chips, chunks)), dma((chips, chunks)),
            dma((chunks, count)), dma((chunks, count)), dma((chunks, count)), dma((chunks, count)),
            dma, dma((size,)), dma((size,)),
            dma((count,)), dma((count,)), dma((count,)), dma((count,)),
            dma((size,)), dma((size,)), dma((count,)), dma((count,)),
        ],
        compiler_params=pltpu.CompilerParams(
            collective_id=ident, has_side_effects=True, vmem_limit_bytes=61 * 2**20
        ),
        cost_estimate=pl.CostEstimate(
            flops=2 * size * rows * width * count * mine,
            bytes_accessed=4 * size * chunks * unit * width,
            transcendentals=0,
        ),
    )(*views, factor, inputs, small)
    total = total.reshape(-1, width).astype(jnp.float32)
    outs = []
    at = 0
    for one in grads:
        outs.append(total[at : at + one.shape[1]])
        at += one.shape[1]
    return outs + [total_in.reshape(-1, width).astype(jnp.float32), small_total.reshape(-1)]


def attend_kernel(count, groups, q, kv, att, sums, kv_all, acc, send, recv):
    here = lax.axis_index("ctx")
    others = [{"ctx": lax.rem(here + t, count)} for t in range(1, count)]
    greet(others)
    key_heads = kv.shape[0] // 2
    rows = kv.shape[2]
    block = rows // 2
    scale = HEAD_SIZE ** (-0.5)

    def out_copy(t):
        return push(kv, kv_all.at[here], send.at[t], recv.at[t], others[t - 1])

    def in_copy(t):
        there = kv_all.at[lax.rem(here + count - t, count)]
        return push(there, there, send.at[t], recv.at[t], others[t - 1])

    for t in range(1, count):
        out_copy(t).start()
    kv_all[here] = kv[...]

    def weights(keys, queries, masked):
        value = jnp.exp(dims_tn(keys, queries) * scale)
        if masked:
            allowed = lax.broadcasted_iota(jnp.int32, value.shape, 1) >= lax.broadcasted_iota(
                jnp.int32, value.shape, 0
            )
            value = jnp.where(allowed, value, 0.0)
        return value

    def apply(values, part):
        return jnp.dot(values, part.astype(jnp.bfloat16), preferred_element_type=jnp.float32)

    @pl.loop(0, key_heads)
    def _(h):
        keys = kv[h]
        values = kv[key_heads + h]
        for g in range(groups):
            head = h * groups + g
            queries = q[head]
            part = weights(keys[:, :block], queries, True)
            acc[head] = apply(values[:, :block], part)
            sums[head] = jnp.sum(part, axis=0, keepdims=True)
            part = weights(keys[:, block:], queries[:, block:], True)
            acc[head, :, block:] += apply(values[:, block:], part)
            sums[head, :, block:] += jnp.sum(part, axis=0, keepdims=True)

    for t in range(1, count):
        there = lax.rem(here + count - t, count)
        in_copy(t).wait_recv()

        @pl.when(there < here)
        def _():
            @pl.loop(0, key_heads)
            def _(h):
                keys = kv_all[there, h]
                values = kv_all[there, key_heads + h]
                for g in range(groups):
                    head = h * groups + g
                    part = weights(keys[:, :block], q[head], False)
                    acc[head] += apply(values[:, :block], part)
                    sums[head] += jnp.sum(part, axis=0, keepdims=True)

        @pl.when(there > here)
        def _():
            @pl.loop(0, key_heads)
            def _(h):
                keys = kv_all[there, h]
                values = kv_all[there, key_heads + h]
                for g in range(groups):
                    head = h * groups + g
                    part = weights(keys, q[head][:, block:], False)
                    acc[head, :, block:] += apply(values, part)
                    sums[head, :, block:] += jnp.sum(part, axis=0, keepdims=True)

    @pl.loop(0, key_heads * groups)
    def _(head):
        att[head] = (acc[head] / sums[head]).astype(jnp.bfloat16)

    for t in range(1, count):
        out_copy(t).wait_send()


def attend_call(ident, q, kv):
    count = lax.axis_size("ctx")
    heads, size, rows = q.shape
    groups = heads // (kv.shape[0] // 2)
    vmem = pl.BlockSpec(memory_space=pltpu.VMEM)
    dma = pltpu.SemaphoreType.DMA
    return pl.pallas_call(
        partial(attend_kernel, count, groups),
        out_shape=[
            jax.ShapeDtypeStruct(q.shape, jnp.bfloat16),
            jax.ShapeDtypeStruct((heads, 1, rows), jnp.float32),
            jax.ShapeDtypeStruct((count,) + kv.shape, jnp.bfloat16),
        ],
        in_specs=[vmem] * 2,
        out_specs=[vmem] * 3,
        scratch_shapes=[pltpu.VMEM(q.shape, jnp.float32), dma((count,)), dma((count,))],
        compiler_params=pltpu.CompilerParams(
            collective_id=ident, has_side_effects=True, vmem_limit_bytes=40 * 2**20
        ),
        cost_estimate=pl.CostEstimate(
            flops=4 * heads * size * rows * rows * count,
            bytes_accessed=4 * (q.size + kv.size * count),
            transcendentals=heads * rows * rows * count,
        ),
    )(q, kv)


def attend_back_kernel(
    chips, count, groups, q, kv_all, grad, att, sums, outs, grad_q, grad_kv, result,
    delta, share, send_buf, recv_buf, own, near, out_sum, in_sum,
    send, recv, own_m, near_s, near_r, ring_s, ring_r
):
    place, chip, core, after, before, peer = places()
    here = lax.axis_index("ctx")
    others = [{"ctx": lax.rem(here + t, count)} for t in range(1, count)]
    greet([{"fsdp": before}, {"fsdp": peer}] + others)

    def near_copy(n):
        return push(
            outs.at[2 * n + 1 - core], near.at[n], near_s.at[n], near_r.at[n], {"fsdp": peer}
        )

    def own_copy(n):
        return pltpu.make_async_copy(outs.at[2 * n + core], own.at[n], own_m.at[n])

    def ring_copy(k):
        return push(out_sum.at[k], in_sum.at[k], ring_s.at[k], ring_r.at[k], {"fsdp": after})

    def term(k):
        owner = lax.rem(chip + chips - k, chips)
        own_copy(owner).wait()
        near_copy(owner).wait_recv()
        return own[owner].astype(jnp.float32) + near[owner].astype(jnp.float32)

    def hop(k):
        value = term(k)
        if k > 1:
            ring_copy(k - 2).wait_recv()
            value = value + in_sum[k - 2].astype(jnp.float32)
        out_sum[k - 1] = value.astype(jnp.bfloat16)
        ring_copy(k - 1).start()

    for n in range(chips):
        near_copy(n).start()
        own_copy(n).start()
    key_heads = kv_all.shape[1] // 2
    rows = q.shape[2]
    block = rows // 2
    scale = HEAD_SIZE ** (-0.5)
    every = slice(0, rows)
    front = slice(0, block)
    back = slice(block, rows)

    def copy(t):
        return push(send_buf.at[t], recv_buf.at[t], send.at[t], recv.at[t], others[t - 1])

    @pl.loop(0, key_heads * groups)
    def _(head):
        delta[head] = jnp.sum(
            grad[head].astype(jnp.float32) * att[head].astype(jnp.float32), axis=0, keepdims=True
        )
        share[head] = 1.0 / sums[head]
        grad_q[head] = jnp.zeros(grad_q.shape[1:], jnp.float32)

    def terms(keys, values, head, span, masked):
        queries = q[head][:, span]
        low = grad[head][:, span]
        probs = jnp.exp(dims_tn(keys, queries) * scale) * share[head][:, span]
        if masked:
            allowed = lax.broadcasted_iota(jnp.int32, probs.shape, 1) >= lax.broadcasted_iota(
                jnp.int32, probs.shape, 0
            )
            probs = jnp.where(allowed, probs, 0.0)
        grad_scores = (probs * (dims_tn(values, low) - delta[head][:, span])).astype(jnp.bfloat16)
        grad_q[head, :, span] += (
            jnp.dot(keys, grad_scores, preferred_element_type=jnp.float32) * scale
        )
        return (
            dims_nt(queries, grad_scores) * scale,
            dims_nt(low, probs.astype(jnp.bfloat16)),
        )

    def over_groups(keys, values, h, span, masked):
        grad_keys, grad_values = terms(keys, values, h * groups, span, masked)
        for g in range(1, groups):
            more_keys, more_values = terms(keys, values, h * groups + g, span, masked)
            grad_keys, grad_values = grad_keys + more_keys, grad_values + more_values
        return grad_keys, grad_values

    for t in range(1, max(count, chips)):
        if t >= count:
            hop(t)
            continue
        there = lax.rem(here + t, count)

        @pl.when(there < here)
        def _():
            @pl.loop(0, key_heads)
            def _(h):
                keys = kv_all[there, h][:, front]
                values = kv_all[there, key_heads + h][:, front]
                grad_keys, grad_values = over_groups(keys, values, h, every, False)
                zeros = jnp.zeros((keys.shape[0], rows - block), jnp.bfloat16)
                send_buf[t, h, :, front] = grad_keys.astype(jnp.bfloat16)
                send_buf[t, key_heads + h, :, front] = grad_values.astype(jnp.bfloat16)
                send_buf[t, h, :, back] = zeros
                send_buf[t, key_heads + h, :, back] = zeros

        @pl.when(there > here)
        def _():
            @pl.loop(0, key_heads)
            def _(h):
                keys = kv_all[there, h]
                values = kv_all[there, key_heads + h]
                grad_keys, grad_values = over_groups(keys, values, h, back, False)
                send_buf[t, h] = grad_keys.astype(jnp.bfloat16)
                send_buf[t, key_heads + h] = grad_values.astype(jnp.bfloat16)

        copy(t).start()
        if t < chips:
            hop(t)

    @pl.loop(0, key_heads)
    def _(h):
        keys = kv_all[here, h]
        values = kv_all[here, key_heads + h]
        grad_keys, grad_values = over_groups(keys[:, front], values[:, front], h, every, True)
        grad_kv[h, :, front] = grad_keys
        grad_kv[key_heads + h, :, front] = grad_values
        grad_keys, grad_values = over_groups(keys[:, back], values[:, back], h, back, True)
        grad_kv[h, :, back] = grad_keys
        grad_kv[key_heads + h, :, back] = grad_values

    for t in range(1, count):
        copy(t).wait_recv()

        @pl.loop(0, 2 * key_heads)
        def _(h):
            grad_kv[h] += recv_buf[t, h].astype(jnp.float32)

    value = term(0)
    ring_copy(chips - 2).wait_recv()
    result[...] = value + in_sum[chips - 2].astype(jnp.float32)
    for t in range(1, count):
        copy(t).wait_send()
    for n in range(chips):
        near_copy(n).wait_send()
    for k in range(chips - 1):
        ring_copy(k).wait_send()


def attend_back_call(ident, q, kv_all, grad, att, sums, outs):
    count = lax.axis_size("ctx")
    heads, size, rows = q.shape
    kv_shape = kv_all.shape[1:]
    chips = outs.shape[0] // 2
    block = outs.shape[1:]
    groups = heads // (kv_shape[0] // 2)
    vmem = pl.BlockSpec(memory_space=pltpu.VMEM)
    dma = pltpu.SemaphoreType.DMA
    return pl.pallas_call(
        partial(attend_back_kernel, chips, count, groups),
        out_shape=[
            jax.ShapeDtypeStruct(q.shape, jnp.float32),
            jax.ShapeDtypeStruct(kv_shape, jnp.float32),
            jax.ShapeDtypeStruct(block, jnp.float32),
        ],
        in_specs=[vmem] * 5 + [pl.BlockSpec(memory_space=pl.ANY)],
        out_specs=[vmem] * 3,
        scratch_shapes=[
            pltpu.VMEM(sums.shape, jnp.float32),
            pltpu.VMEM(sums.shape, jnp.float32),
            pltpu.VMEM(kv_all.shape, jnp.bfloat16),
            pltpu.VMEM(kv_all.shape, jnp.bfloat16),
            pltpu.VMEM((chips,) + block, jnp.bfloat16),
            pltpu.VMEM((chips,) + block, jnp.bfloat16),
            pltpu.VMEM((chips - 1,) + block, jnp.bfloat16),
            pltpu.VMEM((chips - 1,) + block, jnp.bfloat16),
            dma((count,)),
            dma((count,)),
            dma((chips,)),
            dma((chips,)),
            dma((chips,)),
            dma((chips,)),
            dma((chips,)),
        ],
        compiler_params=pltpu.CompilerParams(
            collective_id=ident, has_side_effects=True, vmem_limit_bytes=40 * 2**20
        ),
        cost_estimate=pl.CostEstimate(
            flops=10 * heads * size * rows * rows * count,
            bytes_accessed=4 * (3 * q.size + kv_all.size),
            transcendentals=heads * rows * rows * count,
        ),
    )(q, kv_all, grad, att, sums, outs)


def local(
    hidden_in,
    cotangent,
    norm_mix,
    in_proj,
    conv_kernel,
    out_proj,
    norm_ff1,
    gate1,
    up1,
    down1,
    norm_attn,
    q_proj,
    key_projection,
    value_projection,
    q_norm,
    k_norm,
    o_proj,
    norm_ff2,
    gate2,
    up2,
    down2,
):
    narrow_dtype = jnp.bfloat16
    start = hidden_in[0].astype(jnp.float32)
    token_rows = start.shape[0]
    block = token_rows // 2
    margin = KW - 1
    ctx_count = lax.axis_size("ctx")
    ctx_place = lax.axis_index("ctx")
    is_last = ctx_place == ctx_count - 1
    query_places = dealt_places(
        ctx_place * token_rows + jnp.arange(token_rows, dtype=jnp.int32), block, ctx_count
    )
    freqs = THETA ** (-jnp.arange(HEAD_SIZE // 2, dtype=jnp.float32) * 2.0 / HEAD_SIZE)
    angles = freqs[:, None] * query_places.astype(jnp.float32)[None, :]
    vectors = (
        norm_mix, norm_ff1, norm_attn, norm_ff2, q_norm, k_norm, conv_kernel.reshape(-1)
    )
    lengths = [one.shape[0] for one in vectors]
    vector = jnp.concatenate(vectors)
    vector = jnp.pad(vector, (0, 2048 - sum(lengths))).reshape(16, 128)
    attn_shard = jnp.concatenate([q_proj, key_projection, value_projection, o_proj], axis=0)
    attn_rows = attn_shard.shape[0]
    attn_slice = pick(attn_shard.reshape(ctx_count, -1, MODEL_WIDTH), ctx_place, 0)
    attn_slices = lax.all_gather(attn_slice, "fsdp", axis=0)
    mix_in, mix_out, given, gathered_vectors = head_call(
        4, in_proj, out_proj, cotangent[0], vector
    )
    attn_slices, mix_in = lax.optimization_barrier((attn_slices, mix_in))
    attn_wholes = lax.all_gather(attn_slices, "ctx", axis=1)
    attn_wholes = attn_wholes.reshape(-1, attn_rows, MODEL_WIDTH)
    gathered_vectors = gathered_vectors.reshape(-1, 2048)
    wholes = []
    at = 0
    for one in lengths:
        wholes.append(gathered_vectors[:, at : at + one].reshape(-1))
        at += one
    mix_norm, ff_norm_one, attn_norm, ff_norm_two, query_gain, key_gain, mix_kernel = wholes
    mix_kernel = mix_kernel.reshape(-1, KW)
    kernel = mix_kernel.astype(jnp.float32)
    normed_one, norm_back_one = jax.vjp(rms_scale, start, mix_norm.astype(jnp.float32))
    normed_one_low = normed_one.astype(narrow_dtype)
    projected = dot_rows(normed_one_low, mix_in)
    b_part = projected[:, :MODEL_WIDTH]
    c_part = projected[:, MODEL_WIDTH : 2 * MODEL_WIDTH]
    x_part = projected[:, 2 * MODEL_WIDTH :]
    mixed_low = (b_part * x_part).astype(narrow_dtype)
    front_tail = mixed_low[block - margin : block]
    back_tail = mixed_low[token_rows - margin :]
    edges = extended_2(jnp.concatenate([back_tail, front_tail], axis=0), (("ctx", 0),), margin)
    before_front = edges[:margin]
    before_back = jnp.where(is_last, front_tail, edges[edges.shape[0] - margin :])
    front_ext = jnp.concatenate([before_front, mixed_low[:block]], axis=0).astype(jnp.float32)
    back_ext = jnp.concatenate([before_back, mixed_low[block:]], axis=0).astype(jnp.float32)
    conv_out = jnp.concatenate(
        [conv_apply(front_ext, kernel), conv_apply(back_ext, kernel)], axis=0
    )
    gated_low = (c_part * conv_out).astype(narrow_dtype)
    first = start + dot_rows(gated_low, mix_out)
    normed_two, norm_back_two = jax.vjp(rms_scale, first, ff_norm_one.astype(jnp.float32))
    ff_out_one, inputs_one = ff_call(
        "forward", 1, normed_two.astype(narrow_dtype), gate1, up1, down1
    )
    one_low, ff_out_one = lax.optimization_barrier((normed_one_low, ff_out_one))
    one_blocks = lax.all_gather(one_low, "fsdp", axis=0)
    second = first + ff_out_one
    attn_parts = []
    at = 0
    for one in (q_proj, key_projection, value_projection, o_proj):
        attn_parts.append(attn_wholes[:, at : at + one.shape[0]].reshape(-1, MODEL_WIDTH))
        at += one.shape[0]
    w_query, w_key, w_value, w_output = attn_parts
    normed_three, norm_back_three = jax.vjp(rms_scale, second, attn_norm.astype(jnp.float32))
    three_low = normed_three.astype(narrow_dtype)
    query_raw = dot_rows(w_query, three_low)
    key_raw = dot_rows(w_key, three_low)
    value_raw = dot_rows(w_value, three_low)
    query_heads, query_back = jax.vjp(
        partial(head_prep, angles=angles), query_raw, query_gain.astype(jnp.float32)
    )
    key_heads, key_back = jax.vjp(
        partial(head_prep, angles=angles), key_raw, key_gain.astype(jnp.float32)
    )
    query_narrow = query_heads.astype(narrow_dtype)
    key_value = jnp.concatenate(
        [key_heads, value_raw.reshape(key_heads.shape)], axis=0
    ).astype(narrow_dtype)
    attended_low, exp_sums, key_value_all = attend_call(6, query_narrow, key_value)
    attended_flat = attended_low.reshape(-1, token_rows)
    third = second + lax.dot_general(
        attended_flat, w_output, (((0,), (1,)), ((), ())), preferred_element_type=jnp.float32
    )
    normed_four, norm_back_four = jax.vjp(rms_scale, third, ff_norm_two.astype(jnp.float32))
    four_low, one_blocks = lax.optimization_barrier((normed_four.astype(narrow_dtype), one_blocks))
    grad_four, _, two_gate, two_rest, outs_two = ff_call("both", 2, four_low, gate2, up2, down2, given)
    shards = lax.axis_size("fsdp")
    ff_two_gate = lax.psum(two_gate, "ctx")
    grad_final = cotangent[0].astype(jnp.float32)
    grad_third_part, grad_ff_norm_two = norm_back_four(grad_four)
    grad_third = grad_final + grad_third_part
    output_low = grad_third.astype(narrow_dtype)
    attended_gradient = lax.dot_general(
        w_output, output_low, (((0,), (1,)), ((), ())), preferred_element_type=jnp.float32
    )
    grad_w_output = (
        lax.dot_general(
            output_low, attended_flat, (((0,), (1,)), ((), ())), preferred_element_type=jnp.float32
        )
        .astype(narrow_dtype)
        .reshape(lax.axis_size("fsdp"), -1, MODEL_WIDTH)
    )
    grad_query, grad_key_value, ff_out_two = attend_back_call(
        7,
        query_narrow,
        key_value_all,
        attended_gradient.astype(narrow_dtype).reshape(query_narrow.shape),
        attended_low,
        exp_sums,
        outs_two,
    )
    final = third + ff_out_two
    grad_query, ff_two_gate = lax.optimization_barrier((grad_query, ff_two_gate))
    key_count = grad_key_value.shape[0] // 2
    grad_query_raw, grad_query_gain = query_back(grad_query)
    raw_key_gradient, key_gain_gradient = key_back(grad_key_value[:key_count])
    query_grad_low = grad_query_raw.astype(narrow_dtype)
    key_grad_low = raw_key_gradient.astype(narrow_dtype)
    value_grad_low = grad_key_value[key_count:].astype(narrow_dtype).reshape(key_grad_low.shape)
    grad_three = (
        dot_cols(query_grad_low, w_query)
        + dot_cols(key_grad_low, w_key)
        + dot_cols(value_grad_low, w_value)
    )
    grad_rows = [
        one.reshape(shards, -1, token_rows) for one in (query_grad_low, key_grad_low, value_grad_low)
    ]
    widths = [one.shape[1] for one in grad_rows]
    grad_rows = jnp.concatenate(grad_rows, axis=1).reshape(-1, token_rows)
    grad_w_qkv = (
        dot_plain(grad_rows, three_low).astype(narrow_dtype).reshape(shards, sum(widths), -1)
    )
    grad_second_part, grad_attn_norm = norm_back_three(grad_three)
    grad_second = grad_third + grad_second_part
    two_rest, ff_two_gate = lax.optimization_barrier((two_rest, ff_two_gate))
    ff_two_rest = lax.psum(two_rest, "ctx")
    grad_two, _, one_grads = ff_call(
        "backward", 3, grad_second.astype(narrow_dtype), gate1, up1, down1, inputs_one
    )
    grad_two, one_grads, ff_two_rest = lax.optimization_barrier((grad_two, one_grads, ff_two_rest))
    ff_one = lax.psum(one_grads, "ctx")
    ff_one, ff_two = [
        [
            one[at : at + gate1.shape[0]].astype(jnp.float32)
            for at in range(0, one.shape[0], gate1.shape[0])
        ]
        for one in (ff_one, ff_two_rest)
    ]
    ff_two = [ff_two_gate.astype(jnp.float32)] + ff_two
    grad_first_part, grad_ff_norm_one = norm_back_two(grad_two)
    grad_first = grad_second + grad_first_part
    first_low = grad_first.astype(narrow_dtype)
    grad_gated = dot_plain(first_low, mix_out)
    grad_mix_out = (
        dot_cols(first_low, gated_low).astype(narrow_dtype).reshape(shards, -1, MODEL_WIDTH)
    )
    grad_c_part = grad_gated * conv_out
    grad_conv = grad_gated * c_part
    grad_front_ext = conv_input_grad(grad_conv[:block], kernel)
    grad_back_ext = conv_input_grad(grad_conv[block:], kernel)
    back_before = grad_back_ext[:margin]
    outgoing = jnp.concatenate(
        [grad_front_ext[:margin], jnp.where(is_last, 0.0, back_before)], axis=0
    )
    returned = extended_2(outgoing, (("ctx", 0),), margin)
    from_prev = returned[:margin]
    from_next = returned[returned.shape[0] - margin :]
    own_edge = jnp.where(is_last, back_before, 0.0)
    front_grad = grad_front_ext[margin:]
    back_grad = grad_back_ext[margin:]
    front_grad = jnp.concatenate(
        [front_grad[: block - margin], front_grad[block - margin :] + from_next + own_edge], axis=0
    )
    back_grad = jnp.concatenate(
        [back_grad[: block - margin], back_grad[block - margin :] + from_prev], axis=0
    )
    grad_mixed = jnp.concatenate([front_grad, back_grad], axis=0)
    grad_kernel = kernel_grad(front_ext, grad_conv[:block]) + kernel_grad(
        back_ext, grad_conv[block:]
    )
    grad_projected = jnp.concatenate(
        [grad_mixed * x_part, grad_c_part, grad_mixed * b_part], axis=-1
    ).astype(narrow_dtype)
    grad_one = dot_plain(grad_projected, mix_in)
    grad_start_part, grad_mix_norm = norm_back_one(grad_one)
    grad_start = grad_first + grad_start_part
    smalls = (
        grad_mix_norm,
        grad_kernel.reshape(-1),
        grad_ff_norm_one,
        grad_attn_norm,
        grad_query_gain,
        key_gain_gradient,
        grad_ff_norm_two,
    )
    pieces = [one.reshape(shards, -1) for one in smalls]
    sizes = [one.shape[1] for one in pieces]
    small = jnp.concatenate(pieces + [jnp.zeros((shards, 2048 - sum(sizes)), jnp.float32)], axis=1)
    grad_w_qkv, grad_w_output, grad_mix_out, grad_mix_in, small_sum = tail_call(
        5, [grad_w_qkv, grad_w_output, grad_mix_out], grad_projected, one_blocks,
        small.reshape(shards, 16, 128),
    )
    grad_w_query = grad_w_qkv[: widths[0]]
    grad_w_key = grad_w_qkv[widths[0] : widths[0] + widths[1]]
    grad_w_value = grad_w_qkv[widths[0] + widths[1] :]
    small_out = []
    at = 0
    for one in sizes:
        small_out.append(small_sum[at : at + one])
        at += one
    return (
        final.astype(narrow_dtype)[None],
        grad_start[None],
        small_out[0],
        grad_mix_in,
        small_out[1].reshape(-1, KW),
        grad_mix_out,
        small_out[2],
        ff_one[0],
        ff_one[1],
        ff_one[2],
        small_out[3],
        grad_w_query,
        grad_w_key,
        grad_w_value,
        small_out[4],
        small_out[5],
        grad_w_output,
        small_out[6],
        ff_two[0],
        ff_two[1],
        ff_two[2],
    )


def solution(mesh):
    in_specs = (
        P("fsdp", "ctx", None),
        P("fsdp", "ctx", None),
        P("fsdp"),
        P("fsdp", None),
        P("fsdp", None),
        P("fsdp", None),
        P("fsdp"),
        P("fsdp", None),
        P("fsdp", None),
        P("fsdp", None),
        P("fsdp"),
        P("fsdp", None),
        P("fsdp", None),
        P("fsdp", None),
        P("fsdp"),
        P("fsdp"),
        P("fsdp", None),
        P("fsdp"),
        P("fsdp", None),
        P("fsdp", None),
        P("fsdp", None),
    )
    out_specs = (
        P("fsdp", "ctx", None),
        P("fsdp", "ctx", None),
        P("fsdp"),
        P("fsdp", None),
        P("fsdp", None),
        P("fsdp", None),
        P("fsdp"),
        P("fsdp", None),
        P("fsdp", None),
        P("fsdp", None),
        P("fsdp"),
        P("fsdp", None),
        P("fsdp", None),
        P("fsdp", None),
        P("fsdp"),
        P("fsdp"),
        P("fsdp", None),
        P("fsdp"),
        P("fsdp", None),
        P("fsdp", None),
        P("fsdp", None),
    )
    return jax.shard_map(local, mesh=mesh, in_specs=in_specs, out_specs=out_specs, check_vma=False)
```

time: 1400 us -> 1040 us (0.74)
  matrix products: 176 us -> 60.9 us
  waiting for transfers between devices: 92.1 us -> 30.7 us
  local copies, waits for them, and re-layouts: 99.7 us -> 43.2 us
  blocking collectives: 42.9 us -> 0 us
  other arithmetic: 101 us -> 59.7 us
  Pallas kernels: 845 us -> 809 us
    pallas_call x0 -> x2, Pallas kernels: none -> 98.4 us  [the longest x1 60.5 us: attend_back_call(): pl.pallas_call(partial(attend_back_kernel, chips, count, groups), out_sha...]
    pallas_call x1, Pallas kernels: 319 us -> 234 us  [tail_call(): pl.pallas_call(partial(tail_kernel, chips, count, pieces), out_shape=[jax...]
    pallas_call x3, Pallas kernels: 399 us -> 349 us  [ff_call(): pl.pallas_call(partial(ff_kernel, chips, mode), out_shape=outs, in_specs=...]
    dot_general x9 -> x4, matrix products: 60.7 us -> 14.2 us  [dot_cols(): lax.dot_general(left, right, (((0,), (0,)), ((), ())), preferred_element_...]
    psum x1 -> x0, blocking collectives: 42.9 us -> none  [local(): small_sum = lax.psum(jnp.concatenate(smalls), ('fsdp', 'ctx'))]
    dot_general x5 -> x3, matrix products: 50 us -> 9.29 us  [the longest x1 4.11 us: local(): lax.dot_general(w_output, output_low, (((0,), (1,)), ((), ())), preferred...]
    reduce_scatter x1 -> x0, waiting for transfers between devices: 36 us -> none  [local(): lax.psum_scatter(outs_two, 'fsdp', scatter_dimension=0, tiled=True)]
    gather x6 -> x0, local copies, waits for them, and re-layouts: 29.9 us -> none  [local(): jnp.take(outs_two.reshape(shards, -1), sources, axis=0)]
  transfers between devices with their start and end apart: 14 -> 10, of which waited for: 6 -> 4; matrix products, arithmetic and copies ran while one was open for 17% -> 12% of each run, Pallas kernels for 52% -> 66%
where the time goes in v2:
time: 1040 us; the launch traced here: 1030 us
  Pallas kernels  809 us (78%)
  matrix products  60.9 us (6%)
  other arithmetic  59.7 us (6%)
  local copies, waits for them, and re-layouts  43.2 us (4%)
  waiting for transfers between devices  30.7 us (3%)
  between operations  15.8 us (2%)
  starting transfers between devices  11.3 us (1%)
    pallas_call x3, Pallas kernels, ff_call(): pl.pallas_call(partial(ff_kernel, chips, mode), out_shape=outs, in_specs=...  349 us
    pallas_call x1, Pallas kernels, tail_call(): pl.pallas_call(partial(tail_kernel, chips, count, pieces), out_shape=[jax...  234 us
    pallas_call x1, Pallas kernels, head_call(): pl.pallas_call(partial(head_kernel, chips, count), out_shape=outs, in_spe...  127 us
    pallas_call x1, Pallas kernels, attend_back_call(): pl.pallas_call(partial(attend_back_kernel, chips, count, groups), out_sha...  60.5 us
    pallas_call x1, Pallas kernels, attend_call(): pl.pallas_call(partial(attend_kernel, count, groups), out_shape=[jax.Shap...  37.9 us
    dot_general x3, matrix products, dot_plain(): return jnp.dot(left, right, preferred_element_type=jnp.float32)  22.3 us
  transfers between devices with their start and end apart: 10, of which 4 were waited for; matrix products, arithmetic and copies ran while one was open for 12% of the time, Pallas kernels for 66%

profile of v2, /device:TPU:16, one launch (start us, length us, event | category | flops | bytes accessed | tf_op | source)
XLA Modules:
  0.0 1031.1 jit_solution(4769106692804882323)
XLA Ops:
  7.3 1.5 pad_maximum_fusion.1
  10.8 127.4 %shard_map.364 = (bf16[8,4,144,1536]{3,2,1,0:T(8,128)(2,1)}, bf16[8,4,48,1536]{3,2,1,0:T(8,128)(2,1)}, bf16[8,256,1536]{2,1,0:T(8,128)(2,1)}, bf16[8,16,128]{2,1,0:T(8,128)(2,1)}) custom-call(bf16[4,144,1536]{2,1,0:T(8,128)(2,1)} %bitcast.113, bf16[4,48,1536]{2,1,0:T(8,128)(2,1)} %bitcast.117, bf16[256,1536]{1,0:T(8,128)(2,1)} %bitcast.111, ...), custom_call_target="tpu_custom_call" | custom-call | bytes 37748736 | tf_op jit(solution)/shard_map/pallas_call | solution.py:622
  140.1 1.1 slice_reduce_fusion.2
  141.5 0.9 copy-done.43
  142.4 7.9 fusion.56
  150.6 1.3 collective-permute-start.1
  151.9 4.3 collective-permute-done.1
  156.2 4.0 collective-permute-start
  160.3 1.2 collective-permute-done
  163.7 0.9 slice-done.4
  164.9 1.5 multiply_reduce_fusion.11
  167.5 1.1 multiply_convert_fusion.5.refs_0_
  168.6 103.7 %shard_map.365 = (f32[256,1536]{1,0:T(8,128)}, bf16[8,256,1536]{2,1,0:T(8,128)(2,1)}) custom-call(bf16[256,1536]{1,0:T(8,128)(2,1)} %multiply_convert_fusion.5.refs_0_, bf16[864,1536]{1,0:T(8,128)(2,1)} %refs_2_.5, bf16[864,1536]{1,0:T(8,128)(2,1)} %refs_3_.5, bf16[864,1536]{1,0:T(8,128)(2,1)} %refs_4_.3), custom_call_target="tpu_custom_call" | custom-call | flops 16307453952 | bytes 12582912 | tf_op jit(solution)/shard_map/pallas_call | solution.py:162
  273.5 1.7 multiply_reduce_fusion.10
  275.8 2.3 multiply_reduce_fusion.20
  278.3 2.0 fusion.19
  280.4 7.0 fusion.49
  287.4 1.5 multiply_reduce_fusion.9
  291.1 37.9 %shard_map.366 = (bf16[24,64,256]{2,1,0:T(8,128)(2,1)S(1)}, f32[24,1,256]{2,1,0:T(1,128)S(1)}, bf16[4,16,64,256]{3,2,1,0:T(8,128)(2,1)S(1)}) custom-call(bf16[24,64,256]{2,1,0:T(8,128)(2,1)S(1)} %pad_maximum_fusion.6.q, bf16[16,64,256]{2,1,0:T(8,128)(2,1)S(1)} %pad_maximum_fusion.7.kv), custom_call_target="tpu_custom_call" | custom-call | flops 1610612736 | bytes 5767168 | tf_op jit(solution)/shard_map/pallas_call | solution.py:1051
  329.1 1.5 multiply_reduce_fusion.8
  330.7 1.3 multiply_convert_fusion.3.refs_0_
  332.0 7.4 all-gather.10.cloned.1.call-done
  339.4 125.0 %shard_map.367 = (f32[256,1536]{1,0:T(8,128)}, bf16[8,256,1536]{2,1,0:T(8,128)(2,1)}, bf16[864,1536]{1,0:T(8,128)(2,1)}, bf16[1728,1536]{1,0:T(8,128)(2,1)}, bf16[8,256,1536]{2,1,0:T(8,128)(2,1)}) custom-call(bf16[256,1536]{1,0:T(8,128)(2,1)} %multiply_convert_fusion.3.refs_0_, bf16[8,256,1536]{2,1,0:T(8,128)(2,1)} %get-tuple-element.66.refs_1_, ...), custom_call_target="tpu_custom_call" | custom-call | flops 48922361856 | bytes 12582912 | tf_op jit(solution)/shard_map/pallas_call | solution.py:162
  464.4 1.9 multiply_reduce_fusion
  467.2 4.1 convolution_convert_fusion.3
  471.4 60.5 %shard_map.368 = (f32[24,64,256]{2,1,0:T(8,128)S(1)}, f32[16,64,256]{2,1,0:T(8,128)S(1)}, f32[256,1536]{1,0:T(8,128)S(1)}) custom-call(bf16[24,64,256]{2,1,0:T(8,128)(2,1)S(1)} %copy-done.1, bf16[4,16,64,256]{3,2,1,0:T(8,128)(2,1)S(1)} %copy-done.6, bf16[24,64,256]{2,1,0:T(8,128)(2,1)S(1)} %bitcast.88, bf16[24,64,256]{2,1,0:T(8,128)(2,1)S(1)} %copy-done.3, ...), custom_call_target="tpu_custom_call" | custom-call | flops 4026531840 | bytes 8912896 | tf_op jit(solution)/shard_map/pallas_call | solution.py:1225
  531.9 0.9 convert.42
  533.8 1.3 reshape.455
  536.5 1.3 fusion.29
  537.8 3.3 convolution_bitcast_fusion
  541.0 3.3 convolution_bitcast_fusion.1
  544.3 3.6 convolution_convert_fusion.2
  548.0 17.7 %all-reduce.11.cloned.1.call-done = bf16[864,1536]{1,0:T(8,128)(2,1)} async-done(((bf16[864,1536]{1,0:T(8,128)(2,1)}), bf16[864,1536]{1,0:T(8,128)(2,1)}) %all-reduce.11.cloned.1.call-update) | async-done | bytes 2654224 | tf_op jit(solution)/shard_map/psum | solution.py:1379
  566.4 0.8 copy-done.25
  569.6 5.4 convolution_convert_fusion
  575.0 2.9 multiply_reduce_fusion.2
  578.1 5.0 convert_element_type.226
  583.1 1.8 fusion.47
  584.9 120.8 %shard_map.369 = (f32[256,1536]{1,0:T(8,128)}, bf16[8,256,1536]{2,1,0:T(8,128)(2,1)}, bf16[2592,1536]{1,0:T(8,128)(2,1)}) custom-call(bf16[256,1536]{1,0:T(8,128)(2,1)} %get-tuple-element.155.refs_0_, bf16[8,256,1536]{2,1,0:T(8,128)(2,1)} %get-tuple-element.75.refs_1_, bf16[864,1536]{1,0:T(8,128)(2,1)} %refs_2_.5, bf16[864,1536]{1,0:T(8,128)(2,1)} %refs_3_.5, ...), custom_call_target="tpu_custom_call" | custom-call | flops 48922361856 | bytes 12582912 | tf_op jit(solution)/shard_map/pallas_call | solution.py:162
  705.7 2.4 multiply_reduce_fusion.3
  708.6 1.9 fusion.8
  710.5 5.8 multiply_convert_fusion.1
  716.3 1.7 multiply_reduce_fusion.14
  718.7 3.2 multiply_add_fusion.1
  722.0 3.3 collective-permute-start.3
  725.4 1.8 collective-permute-start.2
  727.2 4.7 convolution_convert_fusion.1
  732.0 5.6 slice_convert_fusion.3
  737.6 0.9 slice.335
  738.6 0.9 slice.340
  740.3 0.9 fusion.36
  741.2 3.3 multiply_convert_fusion.2
  744.5 11.1 %fusion.4 = (f32[1536]{0:T(1024)S(1)}, f32[256]{0:T(256)S(1)}, f32[256,1536]{1,0:T(8,128)}) fusion(bf16[1,256,1536]{2,1,0:T(8,128)(2,1)S(1)} %copy-done.27, f32[256]{0:T(256)S(1)} %copy-done.78, f32[1536]{0:T(1024)S(1)} %copy-done.64, bf16[4608,1536]{1,0:T(8,128)(2,1)} %bitcast.130, bf16[256,1536]{1,0:T(8,128)(2,1)S(1)} %get-tuple-element.165, ...), kind=kOutput, calls=%fused_computation.29 | convolution fusion | flops 3633707264 | bytes 18888704 | tf_op jit(solution)/shard_map/dot_general | solution.py:69
  756.5 3.5 fusion.22
  760.0 4.5 copy.48
  764.4 234.2 %shard_map.370 = (bf16[11,4,16,1536]{3,2,1,0:T(8,128)(2,1)}, bf16[4,144,1536]{2,1,0:T(8,128)(2,1)}, f32[16,128]{1,0:T(8,128)}) custom-call(bf16[4,2,5,4,16,1536]{5,4,3,2,1,0:T(8,128)(2,1)} %bitcast.89, bf16[4,2,3,4,16,1536]{5,4,3,2,1,0:T(8,128)(2,1)} %bitcast.90, bf16[4,2,3,4,16,1536]{5,4,3,2,1,0:T(8,128)(2,1)} %bitcast.91, ...), custom_call_target="tpu_custom_call" | custom-call | flops 3623878656 | bytes 34603008 | tf_op jit(solution)/shard_map/pallas_call | solution.py:915
  1000.3 1.3 fusion.55
  1001.6 1.4 fusion.54
  1003.1 2.0 fusion.51
  1005.0 3.5 fusion.50
  1008.5 2.4 bitcast_convert_fusion
  1011.2 0.9 copy-done.51
  1012.1 2.1 fusion.10
  1014.2 9.8 slice_convert_fusion
  (297 shorter events, 23.4 us)
Async XLA Ops:
  7.2 131.0 %all-gather.6.cloned.1.call-start = ((), (), s32[]{:S(2)}) async-start(), calls=%async_computation | async-start | bytes 3538944 | tf_op jit(solution)/shard_map/all_gather | solution.py:1307
  9.6 266.2 %all-gather.8.cloned.1.call-start = ((), (), s32[]{:S(2)}) async-start(), calls=%async_computation.4 | async-start | bytes 15728640 | tf_op jit(solution)/shard_map/all_gather | solution.py:1312
  138.3 201.1 %all-gather.10.cloned.1.call-start = ((), (), s32[]{:S(2)}) async-start(), calls=%async_computation.5 | async-start | bytes 7077888 | tf_op jit(solution)/shard_map/all_gather | solution.py:1347
  139.9 27.1 %copy-start.55 = (f32[1536]{0:T(1024)}, f32[1536]{0:T(1024)S(1)}, u32[]{:S(2)}) copy-start(f32[1536]{0:T(1024)S(1)} %reshape.463) | copy-start | bytes 18436
  141.2 20.4 %copy-start.57 = (f32[1536]{0:T(1024)}, f32[1536]{0:T(1024)S(1)}, u32[]{:S(2)}) copy-start(f32[1536]{0:T(1024)S(1)} %get-tuple-element.152) | copy-start | bytes 18436
  141.2 20.4 %copy-start.59 = (f32[1536]{0:T(1024)}, f32[1536]{0:T(1024)S(1)}, u32[]{:S(2)}) copy-start(f32[1536]{0:T(1024)S(1)} %get-tuple-element.153) | copy-start | bytes 18436
  141.2 20.4 %copy-start.61 = (f32[1536]{0:T(1024)}, f32[1536]{0:T(1024)S(1)}, u32[]{:S(2)}) copy-start(f32[1536]{0:T(1024)S(1)} %get-tuple-element.154) | copy-start | bytes 18436
  141.3 9.1 copy-start.77
  150.3 12.2 %copy-start.23 = (f32[256,4608]{1,0:T(8,128)}, f32[256,4608]{1,0:T(8,128)S(1)}, u32[]{:S(2)}) copy-start(f32[256,4608]{1,0:T(8,128)S(1)} %fusion.56) | copy-start | bytes 14155780
  150.6 5.6 collective-permute-start.1
  156.2 5.3 collective-permute-start
  161.5 3.1 slice-start.4
  161.7 3.2 slice-start.5
  166.4 107.1 %copy-start.16 = (f32[256,1536]{1,0:T(8,128)}, f32[256,1536]{1,0:T(8,128)S(1)}, u32[]{:S(2)}) copy-start(f32[256,1536]{1,0:T(8,128)S(1)} %get-tuple-element.210) | copy-start | bytes 4718596
  272.3 293.4 %all-reduce.11.cloned.1.call-start = ((), (), s32[]{:S(2)}) async-start(), calls=%async_computation.1 | async-start | bytes 5308416 | tf_op jit(solution)/shard_map/psum | solution.py:1379
  273.1 5.1 copy-start.79
  273.1 16.5 %copy-start.81 = (f32[64]{0:T(128)}, f32[64]{0:T(128)S(1)}, u32[]{:S(2)}) copy-start(f32[64]{0:T(128)S(1)} %reshape.465) | copy-start | bytes 772
  275.1 54.0 %copy-start.14 = (f32[256,1536]{1,0:T(8,128)}, f32[256,1536]{1,0:T(8,128)S(1)}, u32[]{:S(2)}) copy-start(f32[256,1536]{1,0:T(8,128)S(1)} %get-tuple-element.158) | copy-start | bytes 4718596
  275.8 11.6 %copy-start.44 = (bf16[256,1536]{1,0:T(8,128)(2,1)}, bf16[256,1536]{1,0:T(8,128)(2,1)S(1)}, u32[]{:S(2)}) copy-start(bf16[256,1536]{1,0:T(8,128)(2,1)S(1)} %multiply_convert_fusion.4) | copy-start | bytes 2359300
  291.0 38.1 %slice-start.6 = ((s8[4718592]{0:T(1024)(128)(4,1)}), s8[4194304]{0:T(1024)(128)(4,1)S(1)}, s32[]{:S(2)}) async-start(s8[4718592]{0:T(1024)(128)(4,1)} %bitcast.108), calls=%async_computation.12 | async-start | bytes 8388608
  291.1 38.0 %copy-start = (bf16[24,64,256]{2,1,0:T(8,128)(2,1)}, bf16[24,64,256]{2,1,0:T(8,128)(2,1)S(1)}, u32[]{:S(2)}) copy-start(bf16[24,64,256]{2,1,0:T(8,128)(2,1)S(1)} %pad_maximum_fusion.6.q) | copy-start | bytes 2359300
  291.1 38.0 %slice-start.7 = ((s8[4718592]{0:T(1024)(128)(4,1)}), s8[524288]{0:T(1024)(128)(4,1)S(1)}, s32[]{:S(2)}) async-start(s8[4718592]{0:T(1024)(128)(4,1)} %bitcast.108), calls=%async_computation.13 | async-start | bytes 1048576
  330.7 135.6 %copy-start.18 = (f32[256,1536]{1,0:T(8,128)}, f32[256,1536]{1,0:T(8,128)S(1)}, u32[]{:S(2)}) copy-start(f32[256,1536]{1,0:T(8,128)S(1)} %get-tuple-element.216) | copy-start | bytes 4718596
  466.9 4.4 copy-start.20
  466.9 238.7 %all-reduce.13.cloned.1.call-start = ((), (), s32[]{:S(2)}) async-start(), calls=%async_computation.2 | async-start | bytes 10616832 | tf_op jit(solution)/shard_map/psum | solution.py:1427
  467.2 4.2 copy-start.1
  467.2 4.2 copy-start.3
  467.2 4.2 copy-start.6
  537.7 3.3 copy-start.53
  537.8 3.3 copy-start.52
  541.0 3.3 copy-start.4
  541.0 3.3 copy-start.21
  565.7 448.5 %all-reduce.15.cloned.1.call-start = ((), (), s32[]{:S(2)}) async-start(), calls=%async_computation.3 | async-start | bytes 15925248 | tf_op jit(solution)/shard_map/psum | solution.py:1432
  569.0 6.0 slice-start
  569.6 5.4 slice-start.1
  569.6 5.4 copy-start.15
  569.6 5.4 copy-start.49
  569.6 5.4 copy-start.50
  569.6 5.4 copy-start.71
  575.0 2.9 copy-start.76
  578.1 5.0 copy-start.22
  578.1 5.0 copy-start.32
  584.9 120.8 %copy-start.56 = (f32[1536]{0:T(1024)S(1)}, f32[1536]{0:T(1024)}, u32[]{:S(2)}) copy-start(f32[1536]{0:T(1024)} %copy-done.55) | copy-start | bytes 18436
  584.9 120.8 %copy-start.69 = (f32[256]{0:T(256)S(1)}, f32[256]{0:T(256)}, u32[]{:S(2)}) copy-start(f32[256]{0:T(256)} %copy-done.68) | copy-start | bytes 3076
  710.5 16.7 %copy-start.11 = (f32[256,1536]{1,0:T(8,128)}, f32[256,1536]{1,0:T(8,128)S(1)}, u32[]{:S(2)}) copy-start(f32[256,1536]{1,0:T(8,128)S(1)} %fusion.8) | copy-start | bytes 4718596
  710.5 5.8 copy-start.8
  710.5 5.8 copy-start.10
  718.7 13.3 %slice-start.2 = ((s8[5308416]{0:T(1024)(128)(4,1)}), s8[4194304]{0:T(1024)(128)(4,1)S(1)}, s32[]{:S(2)}) async-start(s8[5308416]{0:T(1024)(128)(4,1)} %bitcast.101), calls=%async_computation.8 | async-start | bytes 8388608
  721.9 15.7 %copy-start.38 = (f32[130,1536]{1,0:T(8,128)}, f32[130,1536]{1,0:T(8,128)S(1)}, u32[]{:S(2)}) copy-start(f32[130,1536]{1,0:T(8,128)S(1)} %get-tuple-element.197) | copy-start | bytes 2396164
  721.9 16.7 %copy-start.37 = (f32[130,1536]{1,0:T(8,128)}, f32[130,1536]{1,0:T(8,128)S(1)}, u32[]{:S(2)}) copy-start(f32[130,1536]{1,0:T(8,128)S(1)} %get-tuple-element.198) | copy-start | bytes 2396164
  722.0 18.3 %collective-permute-start.3 = (f32[2,1536]{1,0:T(2,128)S(1)}, f32[2,1536]{1,0:T(2,128)S(1)}, u32[]{:S(2)}, u32[]{:S(2)}) collective-permute-start(f32[2,1536]{1,0:T(2,128)S(1)} %broadcast_select_fusion), channel_id=1, source_target_pairs={{0,8},{8,16},{16,24},{1,9},{9,17},{17,25},{2,10},{10,18},{18,26},{... | collective-permute-start | bytes 36872 | tf_op jit(solution)/shard_map/ppermute | solution.py:29
  725.4 6.6 slice-start.3
  725.4 14.9 %collective-permute-start.2 = (f32[2,1536]{1,0:T(2,128)S(1)}, f32[2,1536]{1,0:T(2,128)S(1)}, u32[]{:S(2)}, u32[]{:S(2)}) collective-permute-start(f32[2,1536]{1,0:T(2,128)S(1)} %slice.337), channel_id=1, source_target_pairs={{8,0},{16,8},{24,16},{9,1},{17,9},{25,17},{10,2},{18,10},{26,18},{... | collective-permute-start | bytes 36872 | tf_op jit(solution)/shard_map/ppermute | solution.py:30
  741.2 3.3 copy-start.27
  741.2 3.3 copy-start.39
  741.2 3.3 copy-start.64
  741.2 3.3 copy-start.78
  744.5 11.2 %copy-start.40 = (bf16[256,1536]{1,0:T(8,128)(2,1)}, bf16[256,1536]{1,0:T(8,128)(2,1)S(1)}, u32[]{:S(2)}) copy-start(bf16[256,1536]{1,0:T(8,128)(2,1)S(1)} %get-tuple-element.164) | copy-start | bytes 2359300
  744.5 11.2 %copy-start.41 = (bf16[256,1536]{1,0:T(8,128)(2,1)}, bf16[256,1536]{1,0:T(8,128)(2,1)S(1)}, u32[]{:S(2)}) copy-start(bf16[256,1536]{1,0:T(8,128)(2,1)S(1)} %get-tuple-element.165) | copy-start | bytes 2359300
  744.5 11.2 %copy-start.65 = (f32[8,192]{1,0:T(8,128)S(1)}, f32[8,192]{1,0:T(8,128)}, u32[]{:S(2)}) copy-start(f32[8,192]{1,0:T(8,128)} %reshape.456) | copy-start | bytes 18436
  744.5 11.2 %copy-start.72 = (f32[8,8]{1,0:T(8,128)S(1)}, f32[8,8]{1,0:T(8,128)}, u32[]{:S(2)}) copy-start(f32[8,8]{1,0:T(8,128)} %reshape.455) | copy-start | bytes 772
  764.4 235.9 %copy-start.74 = (f32[256]{0:T(256)S(1)}, f32[256]{0:T(256)}, u32[]{:S(2)}) copy-start(f32[256]{0:T(256)} %copy-done.73) | copy-start | bytes 3076
  1005.0 3.5 copy-start.48
  1008.5 3.6 copy-start.51
  (47 other events, 78.4 us)
Sparse Core Ops, SparseCore 0:
  10.2 63.7 all-gather.5
  138.4 123.6 all-gather.7
  272.4 66.8 all-gather.9
  467.1 98.5 all-reduce.10
  569.2 122.2 all-reduce.12
  718.1 229.3 all-reduce.14

commit v3 on v2

--- a/solution.py
+++ b/solution.py
@@ -135,12 +135,14 @@
     blocks = jax.ShapeDtypeStruct((size, rows, width), bf16)
     vmem = pl.BlockSpec(memory_space=pltpu.VMEM)
     anywhere = pl.BlockSpec(memory_space=pl.ANY)
-    outs = [jax.ShapeDtypeStruct((rows, width), jnp.float32), blocks]
-    out_specs = [vmem, vmem]
+    outs = [jax.ShapeDtypeStruct((rows, width), jnp.float32)] + [blocks] * forward
+    out_specs = [vmem] * len(outs)
     args = [x, gate, up_w, down]
-    specs = [vmem] * 4
+    specs = [vmem] + [anywhere] * 3
     dma = pltpu.SemaphoreType.DMA
-    scratch = [pltpu.VMEM((rows, width), jnp.float32)]
+    scratch = [] if forward else [pltpu.VMEM(blocks.shape, bf16)]
+    scratch += [pltpu.VMEM(gate.shape, bf16)] * 3 + [dma((3,))]
+    scratch += [pltpu.VMEM((rows, width), jnp.float32)]
     scratch += [pltpu.VMEM((chips, rows, width), bf16)] * 3
     scratch += [pltpu.VMEM((chips + 1, rows, width), bf16)]
     scratch += [dma((chips,))] * 8 + [dma((chips, 4))] * 4
@@ -206,17 +208,18 @@
         x_ref, gate, up_w, down, out, xall = refs[:6]
         rest = refs[6:]
     elif mode == "both":
-        x_ref, y_hbm, gate, up_w, down, out, xall, gate_grads, weight_grads, result = refs[:10]
+        x_ref, y_hbm, gate, up_w, down, out, gate_grads, weight_grads, result, xall = refs[:10]
         rest = refs[10:]
     else:
-        x_ref, y_hbm, gate, up_w, down, out, xall, weight_grads = refs[:8]
+        x_ref, y_hbm, gate, up_w, down, out, weight_grads, xall = refs[:8]
         rest = refs[8:]
-    part, term, other_send, other_recv, in_sum = rest[:5]
-    (up_s, up_r, down_s, down_r, core_s, core_r, ps_s, ps_r, ups_s, ups_r, downs_s, downs_r) = rest[5:17]
+    weights = (gate, up_w, down)
+    gate, up_w, down, weight_m, part, term, other_send, other_recv, in_sum = rest[:9]
+    (up_s, up_r, down_s, down_r, core_s, core_r, ps_s, ps_r, ups_s, ups_r, downs_s, downs_r) = rest[9:21]
     if not forward:
-        yall, hid, dgate, dup, stage, ysem, stage_sem = rest[17:24]
+        yall, hid, dgate, dup, stage, ysem, stage_sem = rest[21:28]
         if mode == "both":
-            out_stage, out_sem = rest[24:]
+            out_stage, out_sem = rest[28:]
     rows, width = x_ref.shape
     units = gate.shape[0]
     place, chip, core, _, _, peer = places()
@@ -226,6 +229,12 @@
     above = {"fsdp": lax.rem(place + 2, 2 * chips)}
     pieces = 4
     piece = rows // pieces
+    loads = [
+        pltpu.make_async_copy(one, into, weight_m.at[n])
+        for n, (one, into) in enumerate(zip(weights, (gate, up_w, down)))
+    ]
+    for one in loads:
+        one.start()
     greet([below, above, {"fsdp": peer}])
 
     def up_rows(d):
@@ -347,6 +356,11 @@
 
         d = turn(r)
 
+        @pl.when(r == 0)
+        def _():
+            for one in loads:
+                one.wait()
+
         @pl.loop(0, 2)
         def _(o):
             @pl.when(o == 1)
@@ -511,10 +525,10 @@
 
 def head_kernel(chips, count, *refs):
     shards = refs[:2]
-    block, vector = refs[2:4]
-    wholes = refs[4:6]
-    blocks, vectors = refs[6:8]
-    local, near_s, near_r, hop_s, hop_r, side_s, side_r, pass_s, pass_r = refs[8:]
+    block, vector, edge = refs[2:5]
+    wholes = refs[5:7]
+    blocks, vectors, edges = refs[7:10]
+    local, near_s, near_r, hop_s, hop_r, side_s, side_r, pass_s, pass_r, edge_s, edge_r = refs[10:]
     place, chip, core, after, before, peer = places()
     here = lax.axis_index("ctx")
     others = [{"ctx": lax.rem(here + t, count)} for t in range(1, count)]
@@ -572,6 +586,14 @@
     came = [one.at[peer] for one in (*wholes, blocks, vectors)]
     sources = [shards[0], shards[1], block, vector]
     order = (3, 0, 1, 2)
+
+    def edge_copy(t):
+        return push(edge, edges.at[t], edge_s.at[t], edge_r.at[t], others[t - 1])
+
+    for t in range(1, count):
+        go(edge_copy(t))
+    first = pltpu.make_async_copy(edge, edges.at[0], edge_s.at[0])
+    first.start()
     for n in order:
         go(hop(0, n))
     keeps = [pltpu.make_async_copy(sources[n], homes[n], local.at[n]) for n in order]
@@ -602,13 +624,16 @@
         for k in range(1, chips):
             for t in range(count if n < 2 else 1):
                 across_in(k, t, n).wait_recv()
+    for t in range(1, count):
+        edge_copy(t).wait_recv()
+    first.wait()
     for one in keeps:
         one.wait()
     for one in started:
         one.wait_send()
 
 
-def head_call(ident, shard_a, shard_b, block, vector):
+def head_call(ident, shard_a, shard_b, block, vector, edge):
     size = lax.axis_size("fsdp")
     count = lax.axis_size("ctx")
     chips = size // 2
@@ -617,25 +642,27 @@
     outs = [jax.ShapeDtypeStruct((size,) + one.shape, jnp.bfloat16) for one in shards]
     outs.append(jax.ShapeDtypeStruct((size,) + block.shape, jnp.bfloat16))
     outs.append(jax.ShapeDtypeStruct((size,) + vector.shape, jnp.bfloat16))
+    outs.append(jax.ShapeDtypeStruct((count,) + edge.shape, jnp.bfloat16))
     anywhere = pl.BlockSpec(memory_space=pl.ANY)
     dma = pltpu.SemaphoreType.DMA
-    whole_a, whole_b, blocks, vectors = pl.pallas_call(
+    whole_a, whole_b, blocks, vectors, edges = pl.pallas_call(
         partial(head_kernel, chips, count),
         out_shape=outs,
-        in_specs=[anywhere] * 4,
-        out_specs=[anywhere] * 4,
+        in_specs=[anywhere] * 5,
+        out_specs=[anywhere] * 5,
         scratch_shapes=[
             dma((4,)), dma((4,)), dma((4,)),
             dma((4, chips)), dma((4, chips)),
             dma((2, chips, count)), dma((2, chips, count)),
             dma((4, chips, count)), dma((4, chips, count)),
+            dma((count,)), dma((count,)),
         ],
         compiler_params=pltpu.CompilerParams(collective_id=ident, has_side_effects=True),
         cost_estimate=pl.CostEstimate(
             flops=0, bytes_accessed=2 * size * (shard_a.size + shard_b.size) * 2, transcendentals=0
         ),
-    )(*shards, block, vector)
-    return whole_a.reshape(-1, width), whole_b.reshape(-1, width), blocks, vectors
+    )(*shards, block, vector, edge)
+    return whole_a.reshape(-1, width), whole_b.reshape(-1, width), blocks, vectors, edges
 
 
 def tail_kernel(chips, count, pieces, *refs):
@@ -992,7 +1019,7 @@
     def apply(values, part):
         return jnp.dot(values, part.astype(jnp.bfloat16), preferred_element_type=jnp.float32)
 
-    @pl.loop(0, key_heads)
+    @pl.loop(0, key_heads, unroll=2)
     def _(h):
         keys = kv[h]
         values = kv[key_heads + h]
@@ -1012,7 +1039,7 @@
 
         @pl.when(there < here)
         def _():
-            @pl.loop(0, key_heads)
+            @pl.loop(0, key_heads, unroll=2)
             def _(h):
                 keys = kv_all[there, h]
                 values = kv_all[there, key_heads + h]
@@ -1024,7 +1051,7 @@
 
         @pl.when(there > here)
         def _():
-            @pl.loop(0, key_heads)
+            @pl.loop(0, key_heads, unroll=2)
             def _(h):
                 keys = kv_all[there, h]
                 values = kv_all[there, key_heads + h]
@@ -1159,7 +1186,7 @@
 
         @pl.when(there < here)
         def _():
-            @pl.loop(0, key_heads)
+            @pl.loop(0, key_heads, unroll=2)
             def _(h):
                 keys = kv_all[there, h][:, front]
                 values = kv_all[there, key_heads + h][:, front]
@@ -1172,7 +1199,7 @@
 
         @pl.when(there > here)
         def _():
-            @pl.loop(0, key_heads)
+            @pl.loop(0, key_heads, unroll=2)
             def _(h):
                 keys = kv_all[there, h]
                 values = kv_all[there, key_heads + h]
@@ -1184,7 +1211,7 @@
         if t < chips:
             hop(t)
 
-    @pl.loop(0, key_heads)
+    @pl.loop(0, key_heads, unroll=2)
     def _(h):
         keys = kv_all[here, h]
         values = kv_all[here, key_heads + h]
@@ -1305,8 +1332,24 @@
     attn_rows = attn_shard.shape[0]
     attn_slice = pick(attn_shard.reshape(ctx_count, -1, MODEL_WIDTH), ctx_place, 0)
     attn_slices = lax.all_gather(attn_slice, "fsdp", axis=0)
-    mix_in, mix_out, given, gathered_vectors = head_call(
-        4, in_proj, out_proj, cotangent[0], vector
+    tails = jnp.concatenate(
+        [
+            hidden_in[0, block - margin : block],
+            hidden_in[0, token_rows - margin :],
+            jnp.zeros((16 - 2 * margin, MODEL_WIDTH), narrow_dtype),
+        ],
+        axis=0,
+    )
+    mix_in, mix_out, given, gathered_vectors, edges = head_call(
+        4, in_proj, out_proj, cotangent[0], vector, tails
+    )
+    edge_rows = jnp.concatenate(
+        [
+            jnp.where(ctx_place == 0, 0.0, edges[1, :margin]).astype(narrow_dtype),
+            jnp.where(is_last, tails[:margin], edges[-1, margin : 2 * margin]),
+            tails[2 * margin :],
+        ],
+        axis=0,
     )
     attn_slices, mix_in = lax.optimization_barrier((attn_slices, mix_in))
     attn_wholes = lax.all_gather(attn_slices, "ctx", axis=1)
@@ -1320,18 +1363,21 @@
     mix_norm, ff_norm_one, attn_norm, ff_norm_two, query_gain, key_gain, mix_kernel = wholes
     mix_kernel = mix_kernel.reshape(-1, KW)
     kernel = mix_kernel.astype(jnp.float32)
-    normed_one, norm_back_one = jax.vjp(rms_scale, start, mix_norm.astype(jnp.float32))
+    gain_one = mix_norm.astype(jnp.float32)
+    normed_one, norm_back_one = jax.vjp(rms_scale, start, gain_one)
     normed_one_low = normed_one.astype(narrow_dtype)
-    projected = dot_rows(normed_one_low, mix_in)
+    edges_low = rms_scale(edge_rows.astype(jnp.float32), gain_one).astype(narrow_dtype)
+    projected_all = dot_rows(jnp.concatenate([normed_one_low, edges_low], axis=0), mix_in)
+    projected = projected_all[:token_rows]
+    edge_mixed = (
+        projected_all[token_rows:, :MODEL_WIDTH] * projected_all[token_rows:, 2 * MODEL_WIDTH :]
+    ).astype(narrow_dtype)
     b_part = projected[:, :MODEL_WIDTH]
     c_part = projected[:, MODEL_WIDTH : 2 * MODEL_WIDTH]
     x_part = projected[:, 2 * MODEL_WIDTH :]
     mixed_low = (b_part * x_part).astype(narrow_dtype)
-    front_tail = mixed_low[block - margin : block]
-    back_tail = mixed_low[token_rows - margin :]
-    edges = extended_2(jnp.concatenate([back_tail, front_tail], axis=0), (("ctx", 0),), margin)
-    before_front = edges[:margin]
-    before_back = jnp.where(is_last, front_tail, edges[edges.shape[0] - margin :])
+    before_front = edge_mixed[:margin]
+    before_back = edge_mixed[margin : 2 * margin]
     front_ext = jnp.concatenate([before_front, mixed_low[:block]], axis=0).astype(jnp.float32)
     back_ext = jnp.concatenate([before_back, mixed_low[block:]], axis=0).astype(jnp.float32)
     conv_out = jnp.concatenate(
@@ -1374,7 +1420,7 @@
     )
     normed_four, norm_back_four = jax.vjp(rms_scale, third, ff_norm_two.astype(jnp.float32))
     four_low, one_blocks = lax.optimization_barrier((normed_four.astype(narrow_dtype), one_blocks))
-    grad_four, _, two_gate, two_rest, outs_two = ff_call("both", 2, four_low, gate2, up2, down2, given)
+    grad_four, two_gate, two_rest, outs_two = ff_call("both", 2, four_low, gate2, up2, down2, given)
     shards = lax.axis_size("fsdp")
     ff_two_gate = lax.psum(two_gate, "ctx")
     grad_final = cotangent[0].astype(jnp.float32)
@@ -1425,7 +1471,7 @@
     grad_second = grad_third + grad_second_part
     two_rest, ff_two_gate = lax.optimization_barrier((two_rest, ff_two_gate))
     ff_two_rest = lax.psum(two_rest, "ctx")
-    grad_two, _, one_grads = ff_call(
+    grad_two, one_grads = ff_call(
         "backward", 3, grad_second.astype(narrow_dtype), gate1, up1, down1, inputs_one
     )
     grad_two, one_grads, ff_two_rest = lax.optimization_barrier((grad_two, one_grads, ff_two_rest))

time: 1040 us -> 1030 us (level)
  Pallas kernels: 809 us -> 795 us
  transfers between devices with their start and end apart: 10 -> 8, of which waited for: 4 -> 2; matrix products, arithmetic and copies ran while one was open for 12% -> 12% of each run, Pallas kernels for 66% -> 66%
where the time goes in v3:
time: 1030 us; the launch traced here: 1020 us
  Pallas kernels  795 us (77%)
  matrix products  61.6 us (6%)
  other arithmetic  60.6 us (6%)
  local copies, waits for them, and re-layouts  49.3 us (5%)
  waiting for transfers between devices  27.7 us (3%)
  between operations  16 us (2%)
    pallas_call x3, Pallas kernels, ff_call(): pl.pallas_call(partial(ff_kernel, chips, mode), out_shape=outs, in_specs=...  341 us
    pallas_call x1, Pallas kernels, tail_call(): pl.pallas_call(partial(tail_kernel, chips, count, pieces), out_shape=[jax...  231 us
    pallas_call x1, Pallas kernels, head_call(): pl.pallas_call(partial(head_kernel, chips, count), out_shape=outs, in_spe...  127 us
    pallas_call x1, Pallas kernels, attend_back_call(): pl.pallas_call(partial(attend_back_kernel, chips, count, groups), out_sha...  59.7 us
    pallas_call x1, Pallas kernels, attend_call(): pl.pallas_call(partial(attend_kernel, count, groups), out_shape=[jax.Shap...  35.4 us
    dot_general x3, matrix products, dot_plain(): return jnp.dot(left, right, preferred_element_type=jnp.float32)  21.8 us
  transfers between devices with their start and end apart: 8, of which 2 were waited for; matrix products, arithmetic and copies ran while one was open for 12% of the time, Pallas kernels for 66%

profile of v3, /device:TPU:16, one launch (start us, length us, event | category | flops | bytes accessed | tf_op | source)
XLA Modules:
  0.0 1016.1 jit_solution(6940467214316259583)
XLA Ops:
  7.3 1.5 pad_maximum_fusion.1
  11.6 127.4 %shard_map.364 = (bf16[8,4,144,1536]{3,2,1,0:T(8,128)(2,1)}, bf16[8,4,48,1536]{3,2,1,0:T(8,128)(2,1)}, bf16[8,256,1536]{2,1,0:T(8,128)(2,1)}, bf16[8,16,128]{2,1,0:T(8,128)(2,1)}, bf16[4,16,1536]{2,1,0:T(8,128)(2,1)}) custom-call(bf16[4,144,1536]{2,1,0:T(8,128)(2,1)} %bitcast.122, bf16[4,48,1536]{2,1,0:T(8,128)(2,1)} %bitcast.126, ...), custom_call_target="tpu_custom_call" | custom-call | bytes 37748736 | tf_op jit(solution)/shard_map/pallas_call | solution.py:648
  142.7 1.1 slice_reduce_fusion.2
  144.4 8.9 fusion.24
  155.1 1.7 copy-done.23
  157.6 1.3 slice-done.4
  159.4 1.5 multiply_reduce_fusion.11
  162.0 1.1 multiply_convert_fusion.5.refs_0_
  163.1 102.2 %shard_map.365 = (f32[256,1536]{1,0:T(8,128)}, bf16[8,256,1536]{2,1,0:T(8,128)(2,1)}) custom-call(bf16[256,1536]{1,0:T(8,128)(2,1)} %multiply_convert_fusion.5.refs_0_, bf16[864,1536]{1,0:T(8,128)(2,1)} %refs_2_.5, bf16[864,1536]{1,0:T(8,128)(2,1)} %refs_3_.5, bf16[864,1536]{1,0:T(8,128)(2,1)} %refs_4_.3), custom_call_target="tpu_custom_call" | custom-call | flops 16307453952 | bytes 12582912 | tf_op jit(solution)/shard_map/pallas_call | solution.py:164
  266.3 1.7 multiply_reduce_fusion.10
  268.6 2.3 multiply_reduce_fusion.20
  271.1 2.0 fusion.19
  273.2 7.1 fusion.59
  280.3 1.5 multiply_reduce_fusion.9
  284.1 35.4 %shard_map.366 = (bf16[24,64,256]{2,1,0:T(8,128)(2,1)S(1)}, f32[24,1,256]{2,1,0:T(1,128)S(1)}, bf16[4,16,64,256]{3,2,1,0:T(8,128)(2,1)S(1)}) custom-call(bf16[24,64,256]{2,1,0:T(8,128)(2,1)S(1)} %pad_maximum_fusion.6.q, bf16[16,64,256]{2,1,0:T(8,128)(2,1)S(1)} %pad_maximum_fusion.7.kv), custom_call_target="tpu_custom_call" | custom-call | flops 1610612736 | bytes 5767168 | tf_op jit(solution)/shard_map/pallas_call | solution.py:1078
  319.5 1.5 multiply_reduce_fusion.8
  321.1 1.3 multiply_convert_fusion.3.refs_0_
  322.4 9.5 all-gather.10.cloned.1.call-done
  331.8 121.9 %shard_map.367 = (f32[256,1536]{1,0:T(8,128)}, bf16[864,1536]{1,0:T(8,128)(2,1)}, bf16[1728,1536]{1,0:T(8,128)(2,1)}, bf16[8,256,1536]{2,1,0:T(8,128)(2,1)}) custom-call(bf16[256,1536]{1,0:T(8,128)(2,1)} %multiply_convert_fusion.3.refs_0_, bf16[8,256,1536]{2,1,0:T(8,128)(2,1)} %get-tuple-element.68.refs_1_, bf16[864,1536]{1,0:T(8,128)(2,1)} %refs_2_.4, ...), custom_call_target="tpu_custom_call" | custom-call | flops 48922361856 | bytes 12582912 | tf_op jit(solution)/shard_map/pallas_call | solution.py:164
  453.7 2.0 multiply_reduce_fusion
  456.2 5.2 convolution_convert_fusion.3
  461.6 1.1 copy-done.1
  462.7 1.1 copy-done.3
  463.8 1.1 copy-done.5
  464.9 1.6 copy-done.7
  466.5 59.7 %shard_map.368 = (f32[24,64,256]{2,1,0:T(8,128)S(1)}, f32[16,64,256]{2,1,0:T(8,128)S(1)}, f32[256,1536]{1,0:T(8,128)S(1)}) custom-call(bf16[24,64,256]{2,1,0:T(8,128)(2,1)S(1)} %copy-done.1, bf16[4,16,64,256]{3,2,1,0:T(8,128)(2,1)S(1)} %copy-done.7, bf16[24,64,256]{2,1,0:T(8,128)(2,1)S(1)} %bitcast.97, bf16[24,64,256]{2,1,0:T(8,128)(2,1)S(1)} %copy-done.3, ...), custom_call_target="tpu_custom_call" | custom-call | flops 4026531840 | bytes 8912896 | tf_op jit(solution)/shard_map/pallas_call | solution.py:1252
  526.3 0.9 convert.42
  528.7 1.3 fusion.33
  530.0 3.3 convolution_bitcast_fusion
  533.2 3.3 convolution_bitcast_fusion.1
  536.6 3.6 convolution_convert_fusion.2
  540.2 1.1 fusion.28
  541.3 18.1 %all-reduce.11.cloned.1.call-done = bf16[864,1536]{1,0:T(8,128)(2,1)} async-done(((bf16[864,1536]{1,0:T(8,128)(2,1)}), bf16[864,1536]{1,0:T(8,128)(2,1)}) %all-reduce.11.cloned.1.call-update) | async-done | bytes 2654224 | tf_op jit(solution)/shard_map/psum | solution.py:1425
  559.7 1.1 copy-done.25
  563.3 5.4 convolution_convert_fusion
  568.7 1.8 multiply_reduce_fusion.2
  570.8 5.0 convert_element_type.240
  575.7 1.8 fusion.57
  577.6 117.3 %shard_map.369 = (f32[256,1536]{1,0:T(8,128)}, bf16[2592,1536]{1,0:T(8,128)(2,1)}) custom-call(bf16[256,1536]{1,0:T(8,128)(2,1)} %get-tuple-element.157.refs_0_, bf16[8,256,1536]{2,1,0:T(8,128)(2,1)} %get-tuple-element.77.refs_1_, bf16[864,1536]{1,0:T(8,128)(2,1)} %refs_2_.5, bf16[864,1536]{1,0:T(8,128)(2,1)} %refs_3_.5, bf16[864,1536]{1,0:T(8,128)(2,1)} %refs_4_.3), custom_call_target="tpu_custom_call" | custom-call | flops 48922361856 | bytes 12582912 | tf_op jit(solution)/shard_map/pallas_call | solution.py:164
  695.0 1.9 multiply_reduce_fusion.3
  697.3 1.9 fusion.8
  699.3 5.3 multiply_convert_fusion.1
  704.6 1.7 multiply_reduce_fusion.14
  707.0 3.1 multiply_add_fusion.1
  710.2 3.4 collective-permute-start.1
  713.6 1.7 collective-permute-start
  715.3 4.7 convolution_convert_fusion.1
  720.0 5.6 slice_convert_fusion.3
  725.7 0.9 slice.365
  726.7 0.9 slice.370
  727.6 1.2 copy.49
  728.8 1.5 add.253
  731.2 3.0 multiply_convert_fusion.2
  734.4 11.1 %fusion.4 = (f32[1536]{0:T(1024)S(1)}, f32[256]{0:T(256)S(1)}, f32[256,1536]{1,0:T(8,128)}) fusion(bf16[1,256,1536]{2,1,0:T(8,128)(2,1)S(1)} %copy-done.28, f32[256]{0:T(256)S(1)} %copy-done.79, f32[1536]{0:T(1024)S(1)} %copy-done.57, bf16[4608,1536]{1,0:T(8,128)(2,1)} %bitcast.139, bf16[256,1536]{1,0:T(8,128)(2,1)S(1)} %get-tuple-element.167, ...), kind=kOutput, calls=%fused_computation.29 | convolution fusion | flops 3633707264 | bytes 18888704 | tf_op jit(solution)/shard_map/dot_general | solution.py:69
  746.3 3.2 fusion.22
  749.4 4.3 copy.48
  753.7 231.5 %shard_map.370 = (bf16[11,4,16,1536]{3,2,1,0:T(8,128)(2,1)}, bf16[4,144,1536]{2,1,0:T(8,128)(2,1)}, f32[16,128]{1,0:T(8,128)}) custom-call(bf16[4,2,5,4,16,1536]{5,4,3,2,1,0:T(8,128)(2,1)} %bitcast.98, bf16[4,2,3,4,16,1536]{5,4,3,2,1,0:T(8,128)(2,1)} %bitcast.99, bf16[4,2,3,4,16,1536]{5,4,3,2,1,0:T(8,128)(2,1)} %bitcast.100, ...), custom_call_target="tpu_custom_call" | custom-call | flops 3623878656 | bytes 34603008 | tf_op jit(solution)/shard_map/pallas_call | solution.py:942
  986.8 1.3 fusion.65
  988.2 1.4 fusion.64
  989.6 2.0 fusion.61
  991.6 3.5 fusion.60
  995.1 2.4 bitcast_convert_fusion
  997.4 1.6 fusion.10
  999.0 9.8 slice_convert_fusion
  (302 shorter events, 24.4 us)
Async XLA Ops:
  7.2 131.9 %all-gather.6.cloned.1.call-start = ((), (), s32[]{:S(2)}) async-start(), calls=%async_computation | async-start | bytes 3538944 | tf_op jit(solution)/shard_map/all_gather | solution.py:1334
  7.3 2.9 copy-start.86
  7.3 2.9 copy-start.87
  7.3 2.9 copy-start.88
  7.3 2.9 copy-start.89
  7.3 2.9 copy-start.90
  7.3 2.9 copy-start.91
  7.3 3.6 copy-start.26
  9.7 258.9 %all-gather.8.cloned.1.call-start = ((), (), s32[]{:S(2)}) async-start(), calls=%async_computation.4 | async-start | bytes 15728640 | tf_op jit(solution)/shard_map/all_gather | solution.py:1355
  139.2 192.6 %all-gather.10.cloned.1.call-start = ((), (), s32[]{:S(2)}) async-start(), calls=%async_computation.5 | async-start | bytes 7077888 | tf_op jit(solution)/shard_map/all_gather | solution.py:1393
  140.1 3.9 copy-start.56
  140.8 20.7 %copy-start.54 = (f32[1536]{0:T(1024)}, f32[1536]{0:T(1024)S(1)}, u32[]{:S(2)}) copy-start(f32[1536]{0:T(1024)S(1)} %reshape.474) | copy-start | bytes 18436
  143.8 10.2 %copy-start.60 = (f32[1536]{0:T(1024)}, f32[1536]{0:T(1024)S(1)}, u32[]{:S(2)}) copy-start(f32[1536]{0:T(1024)S(1)} %get-tuple-element.154) | copy-start | bytes 18436
  143.8 10.2 %copy-start.62 = (f32[1536]{0:T(1024)}, f32[1536]{0:T(1024)S(1)}, u32[]{:S(2)}) copy-start(f32[1536]{0:T(1024)S(1)} %get-tuple-element.155) | copy-start | bytes 18436
  143.8 10.2 %copy-start.64 = (f32[1536]{0:T(1024)}, f32[1536]{0:T(1024)S(1)}, u32[]{:S(2)}) copy-start(f32[1536]{0:T(1024)S(1)} %get-tuple-element.156) | copy-start | bytes 18436
  144.2 9.2 copy-start.42
  153.4 3.4 copy-start.23
  153.7 5.2 slice-start.4
  154.0 5.0 slice-start.5
  157.6 3.3 copy-start.45
  160.9 105.3 %copy-start.15 = (f32[256,1536]{1,0:T(8,128)}, f32[256,1536]{1,0:T(8,128)S(1)}, u32[]{:S(2)}) copy-start(f32[256,1536]{1,0:T(8,128)S(1)} %get-tuple-element.214) | copy-start | bytes 4718596
  265.4 294.0 %all-reduce.11.cloned.1.call-start = ((), (), s32[]{:S(2)}) async-start(), calls=%async_computation.1 | async-start | bytes 5308416 | tf_op jit(solution)/shard_map/psum | solution.py:1425
  265.8 261.4 %copy-start.80 = (f32[64]{0:T(128)}, f32[64]{0:T(128)S(1)}, u32[]{:S(2)}) copy-start(f32[64]{0:T(128)S(1)} %reshape.477) | copy-start | bytes 772
  265.9 16.6 %copy-start.81 = (f32[64]{0:T(128)}, f32[64]{0:T(128)S(1)}, u32[]{:S(2)}) copy-start(f32[64]{0:T(128)S(1)} %reshape.476) | copy-start | bytes 772
  267.9 51.6 %copy-start.13 = (f32[256,1536]{1,0:T(8,128)}, f32[256,1536]{1,0:T(8,128)S(1)}, u32[]{:S(2)}) copy-start(f32[256,1536]{1,0:T(8,128)S(1)} %get-tuple-element.160) | copy-start | bytes 4718596
  268.6 11.7 %copy-start.43 = (bf16[256,1536]{1,0:T(8,128)(2,1)}, bf16[256,1536]{1,0:T(8,128)(2,1)S(1)}, u32[]{:S(2)}) copy-start(bf16[256,1536]{1,0:T(8,128)(2,1)S(1)} %multiply_convert_fusion.4) | copy-start | bytes 2359300
  284.0 35.5 %slice-start.6 = ((s8[4718592]{0:T(1024)(128)(4,1)}), s8[4194304]{0:T(1024)(128)(4,1)S(1)}, s32[]{:S(2)}) async-start(s8[4718592]{0:T(1024)(128)(4,1)} %bitcast.117), calls=%async_computation.12 | async-start | bytes 8388608
  284.0 35.4 %copy-start = (bf16[24,64,256]{2,1,0:T(8,128)(2,1)}, bf16[24,64,256]{2,1,0:T(8,128)(2,1)S(1)}, u32[]{:S(2)}) copy-start(bf16[24,64,256]{2,1,0:T(8,128)(2,1)S(1)} %pad_maximum_fusion.6.q) | copy-start | bytes 2359300
  284.0 35.5 %slice-start.7 = ((s8[4718592]{0:T(1024)(128)(4,1)}), s8[524288]{0:T(1024)(128)(4,1)S(1)}, s32[]{:S(2)}) async-start(s8[4718592]{0:T(1024)(128)(4,1)} %bitcast.117), calls=%async_computation.13 | async-start | bytes 1048576
  321.1 134.7 %copy-start.18 = (f32[256,1536]{1,0:T(8,128)}, f32[256,1536]{1,0:T(8,128)S(1)}, u32[]{:S(2)}) copy-start(f32[256,1536]{1,0:T(8,128)S(1)} %get-tuple-element.220) | copy-start | bytes 4718596
  456.2 5.2 copy-start.20
  461.5 233.4 %all-reduce.13.cloned.1.call-start = ((), (), s32[]{:S(2)}) async-start(), calls=%async_computation.2 | async-start | bytes 10616832 | tf_op jit(solution)/shard_map/psum | solution.py:1473
  530.0 3.3 copy-start.52
  530.0 3.3 copy-start.51
  533.2 3.3 copy-start.4
  533.2 3.3 copy-start.21
  536.6 3.6 copy-start.19
  559.4 439.6 %all-reduce.15.cloned.1.call-start = ((), (), s32[]{:S(2)}) async-start(), calls=%async_computation.3 | async-start | bytes 15925248 | tf_op jit(solution)/shard_map/psum | solution.py:1478
  562.7 6.0 slice-start
  563.3 5.4 slice-start.1
  563.3 5.4 copy-start.14
  563.3 5.4 copy-start.48
  563.3 5.4 copy-start.49
  563.3 5.4 copy-start.72
  570.8 5.0 copy-start.22
  577.5 117.4 %copy-start.16 = (f32[256,1536]{1,0:T(8,128)S(1)}, f32[256,1536]{1,0:T(8,128)}, u32[]{:S(2)}) copy-start(f32[256,1536]{1,0:T(8,128)} %copy-done.15) | copy-start | bytes 4718596
  577.5 117.4 %copy-start.55 = (f32[1536]{0:T(1024)S(1)}, f32[1536]{0:T(1024)}, u32[]{:S(2)}) copy-start(f32[1536]{0:T(1024)} %copy-done.54) | copy-start | bytes 18436
  577.6 117.4 %copy-start.70 = (f32[256]{0:T(256)S(1)}, f32[256]{0:T(256)}, u32[]{:S(2)}) copy-start(f32[256]{0:T(256)} %copy-done.69) | copy-start | bytes 3076
  699.3 5.3 copy-start.9
  699.3 5.3 copy-start.11
  707.0 13.0 %slice-start.2 = ((s8[5308416]{0:T(1024)(128)(4,1)}), s8[4194304]{0:T(1024)(128)(4,1)S(1)}, s32[]{:S(2)}) async-start(s8[5308416]{0:T(1024)(128)(4,1)} %bitcast.110), calls=%async_computation.8 | async-start | bytes 8388608
  710.2 15.5 %copy-start.37 = (f32[130,1536]{1,0:T(8,128)}, f32[130,1536]{1,0:T(8,128)S(1)}, u32[]{:S(2)}) copy-start(f32[130,1536]{1,0:T(8,128)S(1)} %get-tuple-element.201) | copy-start | bytes 2396164
  710.2 20.2 %collective-permute-start.1 = (f32[2,1536]{1,0:T(2,128)S(1)}, f32[2,1536]{1,0:T(2,128)S(1)}, u32[]{:S(2)}, u32[]{:S(2)}) collective-permute-start(f32[2,1536]{1,0:T(2,128)S(1)} %broadcast_select_fusion), channel_id=1, source_target_pairs={{0,8},{8,16},{16,24},{1,9},{9,17},{17,25},{2,10},{10,18},{18,26},{... | collective-permute-start | bytes 36872 | tf_op jit(solution)/shard_map/ppermute | solution.py:29
  713.6 6.4 slice-start.3
  713.6 16.8 %collective-permute-start = (f32[2,1536]{1,0:T(2,128)S(1)}, f32[2,1536]{1,0:T(2,128)S(1)}, u32[]{:S(2)}, u32[]{:S(2)}) collective-permute-start(f32[2,1536]{1,0:T(2,128)S(1)} %slice.367), channel_id=1, source_target_pairs={{8,0},{16,8},{24,16},{9,1},{17,9},{25,17},{10,2},{18,10},{26,18},{... | collective-permute-start | bytes 36872 | tf_op jit(solution)/shard_map/ppermute | solution.py:30
  731.2 3.1 copy-start.28
  731.2 3.1 copy-start.38
  731.2 3.1 copy-start.57
  731.2 3.1 copy-start.79
  734.3 11.2 %copy-start.39 = (bf16[256,1536]{1,0:T(8,128)(2,1)}, bf16[256,1536]{1,0:T(8,128)(2,1)S(1)}, u32[]{:S(2)}) copy-start(bf16[256,1536]{1,0:T(8,128)(2,1)S(1)} %get-tuple-element.166) | copy-start | bytes 2359300
  734.3 11.2 %copy-start.40 = (bf16[256,1536]{1,0:T(8,128)(2,1)}, bf16[256,1536]{1,0:T(8,128)(2,1)S(1)}, u32[]{:S(2)}) copy-start(bf16[256,1536]{1,0:T(8,128)(2,1)S(1)} %get-tuple-element.167) | copy-start | bytes 2359300
  734.4 11.2 %copy-start.73 = (f32[8,8]{1,0:T(8,128)S(1)}, f32[8,8]{1,0:T(8,128)}, u32[]{:S(2)}) copy-start(f32[8,8]{1,0:T(8,128)} %reshape.466) | copy-start | bytes 772
  753.7 233.1 %copy-start.75 = (f32[256]{0:T(256)S(1)}, f32[256]{0:T(256)}, u32[]{:S(2)}) copy-start(f32[256]{0:T(256)} %copy-done.74) | copy-start | bytes 3076
  991.6 3.5 copy-start.47
  (45 other events, 64.9 us)
Sparse Core Ops, SparseCore 0:
  10.2 63.7 all-gather.5
  139.3 123.5 all-gather.7
  265.5 66.2 all-gather.9
  461.6 97.7 all-reduce.10
  562.9 122.2 all-reduce.12
  706.5 219.8 all-reduce.14

commit v4 on v3

--- a/solution.py
+++ b/solution.py
@@ -147,9 +147,8 @@
     scratch += [pltpu.VMEM((chips + 1, rows, width), bf16)]
     scratch += [dma((chips,))] * 8 + [dma((chips, 4))] * 4
     if not forward:
-        for share in (1, 2) if mode == "both" else (3,):
-            outs.append(jax.ShapeDtypeStruct((share * units, width), bf16))
-            out_specs.append(anywhere)
+        outs.append(jax.ShapeDtypeStruct((3 * units, width), bf16))
+        out_specs.append(anywhere)
         if mode == "both":
             outs.append(blocks)
             out_specs.append(anywhere)
@@ -171,9 +170,9 @@
             collective_id=ident, has_side_effects=True, vmem_limit_bytes=61 * 2**20
         ),
         cost_estimate=pl.CostEstimate(
-            flops=2 * products * size * rows * units * width,
-            bytes_accessed=4 * size * rows * width,
-            transcendentals=size * rows * units,
+            flops=1 if mode == "backward" else 2 * products * size * rows * units * width,
+            bytes_accessed=1 if mode == "backward" else 4 * size * rows * width,
+            transcendentals=0 if mode == "backward" else size * rows * units,
         ),
     )(*args)
 
@@ -208,8 +207,8 @@
         x_ref, gate, up_w, down, out, xall = refs[:6]
         rest = refs[6:]
     elif mode == "both":
-        x_ref, y_hbm, gate, up_w, down, out, gate_grads, weight_grads, result, xall = refs[:10]
-        rest = refs[10:]
+        x_ref, y_hbm, gate, up_w, down, out, weight_grads, result, xall = refs[:9]
+        rest = refs[9:]
     else:
         x_ref, y_hbm, gate, up_w, down, out, weight_grads, xall = refs[:8]
         rest = refs[8:]
@@ -438,11 +437,8 @@
         pairs = ((dgate, gate_right), (dup, gate_right), (hid, hid_right))
 
         def stage_copy(n, j):
-            there, at = weight_grads, n
-            if mode == "both":
-                there, at = (gate_grads, 0) if n == 0 else (weight_grads, n - 1)
-            there = there.at[
-                pl.ds(at * units, units), pl.ds(pl.multiple_of(j * step, step), step)
+            there = weight_grads.at[
+                pl.ds(n * units, units), pl.ds(pl.multiple_of(j * step, step), step)
             ]
             return pltpu.make_async_copy(stage.at[j % 2], there, stage_sem.at[j % 2])
 
@@ -1278,11 +1274,7 @@
         compiler_params=pltpu.CompilerParams(
             collective_id=ident, has_side_effects=True, vmem_limit_bytes=40 * 2**20
         ),
-        cost_estimate=pl.CostEstimate(
-            flops=10 * heads * size * rows * rows * count,
-            bytes_accessed=4 * (3 * q.size + kv_all.size),
-            transcendentals=heads * rows * rows * count,
-        ),
+        cost_estimate=pl.CostEstimate(flops=1, bytes_accessed=1, transcendentals=0),
     )(q, kv_all, grad, att, sums, outs)
 
 
@@ -1420,9 +1412,9 @@
     )
     normed_four, norm_back_four = jax.vjp(rms_scale, third, ff_norm_two.astype(jnp.float32))
     four_low, one_blocks = lax.optimization_barrier((normed_four.astype(narrow_dtype), one_blocks))
-    grad_four, two_gate, two_rest, outs_two = ff_call("both", 2, four_low, gate2, up2, down2, given)
+    grad_four, two_grads, outs_two = ff_call("both", 2, four_low, gate2, up2, down2, given)
     shards = lax.axis_size("fsdp")
-    ff_two_gate = lax.psum(two_gate, "ctx")
+    ff_two = lax.psum(two_grads, "ctx")
     grad_final = cotangent[0].astype(jnp.float32)
     grad_third_part, grad_ff_norm_two = norm_back_four(grad_four)
     grad_third = grad_final + grad_third_part
@@ -1447,7 +1439,6 @@
         outs_two,
     )
     final = third + ff_out_two
-    grad_query, ff_two_gate = lax.optimization_barrier((grad_query, ff_two_gate))
     key_count = grad_key_value.shape[0] // 2
     grad_query_raw, grad_query_gain = query_back(grad_query)
     raw_key_gradient, key_gain_gradient = key_back(grad_key_value[:key_count])
@@ -1469,21 +1460,18 @@
     )
     grad_second_part, grad_attn_norm = norm_back_three(grad_three)
     grad_second = grad_third + grad_second_part
-    two_rest, ff_two_gate = lax.optimization_barrier((two_rest, ff_two_gate))
-    ff_two_rest = lax.psum(two_rest, "ctx")
     grad_two, one_grads = ff_call(
         "backward", 3, grad_second.astype(narrow_dtype), gate1, up1, down1, inputs_one
     )
-    grad_two, one_grads, ff_two_rest = lax.optimization_barrier((grad_two, one_grads, ff_two_rest))
+    grad_two, one_grads, ff_two = lax.optimization_barrier((grad_two, one_grads, ff_two))
     ff_one = lax.psum(one_grads, "ctx")
     ff_one, ff_two = [
         [
             one[at : at + gate1.shape[0]].astype(jnp.float32)
             for at in range(0, one.shape[0], gate1.shape[0])
         ]
-        for one in (ff_one, ff_two_rest)
+        for one in (ff_one, ff_two)
     ]
-    ff_two = [ff_two_gate.astype(jnp.float32)] + ff_two
     grad_first_part, grad_ff_norm_one = norm_back_two(grad_two)
     grad_first = grad_second + grad_first_part
     first_low = grad_first.astype(narrow_dtype)

time: 1030 us -> 994 us (0.965)
  waiting for transfers between devices: 27.7 us -> 7.89 us
    psum x2 -> x1, waiting for transfers between devices: 18.1 us -> 0.01 us  [local(): ff_two = lax.psum(two_grads, 'ctx')]
  transfers between devices with their start and end apart: 8 -> 7, of which waited for: 2 -> 1; matrix products, arithmetic and copies ran while one was open for 12% -> 13% of each run, Pallas kernels for 66% -> 68%
where the time goes in v4:
time: 994 us; the launch traced here: 986 us
  Pallas kernels  790 us (79%)
  other arithmetic  63.1 us (6%)
  matrix products  58.3 us (6%)
  local copies, waits for them, and re-layouts  44.1 us (4%)
  between operations  15.7 us (2%)
    pallas_call x3, Pallas kernels, ff_call(): pl.pallas_call(partial(ff_kernel, chips, mode), out_shape=outs, in_specs=...  342 us
    pallas_call x1, Pallas kernels, tail_call(): pl.pallas_call(partial(tail_kernel, chips, count, pieces), out_shape=[jax...  225 us
    pallas_call x1, Pallas kernels, head_call(): pl.pallas_call(partial(head_kernel, chips, count), out_shape=outs, in_spe...  127 us
    pallas_call x1, Pallas kernels, attend_back_call(): pl.pallas_call(partial(attend_back_kernel, chips, count, groups), out_sha...  60.1 us
    pallas_call x1, Pallas kernels, attend_call(): pl.pallas_call(partial(attend_kernel, count, groups), out_shape=[jax.Shap...  35.3 us
    dot_general x3, matrix products, dot_plain(): return jnp.dot(left, right, preferred_element_type=jnp.float32)  21.9 us
  transfers between devices with their start and end apart: 7, of which 1 were waited for; matrix products, arithmetic and copies ran while one was open for 13% of the time, Pallas kernels for 68%

profile of v4, /device:TPU:16, one launch (start us, length us, event | category | flops | bytes accessed | tf_op | source)
XLA Modules:
  0.0 985.5 jit_solution(11936730993291986043)
XLA Ops:
  7.3 1.5 pad_maximum_fusion.1
  8.9 0.8 constant_dynamic-slice_fusion
  11.6 127.4 %shard_map.364 = (bf16[8,4,144,1536]{3,2,1,0:T(8,128)(2,1)}, bf16[8,4,48,1536]{3,2,1,0:T(8,128)(2,1)}, bf16[8,256,1536]{2,1,0:T(8,128)(2,1)}, bf16[8,16,128]{2,1,0:T(8,128)(2,1)}, bf16[4,16,1536]{2,1,0:T(8,128)(2,1)}) custom-call(bf16[4,144,1536]{2,1,0:T(8,128)(2,1)} %bitcast.120, bf16[4,48,1536]{2,1,0:T(8,128)(2,1)} %bitcast.124, ...), custom_call_target="tpu_custom_call" | custom-call | bytes 37748736 | tf_op jit(solution)/shard_map/pallas_call | solution.py:644
  140.8 0.7 fusion.46
  141.5 0.8 broadcast_select_fusion.1
  142.7 1.1 slice_reduce_fusion.2
  144.2 9.2 fusion.24
  153.7 2.0 copy-done.18
  156.8 2.8 multiply_convert_fusion.6
  159.7 1.5 multiply_reduce_fusion.11
  161.3 1.2 multiply_convert_fusion.5.refs_0_
  162.5 102.5 %shard_map.365 = (f32[256,1536]{1,0:T(8,128)}, bf16[8,256,1536]{2,1,0:T(8,128)(2,1)}) custom-call(bf16[256,1536]{1,0:T(8,128)(2,1)} %multiply_convert_fusion.5.refs_0_, bf16[864,1536]{1,0:T(8,128)(2,1)} %refs_2_.5, bf16[864,1536]{1,0:T(8,128)(2,1)} %refs_3_.5, bf16[864,1536]{1,0:T(8,128)(2,1)} %refs_4_.3), custom_call_target="tpu_custom_call" | custom-call | flops 16307453952 | bytes 12582912 | tf_op jit(solution)/shard_map/pallas_call | solution.py:163
  266.0 1.7 multiply_reduce_fusion.10
  267.7 1.1 copy-done.7
  269.0 2.3 multiply_reduce_fusion.20
  271.6 2.0 fusion.19
  273.6 7.3 fusion.59
  281.0 1.5 multiply_reduce_fusion.9
  283.5 0.8 copy-done.19
  284.7 35.3 %shard_map.366 = (bf16[24,64,256]{2,1,0:T(8,128)(2,1)S(1)}, f32[24,1,256]{2,1,0:T(1,128)S(1)}, bf16[4,16,64,256]{3,2,1,0:T(8,128)(2,1)S(1)}) custom-call(bf16[24,64,256]{2,1,0:T(8,128)(2,1)S(1)} %pad_maximum_fusion.6.q, bf16[16,64,256]{2,1,0:T(8,128)(2,1)S(1)} %pad_maximum_fusion.7.kv), custom_call_target="tpu_custom_call" | custom-call | flops 1610612736 | bytes 5767168 | tf_op jit(solution)/shard_map/pallas_call | solution.py:1074
  320.0 1.6 multiply_reduce_fusion.8
  322.8 1.1 multiply_convert_fusion.3.refs_0_
  323.8 7.8 all-gather.10.cloned.1.call-done
  331.6 121.4 %shard_map.367 = (f32[256,1536]{1,0:T(8,128)}, bf16[2592,1536]{1,0:T(8,128)(2,1)}, bf16[8,256,1536]{2,1,0:T(8,128)(2,1)}) custom-call(bf16[256,1536]{1,0:T(8,128)(2,1)} %multiply_convert_fusion.3.refs_0_, bf16[8,256,1536]{2,1,0:T(8,128)(2,1)} %get-tuple-element.63.refs_1_, bf16[864,1536]{1,0:T(8,128)(2,1)} %refs_2_.4, bf16[864,1536]{1,0:T(8,128)(2,1)} %refs_3_.4, ...), custom_call_target="tpu_custom_call" | custom-call | flops 48922361856 | bytes 12582912 | tf_op jit(solution)/shard_map/pallas_call | solution.py:163
  453.7 3.0 multiply_reduce_fusion
  456.7 1.6 fusion.5
  458.3 4.7 convolution_convert_fusion.3
  463.0 60.1 %shard_map.368 = (f32[24,64,256]{2,1,0:T(8,128)S(1)}, f32[16,64,256]{2,1,0:T(8,128)S(1)}, f32[256,1536]{1,0:T(8,128)S(1)}) custom-call(bf16[24,64,256]{2,1,0:T(8,128)(2,1)S(1)} %pad_maximum_fusion.6.q, bf16[4,16,64,256]{3,2,1,0:T(8,128)(2,1)S(1)} %copy-done.1, bf16[24,64,256]{2,1,0:T(8,128)(2,1)S(1)} %bitcast.97, ...), custom_call_target="tpu_custom_call" | custom-call | flops 1 | bytes 1 | tf_op jit(solution)/shard_map/pallas_call | solution.py:1248
  524.6 1.1 copy-done.20
  527.4 2.5 convolution_bitcast_fusion
  529.9 2.1 convolution_bitcast_fusion.1
  532.1 1.8 multiply_reduce_fusion.2
  533.9 1.8 fusion.57
  535.8 117.9 %shard_map.369 = (f32[256,1536]{1,0:T(8,128)}, bf16[2592,1536]{1,0:T(8,128)(2,1)}) custom-call(bf16[256,1536]{1,0:T(8,128)(2,1)} %get-tuple-element.147.refs_0_, bf16[8,256,1536]{2,1,0:T(8,128)(2,1)} %get-tuple-element.70.refs_1_, bf16[864,1536]{1,0:T(8,128)(2,1)} %refs_2_.5, bf16[864,1536]{1,0:T(8,128)(2,1)} %refs_3_.5, bf16[864,1536]{1,0:T(8,128)(2,1)} %refs_4_.3), custom_call_target="tpu_custom_call" | custom-call | flops 1 | bytes 1 | tf_op jit(solution)/shard_map/pallas_call | solution.py:163
  654.1 1.3 copy-done.17
  655.4 3.6 convolution_convert_fusion.2
  659.0 5.4 convolution_convert_fusion
  664.4 1.1 fusion.28
  666.1 1.9 multiply_reduce_fusion.3
  668.4 1.9 fusion.8
  670.4 5.2 multiply_convert_fusion.1
  675.7 1.7 multiply_reduce_fusion.14
  678.0 3.3 multiply_add_fusion.1
  681.4 4.3 collective-permute-start.1
  685.7 1.5 collective-permute-start
  687.3 3.6 convolution_convert_fusion.1
  690.9 10.0 %slice_convert_fusion.3 = (f32[864,1536]{1,0:T(8,128)}, f32[864,1536]{1,0:T(8,128)}, f32[864,1536]{1,0:T(8,128)}) fusion(bf16[2592,1536]{1,0:T(8,128)(2,1)} %all-reduce.10.cloned.1.call-done), kind=kLoop, calls=%fused_computation.16 | loop fusion | flops 3981312 | bytes 23887872 | tf_op jit(solution)/shard_map/convert_element_type | solution.py:1470
  700.9 0.9 slice.369
  701.8 0.9 slice.374
  702.8 1.2 copy.49
  704.0 1.7 add.251
  705.7 0.8 fusion.44
  706.6 3.3 multiply_convert_fusion.2
  709.9 11.3 %fusion.4 = (f32[1536]{0:T(1024)S(1)}, f32[256]{0:T(256)S(1)}, f32[256,1536]{1,0:T(8,128)}) fusion(bf16[1,256,1536]{2,1,0:T(8,128)(2,1)S(1)} %copy-done.23, f32[256]{0:T(256)S(1)} %copy-done.69, f32[1536]{0:T(1024)S(1)} %copy-done.45, bf16[4608,1536]{1,0:T(8,128)(2,1)} %bitcast.137, bf16[256,1536]{1,0:T(8,128)(2,1)S(1)} %get-tuple-element.160, ...), kind=kOutput, calls=%fused_computation.30 | convolution fusion | flops 3633707264 | bytes 18888704 | tf_op jit(solution)/shard_map/dot_general | solution.py:69
  722.1 3.2 fusion.22
  725.2 4.6 copy.48
  729.8 225.1 %shard_map.370 = (bf16[11,4,16,1536]{3,2,1,0:T(8,128)(2,1)}, bf16[4,144,1536]{2,1,0:T(8,128)(2,1)}, f32[16,128]{1,0:T(8,128)}) custom-call(bf16[4,2,5,4,16,1536]{5,4,3,2,1,0:T(8,128)(2,1)} %bitcast.98, bf16[4,2,3,4,16,1536]{5,4,3,2,1,0:T(8,128)(2,1)} %bitcast.99, bf16[4,2,3,4,16,1536]{5,4,3,2,1,0:T(8,128)(2,1)} %bitcast.100, ...), custom_call_target="tpu_custom_call" | custom-call | flops 3623878656 | bytes 34603008 | tf_op jit(solution)/shard_map/pallas_call | solution.py:938
  956.5 1.3 fusion.65
  957.9 1.4 fusion.64
  959.3 2.0 fusion.61
  961.3 3.5 fusion.60
  964.8 2.4 bitcast_convert_fusion
  967.1 1.6 fusion.10
  968.7 9.8 slice_convert_fusion
  (279 shorter events, 18.2 us)
Async XLA Ops:
  7.2 131.9 %all-gather.6.cloned.1.call-start = ((), (), s32[]{:S(2)}) async-start(), calls=%async_computation | async-start | bytes 3538944 | tf_op jit(solution)/shard_map/all_gather | solution.py:1326
  7.2 2.5 copy-start.78
  7.3 2.9 copy-start.79
  7.3 2.9 copy-start.80
  7.3 2.9 copy-start.81
  7.3 2.9 copy-start.82
  7.3 2.9 copy-start.83
  7.3 2.9 copy-start.84
  7.3 3.6 copy-start.21
  9.7 259.3 %all-gather.8.cloned.1.call-start = ((), (), s32[]{:S(2)}) async-start(), calls=%async_computation.3 | async-start | bytes 15728640 | tf_op jit(solution)/shard_map/all_gather | solution.py:1347
  139.2 192.4 %all-gather.10.cloned.1.call-start = ((), (), s32[]{:S(2)}) async-start(), calls=%async_computation.4 | async-start | bytes 7077888 | tf_op jit(solution)/shard_map/all_gather | solution.py:1385
  140.1 3.9 copy-start.44
  143.8 12.1 %copy-start.48 = (f32[1536]{0:T(1024)}, f32[1536]{0:T(1024)S(1)}, u32[]{:S(2)}) copy-start(f32[1536]{0:T(1024)S(1)} %get-tuple-element.144) | copy-start | bytes 18436
  143.8 12.1 %copy-start.50 = (f32[1536]{0:T(1024)}, f32[1536]{0:T(1024)S(1)}, u32[]{:S(2)}) copy-start(f32[1536]{0:T(1024)S(1)} %get-tuple-element.145) | copy-start | bytes 18436
  143.8 12.1 %copy-start.52 = (f32[1536]{0:T(1024)}, f32[1536]{0:T(1024)S(1)}, u32[]{:S(2)}) copy-start(f32[1536]{0:T(1024)S(1)} %get-tuple-element.146) | copy-start | bytes 18436
  143.9 9.6 copy-start.68
  144.2 9.2 copy-start.34
  155.7 4.0 slice-start.2
  155.9 3.7 slice-start.3
  156.8 2.8 copy-start.24
  156.8 2.9 copy-start.26
  156.8 2.9 copy-start.22
  161.2 103.8 %copy-start.74 = (f32[256]{0:T(256)}, f32[256]{0:T(256)S(1)}, u32[]{:S(2)}) copy-start(f32[256]{0:T(256)S(1)} %get-tuple-element.204) | copy-start | bytes 3076
  161.2 104.7 %copy-start.10 = (f32[256,1536]{1,0:T(8,128)}, f32[256,1536]{1,0:T(8,128)S(1)}, u32[]{:S(2)}) copy-start(f32[256,1536]{1,0:T(8,128)S(1)} %get-tuple-element.205) | copy-start | bytes 4718596
  161.3 103.8 %copy-start.58 = (f32[256]{0:T(256)}, f32[256]{0:T(256)S(1)}, u32[]{:S(2)}) copy-start(f32[256]{0:T(256)S(1)} %fusion.52) | copy-start | bytes 3076
  265.1 400.4 %all-reduce.10.cloned.1.call-start = ((), (), s32[]{:S(2)}) async-start(), calls=%async_computation.1 | async-start | bytes 15925248 | tf_op jit(solution)/shard_map/psum | solution.py:1417
  265.6 5.8 copy-start.70
  265.6 17.5 %copy-start.72 = (f32[64]{0:T(128)}, f32[64]{0:T(128)S(1)}, u32[]{:S(2)}) copy-start(f32[64]{0:T(128)S(1)} %reshape.476) | copy-start | bytes 772
  267.6 3.7 copy-start.66
  267.7 3.7 copy-start.60
  269.0 12.0 %copy-start.35 = (bf16[256,1536]{1,0:T(8,128)(2,1)}, bf16[256,1536]{1,0:T(8,128)(2,1)S(1)}, u32[]{:S(2)}) copy-start(bf16[256,1536]{1,0:T(8,128)(2,1)S(1)} %multiply_convert_fusion.4) | copy-start | bytes 2359300
  284.6 35.4 %slice-start.4 = ((s8[4718592]{0:T(1024)(128)(4,1)}), s8[4194304]{0:T(1024)(128)(4,1)S(1)}, s32[]{:S(2)}) async-start(s8[4718592]{0:T(1024)(128)(4,1)} %bitcast.115), calls=%async_computation.9 | async-start | bytes 8388608
  284.6 35.4 %copy-start.8 = (f32[256,1536]{1,0:T(8,128)S(1)}, f32[256,1536]{1,0:T(8,128)}, u32[]{:S(2)}) copy-start(f32[256,1536]{1,0:T(8,128)} %copy-done.7) | copy-start | bytes 4718596
  284.6 35.4 %slice-start.5 = ((s8[4718592]{0:T(1024)(128)(4,1)}), s8[524288]{0:T(1024)(128)(4,1)S(1)}, s32[]{:S(2)}) async-start(s8[4718592]{0:T(1024)(128)(4,1)} %bitcast.115), calls=%async_computation.10 | async-start | bytes 1048576
  453.0 515.7 %all-reduce.12.cloned.1.call-start = ((), (), s32[]{:S(2)}) async-start(), calls=%async_computation.2 | async-start | bytes 15925248 | tf_op jit(solution)/shard_map/psum | solution.py:1467
  453.7 3.0 copy-start.77
  453.7 3.0 copy-start.14
  453.7 3.0 copy-start.29
  458.3 75.6 %copy-start.16 = (f32[256,1536]{1,0:T(8,128)}, f32[256,1536]{1,0:T(8,128)S(1)}, u32[]{:S(2)}) copy-start(f32[256,1536]{1,0:T(8,128)S(1)} %fusion.5) | copy-start | bytes 4718596
  458.3 4.7 copy-start.1
  523.3 6.6 copy-start.41
  526.7 5.3 slice-start
  527.4 4.7 slice-start.1
  535.8 118.1 %copy-start.54 = (f32[1536]{0:T(1024)S(1)}, f32[1536]{0:T(1024)}, u32[]{:S(2)}) copy-start(f32[1536]{0:T(1024)} %get-tuple-element.123) | copy-start | bytes 18436
  535.8 118.2 %slice-start.6 = ((bf16[16,64,256]{2,1,0:T(8,128)(2,1)}), bf16[8,64,256]{2,1,0:T(8,128)(2,1)S(1)}, s32[]{:S(2)}) async-start(bf16[16,64,256]{2,1,0:T(8,128)(2,1)} %copy-done.41), calls=%async_computation.11 | async-start | bytes 524288 | tf_op jit(solution)/shard_map/slice | solution.py:1447
  535.8 118.2 %copy-start.43 = (bf16[8,64,256]{2,1,0:T(8,128)(2,1)S(1)}, bf16[8,64,256]{2,1,0:T(8,128)(2,1)}, u32[]{:S(2)}) copy-start(bf16[8,64,256]{2,1,0:T(8,128)(2,1)} %copy-done.42) | copy-start | bytes 786436
  655.4 3.6 copy-start.36
  659.0 5.4 copy-start.3
  659.0 5.4 copy-start.15
  666.1 2.4 copy-start.28
  670.4 5.3 copy-start.5
  678.0 9.2 copy-start.38
  681.3 19.6 %copy-start.30 = (f32[130,1536]{1,0:T(8,128)}, f32[130,1536]{1,0:T(8,128)S(1)}, u32[]{:S(2)}) copy-start(f32[130,1536]{1,0:T(8,128)S(1)} %get-tuple-element.192) | copy-start | bytes 2396164
  681.4 24.3 %collective-permute-start.1 = (f32[2,1536]{1,0:T(2,128)S(1)}, f32[2,1536]{1,0:T(2,128)S(1)}, u32[]{:S(2)}, u32[]{:S(2)}) collective-permute-start(f32[2,1536]{1,0:T(2,128)S(1)} %broadcast_select_fusion), channel_id=1, source_target_pairs={{0,8},{8,16},{16,24},{1,9},{9,17},{17,25},{2,10},{10,18},{18,26},{... | collective-permute-start | bytes 36872 | tf_op jit(solution)/shard_map/ppermute | solution.py:29
  685.7 20.0 %collective-permute-start = (f32[2,1536]{1,0:T(2,128)S(1)}, f32[2,1536]{1,0:T(2,128)S(1)}, u32[]{:S(2)}, u32[]{:S(2)}) collective-permute-start(f32[2,1536]{1,0:T(2,128)S(1)} %slice.371), channel_id=1, source_target_pairs={{8,0},{16,8},{24,16},{9,1},{17,9},{25,17},{10,2},{18,10},{26,18},{... | collective-permute-start | bytes 36872 | tf_op jit(solution)/shard_map/ppermute | solution.py:30
  706.5 3.4 copy-start.23
  706.5 3.4 copy-start.31
  706.5 3.4 copy-start.45
  706.5 3.4 copy-start.69
  709.9 11.4 %copy-start.32 = (bf16[256,1536]{1,0:T(8,128)(2,1)}, bf16[256,1536]{1,0:T(8,128)(2,1)S(1)}, u32[]{:S(2)}) copy-start(bf16[256,1536]{1,0:T(8,128)(2,1)S(1)} %get-tuple-element.159) | copy-start | bytes 2359300
  709.9 11.3 %copy-start.33 = (bf16[256,1536]{1,0:T(8,128)(2,1)}, bf16[256,1536]{1,0:T(8,128)(2,1)S(1)}, u32[]{:S(2)}) copy-start(bf16[256,1536]{1,0:T(8,128)(2,1)S(1)} %get-tuple-element.160) | copy-start | bytes 2359300
  729.8 226.7 %copy-start.65 = (f32[256]{0:T(256)S(1)}, f32[256]{0:T(256)}, u32[]{:S(2)}) copy-start(f32[256]{0:T(256)} %copy-done.64) | copy-start | bytes 3076
  961.3 3.5 copy-start.39
  964.8 2.4 copy-start.40
  (35 other events, 47.5 us)
Sparse Core Ops, SparseCore 0:
  10.2 63.7 all-gather.5
  139.3 123.5 all-gather.7
  265.2 66.3 all-gather.9
  453.2 187.2 all-reduce.9
  677.5 211.9 all-reduce.11

commit v5 on v4

--- a/solution.py
+++ b/solution.py
@@ -145,7 +145,7 @@
     scratch += [pltpu.VMEM((rows, width), jnp.float32)]
     scratch += [pltpu.VMEM((chips, rows, width), bf16)] * 3
     scratch += [pltpu.VMEM((chips + 1, rows, width), bf16)]
-    scratch += [dma((chips,))] * 8 + [dma((chips, 4))] * 4
+    scratch += [dma((chips,))] * 8 + [dma((chips, 8 if forward else 4))] * 4
     if not forward:
         outs.append(jax.ShapeDtypeStruct((3 * units, width), bf16))
         out_specs.append(anywhere)
@@ -226,7 +226,7 @@
     high_side = chip < chips - 1
     below = {"fsdp": lax.rem(place + 2 * chips - 2, 2 * chips)}
     above = {"fsdp": lax.rem(place + 2, 2 * chips)}
-    pieces = 4
+    pieces = ups_s.shape[1]
     piece = rows // pieces
     loads = [
         pltpu.make_async_copy(one, into, weight_m.at[n])

time: 994 us -> 991 us (level)
  no operation moved by 1% of the time
where the time goes in v5:
time: 991 us; the launch traced here: 982 us
  Pallas kernels  787 us (79%)
  other arithmetic  63.1 us (6%)
  matrix products  58.3 us (6%)
  local copies, waits for them, and re-layouts  44.3 us (4%)
  between operations  15.7 us (2%)
    pallas_call x3, Pallas kernels, ff_call(): pl.pallas_call(partial(ff_kernel, chips, mode), out_shape=outs, in_specs=...  339 us
    pallas_call x1, Pallas kernels, tail_call(): pl.pallas_call(partial(tail_kernel, chips, count, pieces), out_shape=[jax...  225 us
    pallas_call x1, Pallas kernels, head_call(): pl.pallas_call(partial(head_kernel, chips, count), out_shape=outs, in_spe...  127 us
    pallas_call x1, Pallas kernels, attend_back_call(): pl.pallas_call(partial(attend_back_kernel, chips, count, groups), out_sha...  60.1 us
    pallas_call x1, Pallas kernels, attend_call(): pl.pallas_call(partial(attend_kernel, count, groups), out_shape=[jax.Shap...  34.6 us
    dot_general x3, matrix products, dot_plain(): return jnp.dot(left, right, preferred_element_type=jnp.float32)  21.9 us
  transfers between devices with their start and end apart: 7, of which 1 were waited for; matrix products, arithmetic and copies ran while one was open for 13% of the time, Pallas kernels for 68%

profile of v5, /device:TPU:16, one launch (start us, length us, event | category | flops | bytes accessed | tf_op | source)
XLA Modules:
  0.0 982.2 jit_solution(14984271481761633303)
XLA Ops:
  7.3 1.5 pad_maximum_fusion.1
  8.9 0.8 constant_dynamic-slice_fusion
  11.6 127.4 %shard_map.364 = (bf16[8,4,144,1536]{3,2,1,0:T(8,128)(2,1)}, bf16[8,4,48,1536]{3,2,1,0:T(8,128)(2,1)}, bf16[8,256,1536]{2,1,0:T(8,128)(2,1)}, bf16[8,16,128]{2,1,0:T(8,128)(2,1)}, bf16[4,16,1536]{2,1,0:T(8,128)(2,1)}) custom-call(bf16[4,144,1536]{2,1,0:T(8,128)(2,1)} %bitcast.120, bf16[4,48,1536]{2,1,0:T(8,128)(2,1)} %bitcast.124, ...), custom_call_target="tpu_custom_call" | custom-call | bytes 37748736 | tf_op jit(solution)/shard_map/pallas_call | solution.py:644
  140.8 0.7 fusion.46
  141.5 0.8 broadcast_select_fusion.1
  142.7 1.1 slice_reduce_fusion.2
  144.2 9.2 fusion.24
  153.7 2.0 copy-done.18
  156.8 2.8 multiply_convert_fusion.6
  159.7 1.5 multiply_reduce_fusion.11
  161.3 1.2 multiply_convert_fusion.5.refs_0_
  162.5 100.3 %shard_map.365 = (f32[256,1536]{1,0:T(8,128)}, bf16[8,256,1536]{2,1,0:T(8,128)(2,1)}) custom-call(bf16[256,1536]{1,0:T(8,128)(2,1)} %multiply_convert_fusion.5.refs_0_, bf16[864,1536]{1,0:T(8,128)(2,1)} %refs_2_.5, bf16[864,1536]{1,0:T(8,128)(2,1)} %refs_3_.5, bf16[864,1536]{1,0:T(8,128)(2,1)} %refs_4_.3), custom_call_target="tpu_custom_call" | custom-call | flops 16307453952 | bytes 12582912 | tf_op jit(solution)/shard_map/pallas_call | solution.py:163
  263.7 1.7 multiply_reduce_fusion.10
  265.4 1.1 copy-done.7
  266.8 2.3 multiply_reduce_fusion.20
  269.3 2.0 fusion.19
  271.4 7.5 fusion.59
  278.9 1.5 multiply_reduce_fusion.9
  281.4 0.8 copy-done.19
  282.5 34.6 %shard_map.366 = (bf16[24,64,256]{2,1,0:T(8,128)(2,1)S(1)}, f32[24,1,256]{2,1,0:T(1,128)S(1)}, bf16[4,16,64,256]{3,2,1,0:T(8,128)(2,1)S(1)}) custom-call(bf16[24,64,256]{2,1,0:T(8,128)(2,1)S(1)} %pad_maximum_fusion.6.q, bf16[16,64,256]{2,1,0:T(8,128)(2,1)S(1)} %pad_maximum_fusion.7.kv), custom_call_target="tpu_custom_call" | custom-call | flops 1610612736 | bytes 5767168 | tf_op jit(solution)/shard_map/pallas_call | solution.py:1074
  317.2 1.6 multiply_reduce_fusion.8
  319.9 1.1 multiply_convert_fusion.3.refs_0_
  321.0 7.3 all-gather.10.cloned.1.call-done
  328.3 121.4 %shard_map.367 = (f32[256,1536]{1,0:T(8,128)}, bf16[2592,1536]{1,0:T(8,128)(2,1)}, bf16[8,256,1536]{2,1,0:T(8,128)(2,1)}) custom-call(bf16[256,1536]{1,0:T(8,128)(2,1)} %multiply_convert_fusion.3.refs_0_, bf16[8,256,1536]{2,1,0:T(8,128)(2,1)} %get-tuple-element.63.refs_1_, bf16[864,1536]{1,0:T(8,128)(2,1)} %refs_2_.4, bf16[864,1536]{1,0:T(8,128)(2,1)} %refs_3_.4, ...), custom_call_target="tpu_custom_call" | custom-call | flops 48922361856 | bytes 12582912 | tf_op jit(solution)/shard_map/pallas_call | solution.py:163
  450.4 3.0 multiply_reduce_fusion
  453.4 1.6 fusion.5
  455.0 4.7 convolution_convert_fusion.3
  459.7 60.1 %shard_map.368 = (f32[24,64,256]{2,1,0:T(8,128)S(1)}, f32[16,64,256]{2,1,0:T(8,128)S(1)}, f32[256,1536]{1,0:T(8,128)S(1)}) custom-call(bf16[24,64,256]{2,1,0:T(8,128)(2,1)S(1)} %pad_maximum_fusion.6.q, bf16[4,16,64,256]{3,2,1,0:T(8,128)(2,1)S(1)} %copy-done.1, bf16[24,64,256]{2,1,0:T(8,128)(2,1)S(1)} %bitcast.97, ...), custom_call_target="tpu_custom_call" | custom-call | flops 1 | bytes 1 | tf_op jit(solution)/shard_map/pallas_call | solution.py:1248
  521.3 1.1 copy-done.20
  524.1 2.5 convolution_bitcast_fusion
  526.6 2.1 convolution_bitcast_fusion.1
  528.8 1.8 multiply_reduce_fusion.2
  530.6 1.8 fusion.57
  532.5 117.6 %shard_map.369 = (f32[256,1536]{1,0:T(8,128)}, bf16[2592,1536]{1,0:T(8,128)(2,1)}) custom-call(bf16[256,1536]{1,0:T(8,128)(2,1)} %get-tuple-element.147.refs_0_, bf16[8,256,1536]{2,1,0:T(8,128)(2,1)} %get-tuple-element.70.refs_1_, bf16[864,1536]{1,0:T(8,128)(2,1)} %refs_2_.5, bf16[864,1536]{1,0:T(8,128)(2,1)} %refs_3_.5, bf16[864,1536]{1,0:T(8,128)(2,1)} %refs_4_.3), custom_call_target="tpu_custom_call" | custom-call | flops 1 | bytes 1 | tf_op jit(solution)/shard_map/pallas_call | solution.py:163
  650.5 1.3 copy-done.17
  651.8 3.6 convolution_convert_fusion.2
  655.4 5.4 convolution_convert_fusion
  660.8 1.1 fusion.28
  662.5 1.9 multiply_reduce_fusion.3
  664.9 1.9 fusion.8
  666.8 5.2 multiply_convert_fusion.1
  672.1 1.7 multiply_reduce_fusion.14
  674.5 3.3 multiply_add_fusion.1
  677.8 4.5 collective-permute-start.1
  682.3 1.5 collective-permute-start
  683.9 3.6 convolution_convert_fusion.1
  687.5 9.9 %slice_convert_fusion.3 = (f32[864,1536]{1,0:T(8,128)}, f32[864,1536]{1,0:T(8,128)}, f32[864,1536]{1,0:T(8,128)}) fusion(bf16[2592,1536]{1,0:T(8,128)(2,1)} %all-reduce.10.cloned.1.call-done), kind=kLoop, calls=%fused_computation.16 | loop fusion | flops 3981312 | bytes 23887872 | tf_op jit(solution)/shard_map/convert_element_type | solution.py:1470
  697.5 0.9 slice.369
  698.4 0.9 slice.374
  699.4 1.2 copy.49
  700.5 1.7 add.251
  702.3 0.8 fusion.44
  703.2 3.3 multiply_convert_fusion.2
  706.5 11.3 %fusion.4 = (f32[1536]{0:T(1024)S(1)}, f32[256]{0:T(256)S(1)}, f32[256,1536]{1,0:T(8,128)}) fusion(bf16[1,256,1536]{2,1,0:T(8,128)(2,1)S(1)} %copy-done.23, f32[256]{0:T(256)S(1)} %copy-done.69, f32[1536]{0:T(1024)S(1)} %copy-done.45, bf16[4608,1536]{1,0:T(8,128)(2,1)} %bitcast.137, bf16[256,1536]{1,0:T(8,128)(2,1)S(1)} %get-tuple-element.160, ...), kind=kOutput, calls=%fused_computation.30 | convolution fusion | flops 3633707264 | bytes 18888704 | tf_op jit(solution)/shard_map/dot_general | solution.py:69
  718.6 3.2 fusion.22
  721.8 4.6 copy.48
  726.4 225.2 %shard_map.370 = (bf16[11,4,16,1536]{3,2,1,0:T(8,128)(2,1)}, bf16[4,144,1536]{2,1,0:T(8,128)(2,1)}, f32[16,128]{1,0:T(8,128)}) custom-call(bf16[4,2,5,4,16,1536]{5,4,3,2,1,0:T(8,128)(2,1)} %bitcast.98, bf16[4,2,3,4,16,1536]{5,4,3,2,1,0:T(8,128)(2,1)} %bitcast.99, bf16[4,2,3,4,16,1536]{5,4,3,2,1,0:T(8,128)(2,1)} %bitcast.100, ...), custom_call_target="tpu_custom_call" | custom-call | flops 3623878656 | bytes 34603008 | tf_op jit(solution)/shard_map/pallas_call | solution.py:938
  953.2 1.3 fusion.65
  954.6 1.4 fusion.64
  956.0 2.0 fusion.61
  958.0 3.5 fusion.60
  961.4 2.4 bitcast_convert_fusion
  963.8 1.6 fusion.10
  965.4 9.8 slice_convert_fusion
  (279 shorter events, 18.2 us)
Async XLA Ops:
  7.2 131.9 %all-gather.6.cloned.1.call-start = ((), (), s32[]{:S(2)}) async-start(), calls=%async_computation | async-start | bytes 3538944 | tf_op jit(solution)/shard_map/all_gather | solution.py:1326
  7.2 2.5 copy-start.78
  7.3 2.9 copy-start.79
  7.3 2.9 copy-start.80
  7.3 2.9 copy-start.81
  7.3 2.9 copy-start.82
  7.3 2.9 copy-start.83
  7.3 2.9 copy-start.84
  7.3 3.6 copy-start.21
  9.7 257.1 %all-gather.8.cloned.1.call-start = ((), (), s32[]{:S(2)}) async-start(), calls=%async_computation.3 | async-start | bytes 15728640 | tf_op jit(solution)/shard_map/all_gather | solution.py:1347
  139.2 189.1 %all-gather.10.cloned.1.call-start = ((), (), s32[]{:S(2)}) async-start(), calls=%async_computation.4 | async-start | bytes 7077888 | tf_op jit(solution)/shard_map/all_gather | solution.py:1385
  140.1 3.9 copy-start.44
  143.8 12.1 %copy-start.48 = (f32[1536]{0:T(1024)}, f32[1536]{0:T(1024)S(1)}, u32[]{:S(2)}) copy-start(f32[1536]{0:T(1024)S(1)} %get-tuple-element.144) | copy-start | bytes 18436
  143.8 12.1 %copy-start.50 = (f32[1536]{0:T(1024)}, f32[1536]{0:T(1024)S(1)}, u32[]{:S(2)}) copy-start(f32[1536]{0:T(1024)S(1)} %get-tuple-element.145) | copy-start | bytes 18436
  143.8 12.1 %copy-start.52 = (f32[1536]{0:T(1024)}, f32[1536]{0:T(1024)S(1)}, u32[]{:S(2)}) copy-start(f32[1536]{0:T(1024)S(1)} %get-tuple-element.146) | copy-start | bytes 18436
  143.9 9.6 copy-start.68
  144.2 9.2 copy-start.34
  155.7 4.0 slice-start.2
  155.9 3.7 slice-start.3
  156.8 2.8 copy-start.24
  156.8 2.9 copy-start.26
  156.8 2.9 copy-start.22
  161.2 101.6 %copy-start.74 = (f32[256]{0:T(256)}, f32[256]{0:T(256)S(1)}, u32[]{:S(2)}) copy-start(f32[256]{0:T(256)S(1)} %get-tuple-element.204) | copy-start | bytes 3076
  161.2 102.5 %copy-start.10 = (f32[256,1536]{1,0:T(8,128)}, f32[256,1536]{1,0:T(8,128)S(1)}, u32[]{:S(2)}) copy-start(f32[256,1536]{1,0:T(8,128)S(1)} %get-tuple-element.205) | copy-start | bytes 4718596
  161.3 101.5 %copy-start.58 = (f32[256]{0:T(256)}, f32[256]{0:T(256)S(1)}, u32[]{:S(2)}) copy-start(f32[256]{0:T(256)S(1)} %fusion.52) | copy-start | bytes 3076
  262.8 399.1 %all-reduce.10.cloned.1.call-start = ((), (), s32[]{:S(2)}) async-start(), calls=%async_computation.1 | async-start | bytes 15925248 | tf_op jit(solution)/shard_map/psum | solution.py:1417
  263.3 5.8 copy-start.70
  263.4 17.7 %copy-start.72 = (f32[64]{0:T(128)}, f32[64]{0:T(128)S(1)}, u32[]{:S(2)}) copy-start(f32[64]{0:T(128)S(1)} %reshape.476) | copy-start | bytes 772
  265.4 3.7 copy-start.66
  265.4 3.6 copy-start.60
  266.7 12.1 %copy-start.35 = (bf16[256,1536]{1,0:T(8,128)(2,1)}, bf16[256,1536]{1,0:T(8,128)(2,1)S(1)}, u32[]{:S(2)}) copy-start(bf16[256,1536]{1,0:T(8,128)(2,1)S(1)} %multiply_convert_fusion.4) | copy-start | bytes 2359300
  282.4 34.7 %slice-start.4 = ((s8[4718592]{0:T(1024)(128)(4,1)}), s8[4194304]{0:T(1024)(128)(4,1)S(1)}, s32[]{:S(2)}) async-start(s8[4718592]{0:T(1024)(128)(4,1)} %bitcast.115), calls=%async_computation.9 | async-start | bytes 8388608
  282.5 34.6 %copy-start.8 = (f32[256,1536]{1,0:T(8,128)S(1)}, f32[256,1536]{1,0:T(8,128)}, u32[]{:S(2)}) copy-start(f32[256,1536]{1,0:T(8,128)} %copy-done.7) | copy-start | bytes 4718596
  282.5 34.6 %slice-start.5 = ((s8[4718592]{0:T(1024)(128)(4,1)}), s8[524288]{0:T(1024)(128)(4,1)S(1)}, s32[]{:S(2)}) async-start(s8[4718592]{0:T(1024)(128)(4,1)} %bitcast.115), calls=%async_computation.10 | async-start | bytes 1048576
  449.7 515.7 %all-reduce.12.cloned.1.call-start = ((), (), s32[]{:S(2)}) async-start(), calls=%async_computation.2 | async-start | bytes 15925248 | tf_op jit(solution)/shard_map/psum | solution.py:1467
  450.4 3.0 copy-start.77
  450.4 3.0 copy-start.14
  450.4 3.0 copy-start.29
  455.0 75.6 %copy-start.16 = (f32[256,1536]{1,0:T(8,128)}, f32[256,1536]{1,0:T(8,128)S(1)}, u32[]{:S(2)}) copy-start(f32[256,1536]{1,0:T(8,128)S(1)} %fusion.5) | copy-start | bytes 4718596
  455.0 4.7 copy-start.1
  519.9 6.6 copy-start.41
  523.4 5.3 slice-start
  524.1 4.7 slice-start.1
  532.5 117.8 %copy-start.54 = (f32[1536]{0:T(1024)S(1)}, f32[1536]{0:T(1024)}, u32[]{:S(2)}) copy-start(f32[1536]{0:T(1024)} %get-tuple-element.123) | copy-start | bytes 18436
  532.5 117.9 %slice-start.6 = ((bf16[16,64,256]{2,1,0:T(8,128)(2,1)}), bf16[8,64,256]{2,1,0:T(8,128)(2,1)S(1)}, s32[]{:S(2)}) async-start(bf16[16,64,256]{2,1,0:T(8,128)(2,1)} %copy-done.41), calls=%async_computation.11 | async-start | bytes 524288 | tf_op jit(solution)/shard_map/slice | solution.py:1447
  532.5 117.9 %copy-start.43 = (bf16[8,64,256]{2,1,0:T(8,128)(2,1)S(1)}, bf16[8,64,256]{2,1,0:T(8,128)(2,1)}, u32[]{:S(2)}) copy-start(bf16[8,64,256]{2,1,0:T(8,128)(2,1)} %copy-done.42) | copy-start | bytes 786436
  651.8 3.6 copy-start.36
  655.4 5.4 copy-start.3
  655.4 5.4 copy-start.15
  662.5 2.4 copy-start.28
  666.8 5.3 copy-start.5
  674.5 9.4 copy-start.38
  677.7 19.7 %copy-start.30 = (f32[130,1536]{1,0:T(8,128)}, f32[130,1536]{1,0:T(8,128)S(1)}, u32[]{:S(2)}) copy-start(f32[130,1536]{1,0:T(8,128)S(1)} %get-tuple-element.192) | copy-start | bytes 2396164
  677.8 24.4 %collective-permute-start.1 = (f32[2,1536]{1,0:T(2,128)S(1)}, f32[2,1536]{1,0:T(2,128)S(1)}, u32[]{:S(2)}, u32[]{:S(2)}) collective-permute-start(f32[2,1536]{1,0:T(2,128)S(1)} %broadcast_select_fusion), channel_id=1, source_target_pairs={{0,8},{8,16},{16,24},{1,9},{9,17},{17,25},{2,10},{10,18},{18,26},{... | collective-permute-start | bytes 36872 | tf_op jit(solution)/shard_map/ppermute | solution.py:29
  682.3 20.0 %collective-permute-start = (f32[2,1536]{1,0:T(2,128)S(1)}, f32[2,1536]{1,0:T(2,128)S(1)}, u32[]{:S(2)}, u32[]{:S(2)}) collective-permute-start(f32[2,1536]{1,0:T(2,128)S(1)} %slice.371), channel_id=1, source_target_pairs={{8,0},{16,8},{24,16},{9,1},{17,9},{25,17},{10,2},{18,10},{26,18},{... | collective-permute-start | bytes 36872 | tf_op jit(solution)/shard_map/ppermute | solution.py:30
  703.1 3.4 copy-start.23
  703.1 3.4 copy-start.31
  703.1 3.4 copy-start.45
  703.1 3.4 copy-start.69
  706.5 11.3 %copy-start.32 = (bf16[256,1536]{1,0:T(8,128)(2,1)}, bf16[256,1536]{1,0:T(8,128)(2,1)S(1)}, u32[]{:S(2)}) copy-start(bf16[256,1536]{1,0:T(8,128)(2,1)S(1)} %get-tuple-element.159) | copy-start | bytes 2359300
  706.5 11.3 %copy-start.33 = (bf16[256,1536]{1,0:T(8,128)(2,1)}, bf16[256,1536]{1,0:T(8,128)(2,1)S(1)}, u32[]{:S(2)}) copy-start(bf16[256,1536]{1,0:T(8,128)(2,1)S(1)} %get-tuple-element.160) | copy-start | bytes 2359300
  726.4 226.8 %copy-start.65 = (f32[256]{0:T(256)S(1)}, f32[256]{0:T(256)}, u32[]{:S(2)}) copy-start(f32[256]{0:T(256)} %copy-done.64) | copy-start | bytes 3076
  958.0 3.5 copy-start.39
  961.4 2.4 copy-start.40
  (35 other events, 47.5 us)
Sparse Core Ops, SparseCore 0:
  10.2 63.7 all-gather.5
  139.3 123.5 all-gather.7
  264.6 63.6 all-gather.9
  449.8 187.2 all-reduce.9
  673.9 212.3 all-reduce.11
